TPU v7x, 256 devices: a whole 4x4x8 slice. The times are simulated.
256 devices in a mesh: lat: 8 (over z), lon: 8 (over x, y_lo), mem: 4 (over y_hi, core).
Axes of the slice: x: 4, y: 4 (y_hi: 2, y_lo: 2; y = y_hi * 2 + y_lo), z: 8, core: 2. Of those that a mesh axis runs over, the one named last changes fastest.
Arguments:
- gradients: float32 [4, 16, 768, 3072], P('mem', None, 'lat', 'lon'), may hold values from -10 to 10
- ritz_vectors: float32 [80, 16, 256, 1024], P(None, 'mem', 'lat', 'lon'), may hold values from -6 to 6
- ritz_values: float32 [80], replicated, may hold values from 1.5 to 50
Outputs:
- preconditioned: float32 [4, 16, 768, 3072], P('mem', None, 'lat', 'lon')
- coefficients: float32 [4, 80], replicated
All inputs are finite; a program needn't handle non-finite values.
Results may differ from a plain program's by a relative error of at most 0.00013.
Values sent between devices are 32-bit elements; how exact they have to be, the bound alone decides.
No kernel may reach another device: no remote copies, remote signals or barrier semaphores. Data moves between devices by JAX's collectives and lax.ppermute only.
A program may use at most 128 MiB of HBM per device.

v0:
```python
import jax
import jax.numpy as jnp
from jax import lax
from jax.sharding import PartitionSpec as P

LEVELS = 16


TENT = (1.0 / 9.0, 2.0 / 9.0, 3.0 / 9.0, 2.0 / 9.0, 1.0 / 9.0)


def padded_2(value, sides, width):
    for axis, dim in sides:
        size, length = (lax.axis_size(axis), value.shape[dim])
        up = [(i, (i + 1) % size) for i in range(size)]
        down = [(j, i) for i, j in up]
        last = lax.slice_in_dim(value, length - width, length, axis=dim)
        leading = lax.slice_in_dim(value, 0, width, axis=dim)
        before = lax.ppermute(last, axis, up)
        after = lax.ppermute(leading, axis, down)
        value = jnp.concatenate([before, value, after], axis=dim)
    return value


def restrict_padded(padded):
    rows = (padded.shape[-2] - 2) // 3
    cols = (padded.shape[-1] - 2) // 3
    along = TENT[0] * padded[..., 0 : 3 * rows - 2 : 3, :]
    for offset in range(1, 5):
        along = along + TENT[offset] * padded[..., offset : offset + 3 * rows - 2 : 3, :]
    result = TENT[0] * along[..., 0 : 3 * cols - 2 : 3]
    for offset in range(1, 5):
        result = result + TENT[offset] * along[..., offset : offset + 3 * cols - 2 : 3]
    return result


def prolong_padded(padded):
    center = padded[..., 1:-1, :]
    first = (2.0 * center + padded[..., :-2, :]) * (1.0 / 3.0)
    third = (2.0 * center + padded[..., 2:, :]) * (1.0 / 3.0)
    stacked = jnp.stack([first, center, third], axis=-2)
    shape = stacked.shape
    rowwise = stacked.reshape(shape[:-3] + (shape[-3] * 3, shape[-1]))
    center = rowwise[..., 1:-1]
    first = (2.0 * center + rowwise[..., :-2]) * (1.0 / 3.0)
    third = (2.0 * center + rowwise[..., 2:]) * (1.0 / 3.0)
    stacked = jnp.stack([first, center, third], axis=-1)
    shape = stacked.shape
    return stacked.reshape(shape[:-2] + (shape[-2] * 3,))


def clear_ends(padded):
    rows = padded.shape[2]
    position = lax.broadcasted_iota(jnp.int32, (1, 1, rows, 1), 2)
    band = lax.axis_index("lat")
    first_band = band == 0
    last_band = band == lax.axis_size("lat") - 1
    dropped = jnp.logical_or(
        jnp.logical_and(position == 0, first_band), jnp.logical_and(position == rows - 1, last_band)
    )
    return jnp.where(dropped, jnp.zeros_like(padded), padded)


def restrict_tile(field):
    padded = padded_2(field, (("lat", 2), ("lon", 3)), 1)
    return restrict_padded(clear_ends(padded))


def prolong_tile(field):
    padded = padded_2(field, (("lat", 2), ("lon", 3)), 1)
    return prolong_padded(clear_ends(padded))


def levels_products(ritz_vectors, coarse):
    return jnp.einsum("klyx,mlyx->mk", ritz_vectors, coarse, precision=lax.Precision.HIGHEST)


def levels_update(ritz_vectors, coefficients):
    return jnp.einsum("klyx,mk->mlyx", ritz_vectors, coefficients, precision=lax.Precision.HIGHEST)


def finish_coefficients(partial_sums, ritz_values, coarse):
    cells = LEVELS * coarse.shape[2] * lax.axis_size("lat") * coarse.shape[3] * lax.axis_size("lon")
    projections = lax.psum(partial_sums, ("lat", "lon", "mem")) * (1.0 / cells)
    return (1.0 / ritz_values - 1.0)[None, :] * projections


def per_device(gradients, ritz_vectors, ritz_values):
    coarse = restrict_tile(gradients)
    spread = lax.all_to_all(coarse, "mem", split_axis=1, concat_axis=0, tiled=True)
    coefficients = finish_coefficients(levels_products(ritz_vectors, spread), ritz_values, spread)
    corrected = spread + levels_update(ritz_vectors, coefficients)
    returned = lax.all_to_all(corrected, "mem", split_axis=0, concat_axis=1, tiled=True)
    preconditioned = prolong_tile(returned)
    return (preconditioned, coefficients)


def solution(mesh):
    placed = (P("mem", None, "lat", "lon"), P(None, "mem", "lat", "lon"), P())
    return jax.shard_map(
        per_device,
        mesh=mesh,
        in_specs=placed,
        out_specs=(P("mem", None, "lat", "lon"), P()),
        check_vma=False,
    )
```

profile of v0, /device:TPU:1, one launch (start us, length us, event | category | flops | bytes accessed | tf_op | source)
XLA Modules:
  0.0 222.1 jit_solution(4740134516533410978)
XLA Ops:
  1.7 6.5 %collective-permute-start.1 = (f32[1,16,1,384]{3,1,2,0:T(8,128)S(1)}, f32[1,16,1,384]{3,1,2,0:T(8,128)S(1)}, u32[]{:S(2)}, u32[]{:S(2)}) collective-permute-start(f32[1,16,1,384]{3,1,2,0:T(8,128)S(1)} %copy.73), channel_id=1, source_target_pairs={{32,0},{64,32},{96,64},{128,96},{160,128},{192,160},{224,192},{0,2... | collective-permute-start | bytes 73736 | tf_op jit(solution)/shard_map/ppermute | solution.py:20
  9.2 2.9 %collective-permute-done = f32[1,16,1,384]{3,1,2,0:T(8,128)S(1)} collective-permute-done((f32[1,16,1,384]{3,1,2,0:T(8,128)S(1)}, f32[1,16,1,384]{3,1,2,0:T(8,128)S(1)}, u32[]{:S(2)}, u32[]{:S(2)}) %collective-permute-start) | collective-permute-done | bytes 24608 | tf_op jit(solution)/shard_map/ppermute | solution.py:19
  12.1 1.7 pad_maximum_fusion.4
  14.5 3.5 %collective-permute-start.3 = (f32[1,16,98,1]{2,1,3,0:T(8,128)S(1)}, f32[1,16,98,1]{2,1,3,0:T(8,128)S(1)}, u32[]{:S(2)}, u32[]{:S(2)}) collective-permute-start(f32[1,16,98,1]{2,1,3,0:T(8,128)S(1)} %copy.56), channel_id=1, source_target_pairs={{4,0},{8,4},{12,8},{16,12},{20,16},{24,20},{28,24},{0,28},{5,1},{9... | collective-permute-start | bytes 18824 | tf_op jit(solution)/shard_map/ppermute | solution.py:20
  18.0 4.6 %collective-permute-done.2 = f32[1,16,98,1]{2,1,3,0:T(8,128)S(1)} collective-permute-done((f32[1,16,98,1]{2,1,3,0:T(8,128)S(1)}, f32[1,16,98,1]{2,1,3,0:T(8,128)S(1)}, u32[]{:S(2)}, u32[]{:S(2)}) %collective-permute-start.2) | collective-permute-done | bytes 6304 | tf_op jit(solution)/shard_map/ppermute | solution.py:19
  22.6 1.3 copy.57
  25.1 3.6 %maximum_select_fusion = f32[1,16,98,386]{3,2,1,0:T(8,128)S(1)} fusion(f32[1,16,98,1]{3,2,1,0:T(8,128)} %copy.58, f32[1,16,1,384]{3,2,1,0:T(1,128)S(1)} %copy.54, f32[1,16,96,384]{3,2,1,0:T(8,128)} %param.3, f32[1,16,1,384]{3,2,1,0:T(1,128)S(1)} %copy.53, f32[1,16,98,1]{3,2,1,0:T(8,128)} %copy.57, pred[98]{0:T(512)(128)(4,1)S(1)} %and_or_fusion), kind=kLoop, calls=%fused_computation.4 | loop fusion | flops 3026240 | bytes 4842082 | tf_op jit(solution)/shard_map/jit(_where)/select_n | solution.py:61
  28.8 3.3 %slice.80 = f32[1,16,32,386]{3,2,1,0:T(8,128)} slice(f32[1,16,98,386]{3,2,1,0:T(8,128)S(1)} %maximum_select_fusion), slice={[0:1:1], [0:16:1], [4:98:3], [0:386:1]} | slice | bytes 1581056 | tf_op jit(solution)/shard_map/slice | solution.py:30
  32.1 3.1 %slice.79 = f32[1,16,32,386]{3,2,1,0:T(8,128)} slice(f32[1,16,98,386]{3,2,1,0:T(8,128)S(1)} %maximum_select_fusion), slice={[0:1:1], [0:16:1], [3:97:3], [0:386:1]} | slice | bytes 1581056 | tf_op jit(solution)/shard_map/slice | solution.py:30
  35.1 3.0 %slice.78 = f32[1,16,32,386]{3,2,1,0:T(8,128)} slice(f32[1,16,98,386]{3,2,1,0:T(8,128)S(1)} %maximum_select_fusion), slice={[0:1:1], [0:16:1], [2:96:3], [0:386:1]} | slice | bytes 1581056 | tf_op jit(solution)/shard_map/slice | solution.py:30
  38.1 3.0 %slice.77 = f32[1,16,32,386]{3,2,1,0:T(8,128)} slice(f32[1,16,98,386]{3,2,1,0:T(8,128)S(1)} %maximum_select_fusion), slice={[0:1:1], [0:16:1], [1:95:3], [0:386:1]} | slice | bytes 1581056 | tf_op jit(solution)/shard_map/slice | solution.py:30
  41.1 3.0 %slice.76 = f32[1,16,32,386]{3,2,1,0:T(8,128)} slice(f32[1,16,98,386]{3,2,1,0:T(8,128)S(1)} %maximum_select_fusion), slice={[0:1:1], [0:16:1], [0:94:3], [0:386:1]} | slice | bytes 1581056 | tf_op jit(solution)/shard_map/slice | solution.py:28
  44.1 3.1 %multiply_add_fusion = f32[1,16,32,386]{3,2,1,0:T(8,128)S(1)} fusion(f32[1,16,32,386]{3,2,1,0:T(8,128)} %slice.80, f32[1,16,32,386]{3,2,1,0:T(8,128)} %slice.79, f32[1,16,32,386]{3,2,1,0:T(8,128)} %slice.78, f32[1,16,32,386]{3,2,1,0:T(8,128)} %slice.77, f32[1,16,32,386]{3,2,1,0:T(8,128)} %slice.76), kind=kLoop, calls=%fused_computation.8 | loop fusion | flops 1778688 | bytes 4743168 | tf_op jit(solution)/shard_map/add | solution.py:30
  47.3 6.2 %slice.85 = f32[1,16,32,128]{3,2,1,0:T(8,128)S(1)} slice(f32[1,16,32,386]{3,2,1,0:T(8,128)S(1)} %multiply_add_fusion), slice={[0:1:1], [0:16:1], [0:32:1], [4:386:3]} | slice | bytes 524288 | tf_op jit(solution)/shard_map/slice | solution.py:33
  53.5 6.3 %slice.84 = f32[1,16,32,128]{3,2,1,0:T(8,128)S(1)} slice(f32[1,16,32,386]{3,2,1,0:T(8,128)S(1)} %multiply_add_fusion), slice={[0:1:1], [0:16:1], [0:32:1], [3:385:3]} | slice | bytes 524288 | tf_op jit(solution)/shard_map/slice | solution.py:33
  59.7 6.1 %slice.83 = f32[1,16,32,128]{3,2,1,0:T(8,128)S(1)} slice(f32[1,16,32,386]{3,2,1,0:T(8,128)S(1)} %multiply_add_fusion), slice={[0:1:1], [0:16:1], [0:32:1], [2:384:3]} | slice | bytes 524288 | tf_op jit(solution)/shard_map/slice | solution.py:33
  65.9 6.2 %slice.82 = f32[1,16,32,128]{3,2,1,0:T(8,128)S(1)} slice(f32[1,16,32,386]{3,2,1,0:T(8,128)S(1)} %multiply_add_fusion), slice={[0:1:1], [0:16:1], [0:32:1], [1:383:3]} | slice | bytes 524288 | tf_op jit(solution)/shard_map/slice | solution.py:33
  72.1 6.2 %slice.81 = f32[1,16,32,128]{3,2,1,0:T(8,128)S(1)} slice(f32[1,16,32,386]{3,2,1,0:T(8,128)S(1)} %multiply_add_fusion), slice={[0:1:1], [0:16:1], [0:32:1], [0:382:3]} | slice | bytes 524288 | tf_op jit(solution)/shard_map/slice | solution.py:31
  79.2 7.7 %all-to-all-start = ((f32[1,16,32,128]{3,2,0,1:T(8,128)}), f32[1,16,32,128]{3,2,0,1:T(8,128)S(1)}, u32[]{:S(2)}, u32[]{:S(2)}) async-start(f32[1,16,32,128]{3,2,0,1:T(8,128)} %add_bitcast_fusion), calls=%async_computation | async-start | bytes 524288 | tf_op jit(solution)/shard_map/all_to_all | solution.py:90
  86.9 6.7 %all-to-all-done = f32[1,16,32,128]{3,2,0,1:T(8,128)S(1)} async-done(((f32[1,16,32,128]{3,2,0,1:T(8,128)}), f32[1,16,32,128]{3,2,0,1:T(8,128)S(1)}, u32[]{:S(2)}, u32[]{:S(2)}) %all-to-all-start) | async-done | bytes 262176 | tf_op jit(solution)/shard_map/all_to_all | solution.py:90
  93.5 9.0 %fusion.4 = f32[4,80]{1,0:T(4,128)S(1)} fusion(f32[80,4,32,128]{3,2,1,0:T(8,128)} %param.4, f32[4,4,32,128]{3,2,1,0:T(8,128)S(1)} %bitcast.32), kind=kOutput, calls=%fused_computation.7 | convolution fusion | flops 62914560 | bytes 5506304 | tf_op jit(solution)/shard_map/klyx,mlyx->mk/dot_general | solution.py:75
  102.5 72.3 %psum.7 = f32[4,80]{1,0:T(4,128)S(1)} all-reduce(f32[4,80]{1,0:T(4,128)S(1)} %fusion.4), channel_id=1, replica_groups=mesh['lat'=8,'lon'=8,'mem'=4] {'lat','lon','mem'}, use_global_device_ids=true, to_apply=%region_0.1 | all-reduce | flops 320 | bytes 2560 | tf_op jit(solution)/shard_map/psum | solution.py:84
  174.8 7.7 %fusion = f32[4,4,32,128]{3,0,2,1:T(4,128)S(1)} fusion(f32[80,4,32,128]{3,2,1,0:T(8,128)} %param.4, f32[4,80]{1,0:T(4,128)S(1)} %broadcast_multiply_fusion), kind=kOutput, calls=%fused_computation | convolution fusion | flops 62914560 | bytes 5506304 | tf_op jit(solution)/shard_map/klyx,mk->mlyx/dot_general | solution.py:79
  182.6 9.6 %all_to_all.24 = f32[4,4,32,128]{3,2,1,0:T(8,128)S(1)} all-to-all(f32[4,4,32,128]{3,2,1,0:T(8,128)S(1)} %copy_add_fusion), channel_id=1, replica_groups=mesh['lat'=8,'lon'=8,'mem'=4] {'mem'}, dimensions={0} | all-to-all | bytes 524288 | tf_op jit(solution)/shard_map/all_to_all | solution.py:93
  192.2 1.9 collective-permute-start.4
  196.8 1.4 collective-permute-start.6
  198.2 2.5 %collective-permute-start.7 = (f32[1,16,34,1]{3,2,1,0:T(8,128)S(1)}, f32[1,16,34,1]{3,2,1,0:T(8,128)S(1)}, u32[]{:S(2)}, u32[]{:S(2)}) collective-permute-start(f32[1,16,34,1]{3,2,1,0:T(8,128)S(1)} %get-tuple-element.21), channel_id=1, source_target_pairs={{4,0},{8,4},{12,8},{16,12},{20,16},{24,20},{28,24},{0,28},{5,1},{9... | collective-permute-start | bytes 6536 | tf_op jit(solution)/shard_map/ppermute | solution.py:20
  200.7 10.2 %collective-permute-done.6 = f32[1,16,34,1]{3,2,1,0:T(8,128)S(1)} collective-permute-done((f32[1,16,34,1]{3,2,1,0:T(8,128)S(1)}, f32[1,16,34,1]{3,2,1,0:T(8,128)S(1)}, u32[]{:S(2)}, u32[]{:S(2)}) %collective-permute-start.6) | collective-permute-done | bytes 2208 | tf_op jit(solution)/shard_map/ppermute | solution.py:19
  210.9 2.8 %collective-permute-done.7 = f32[1,16,34,1]{3,2,1,0:T(8,128)S(1)} collective-permute-done((f32[1,16,34,1]{3,2,1,0:T(8,128)S(1)}, f32[1,16,34,1]{3,2,1,0:T(8,128)S(1)}, u32[]{:S(2)}, u32[]{:S(2)}) %collective-permute-start.7) | collective-permute-done | bytes 2208 | tf_op jit(solution)/shard_map/ppermute | solution.py:20
  215.9 1.6 pad_maximum_fusion
  217.4 2.4 %copy.67 = f32[1,16,96,128,3]{2,1,4,3,0:T(8,128)S(1)} copy(f32[1,16,96,128,3]{3,1,2,4,0:T(8,128)} %pad_maximum_fusion) | data formatting | bytes 4718592 | tf_op jit(solution)/shard_map/stack | solution.py:47
  219.9 2.2 copy.68
  (33 shorter events, 9.7 us)
Async XLA Ops:
  1.7 7.4 %collective-permute-start.1 = (f32[1,16,1,384]{3,1,2,0:T(8,128)S(1)}, f32[1,16,1,384]{3,1,2,0:T(8,128)S(1)}, u32[]{:S(2)}, u32[]{:S(2)}) collective-permute-start(f32[1,16,1,384]{3,1,2,0:T(8,128)S(1)} %copy.73), channel_id=1, source_target_pairs={{32,0},{64,32},{96,64},{128,96},{160,128},{192,160},{224,192},{0,2... | collective-permute-start | bytes 73736 | tf_op jit(solution)/shard_map/ppermute | solution.py:20
  8.2 3.9 %collective-permute-start = (f32[1,16,1,384]{3,1,2,0:T(8,128)S(1)}, f32[1,16,1,384]{3,1,2,0:T(8,128)S(1)}, u32[]{:S(2)}, u32[]{:S(2)}) collective-permute-start(f32[1,16,1,384]{3,1,2,0:T(8,128)S(1)} %copy.72), channel_id=1, source_target_pairs={{0,32},{32,64},{64,96},{96,128},{128,160},{160,192},{192,224},{224... | collective-permute-start | bytes 73736 | tf_op jit(solution)/shard_map/ppermute | solution.py:19
  14.5 9.4 %collective-permute-start.3 = (f32[1,16,98,1]{2,1,3,0:T(8,128)S(1)}, f32[1,16,98,1]{2,1,3,0:T(8,128)S(1)}, u32[]{:S(2)}, u32[]{:S(2)}) collective-permute-start(f32[1,16,98,1]{2,1,3,0:T(8,128)S(1)} %copy.56), channel_id=1, source_target_pairs={{4,0},{8,4},{12,8},{16,12},{20,16},{24,20},{28,24},{0,28},{5,1},{9... | collective-permute-start | bytes 18824 | tf_op jit(solution)/shard_map/ppermute | solution.py:20
  18.0 4.6 %collective-permute-start.2 = (f32[1,16,98,1]{2,1,3,0:T(8,128)S(1)}, f32[1,16,98,1]{2,1,3,0:T(8,128)S(1)}, u32[]{:S(2)}, u32[]{:S(2)}) collective-permute-start(f32[1,16,98,1]{2,1,3,0:T(8,128)S(1)} %copy.55), channel_id=1, source_target_pairs={{0,4},{4,8},{8,12},{12,16},{16,20},{20,24},{24,28},{28,0},{1,5},{5... | collective-permute-start | bytes 18824 | tf_op jit(solution)/shard_map/ppermute | solution.py:19
  47.3 39.6 %copy-start.1 = (f32[80]{0:T(128)S(1)}, f32[80]{0:T(128)}, u32[]{:S(2)}) copy-start(f32[80]{0:T(128)} %param.5) | copy-start | bytes 964
  79.2 14.4 %all-to-all-start = ((f32[1,16,32,128]{3,2,0,1:T(8,128)}), f32[1,16,32,128]{3,2,0,1:T(8,128)S(1)}, u32[]{:S(2)}, u32[]{:S(2)}) async-start(f32[1,16,32,128]{3,2,0,1:T(8,128)} %add_bitcast_fusion), calls=%async_computation | async-start | bytes 524288 | tf_op jit(solution)/shard_map/all_to_all | solution.py:90
  174.8 17.4 %copy-start = (f32[4,80]{1,0:T(4,128)}, f32[4,80]{1,0:T(4,128)S(1)}, u32[]{:S(2)}) copy-start(f32[4,80]{1,0:T(4,128)S(1)} %broadcast_multiply_fusion) | copy-start | bytes 3844
  192.2 3.8 %collective-permute-start.4 = (f32[1,16,1,128]{3,2,1,0:T(1,128)S(1)}, f32[1,16,1,128]{3,2,1,0:T(1,128)S(1)}, u32[]{:S(2)}, u32[]{:S(2)}) collective-permute-start(f32[1,16,1,128]{3,2,1,0:T(1,128)S(1)} %get-tuple-element.22), channel_id=1, source_target_pairs={{0,32},{32,64},{64,96},{96,128},{128,160},{160,192},{192,224},{224... | collective-permute-start | bytes 24584 | tf_op jit(solution)/shard_map/ppermute | solution.py:19
  194.1 2.5 %collective-permute-start.5 = (f32[1,16,1,128]{3,2,1,0:T(1,128)S(1)}, f32[1,16,1,128]{3,2,1,0:T(1,128)S(1)}, u32[]{:S(2)}, u32[]{:S(2)}) collective-permute-start(f32[1,16,1,128]{3,2,1,0:T(1,128)S(1)} %get-tuple-element.23), channel_id=1, source_target_pairs={{32,0},{64,32},{96,64},{128,96},{160,128},{192,160},{224,192},{0,2... | collective-permute-start | bytes 24584 | tf_op jit(solution)/shard_map/ppermute | solution.py:20
  196.8 14.1 %collective-permute-start.6 = (f32[1,16,34,1]{3,2,1,0:T(8,128)S(1)}, f32[1,16,34,1]{3,2,1,0:T(8,128)S(1)}, u32[]{:S(2)}, u32[]{:S(2)}) collective-permute-start(f32[1,16,34,1]{3,2,1,0:T(8,128)S(1)} %get-tuple-element.20), channel_id=1, source_target_pairs={{0,4},{4,8},{8,12},{12,16},{16,20},{20,24},{24,28},{28,0},{1,5},{5... | collective-permute-start | bytes 6536 | tf_op jit(solution)/shard_map/ppermute | solution.py:19
  198.2 15.5 %collective-permute-start.7 = (f32[1,16,34,1]{3,2,1,0:T(8,128)S(1)}, f32[1,16,34,1]{3,2,1,0:T(8,128)S(1)}, u32[]{:S(2)}, u32[]{:S(2)}) collective-permute-start(f32[1,16,34,1]{3,2,1,0:T(8,128)S(1)} %get-tuple-element.21), channel_id=1, source_target_pairs={{4,0},{8,4},{12,8},{16,12},{20,16},{24,20},{28,24},{0,28},{5,1},{9... | collective-permute-start | bytes 6536 | tf_op jit(solution)/shard_map/ppermute | solution.py:20
where the time goes:
time: 222 us
  blocking collectives  81.9 us (37%)
  local copies, waits for them, and re-layouts  56.3 us (25%)
  waiting for transfers between devices  29.7 us (13%)
  starting transfers between devices  24.4 us (11%)
  matrix products  16.7 us (8%)
  other arithmetic  12.2 us (5%)
    psum x1, blocking collectives, finish_coefficients(): projections = lax.psum(partial_sums, ('lat', 'lon', 'mem')) * (1.0 / cells)  72.3 us
    slice x4, local copies, waits for them, and re-layouts, restrict_padded(): result = result + TENT[offset] * along[..., offset:offset + 3 * cols - 2:3]  24.8 us
    ppermute x4, waiting for transfers between devices, padded_2(): before = lax.ppermute(last, axis, up)  18.7 us
    ppermute x4, starting transfers between devices, padded_2(): after = lax.ppermute(leading, axis, down)  13.4 us
    slice x4, local copies, waits for them, and re-layouts, restrict_padded(): padded[..., offset:offset + 3 * rows - 2:3, :]  12.3 us
    all_to_all x1, blocking collectives, per_device(): lax.all_to_all(corrected, 'mem', split_axis=0, concat_axis=1, tiled=True)  9.63 us
    dot_general x1, matrix products, levels_products(): jnp.einsum('klyx,mlyx->mk', ritz_vectors, coarse, precision=lax.Precision...  9 us
    dot_general x1, matrix products, levels_update(): jnp.einsum('klyx,mk->mlyx', ritz_vectors, coefficients, precision=lax.Pre...  7.74 us
  transfers between devices with their start and end apart: 9, of which 8 were waited for; matrix products, arithmetic and copies ran while one was open for 1% of the time, Pallas kernels for 0%

commit v1 on v0

v1 whole, which is shorter than its diff:
```python
import jax
import jax.numpy as jnp
from jax import lax
from jax.experimental import pallas as pl
from jax.experimental.pallas import tpu as pltpu
from jax.sharding import PartitionSpec as P

F32 = jnp.float32
BF16 = jnp.bfloat16
RITZ = 80
GROUPS = 4
DEPTH = 4
ROWS = 32
COLS = 128
MAIN = DEPTH * ROWS
HALO = 16
BLOCK = MAIN + HALO
EDGE_ROWS = 16 * GROUPS
BAND = EDGE_ROWS + DEPTH * RITZ
SIDE = 2 * RITZ + 4 * GROUPS
CHUNK = 8
VMEM_LIMIT = 40 * 1024 * 1024


def iota(shape, dim):
    return lax.broadcasted_iota(jnp.int32, shape, dim)


def diagonal(rows):
    return iota((rows, COLS), 0) == iota((rows, COLS), 1)


def column_to_row(column, mask):
    spread = jnp.broadcast_to(column, mask.shape)
    return jnp.sum(jnp.where(mask, spread, 0.0), axis=0, keepdims=True)


def row_to_column(row, mask):
    spread = jnp.broadcast_to(row, mask.shape)
    return jnp.sum(jnp.where(mask, spread, 0.0), axis=1, keepdims=True)


def stack_rows(rows):
    position = iota((8, COLS), 0)
    result = jnp.zeros((8, COLS), F32)
    for index, row in enumerate(rows):
        result = jnp.where(position == index, jnp.broadcast_to(row, (8, COLS)), result)
    return result


def dot_split(value, weights):
    high = value.astype(BF16)
    low = (value - high.astype(F32)).astype(BF16)
    return jnp.dot(high, weights, preferred_element_type=F32) + jnp.dot(low, weights, preferred_element_type=F32)


def restrict_kernel(
    where_ref, g0_ref, g1_ref, g2_ref, first_ref, last_ref, x_ref, e_ref, h_ref, down_ref, up_ref, a_ref, w_ref
):
    step = pl.program_id(0)

    @pl.when(step == 0)
    def _():
        fine = iota((3 * COLS, 2 * COLS), 0)
        coarse = iota((3 * COLS, 2 * COLS), 1)
        tent = jnp.maximum(3 - jnp.abs(fine - 3 * coarse - 1), 0)
        left = jnp.logical_and(coarse == COLS, fine == 0)
        right = jnp.logical_and(coarse == COLS + 1, fine == 3 * COLS - 1)
        outer = jnp.where(jnp.logical_or(left, right), 1, 0)
        w_ref[...] = jnp.where(coarse < COLS, tent, outer).astype(F32).astype(BF16)

    position = iota((ROWS, COLS), 0)
    for part, g_ref in enumerate((g0_ref, g1_ref, g2_ref)):
        lanes = slice(COLS * part, COLS * (part + 1))
        for level in range(DEPTH):
            first = g_ref[0, level, pl.ds(0, ROWS, stride=3), :]
            middle = g_ref[0, level, pl.ds(1, ROWS, stride=3), :]
            third = g_ref[0, level, pl.ds(2, ROWS, stride=3), :]
            before = jnp.where(position == 0, 0.0, pltpu.roll(third, 1, 0))
            after = jnp.where(position == ROWS - 1, 0.0, pltpu.roll(first, ROWS - 1, 0))
            a_ref[ROWS * level : ROWS * (level + 1), lanes] = before + after + 2.0 * (first + third) + 3.0 * middle
            a_ref[MAIN + level : MAIN + level + 1, lanes] = first[0:1]
            a_ref[MAIN + DEPTH + level : MAIN + DEPTH + level + 1, lanes] = third[ROWS - 1 : ROWS]
    coarse = dot_split(a_ref[...], w_ref[...]) * (1.0 / 81.0)
    main, edge = coarse[:MAIN], coarse[MAIN:]
    e_ref[0] = main
    h_ref[0] = edge
    x_ref[0, :MAIN] = main[:, :COLS]
    x_ref[0, MAIN : MAIN + 8] = edge[:, :COLS]
    square, corner = diagonal(MAIN), diagonal(8)
    sides = []
    for lane in (COLS, COLS + 1):
        sides.append(column_to_row(main[:, lane : lane + 1], square))
        sides.append(column_to_row(edge[:, lane : lane + 1], corner))
    x_ref[0, MAIN + 8 : BLOCK] = stack_rows(sides)
    for ref, row, half in ((down_ref, ROWS - 1, edge[DEPTH:]), (up_ref, 0, edge[:DEPTH])):
        inner = [main[ROWS * level + row : ROWS * level + row + 1] for level in range(DEPTH)]
        sent = jnp.concatenate(inner + [half], axis=0)
        ref[pl.ds(16 * step, 8), :] = sent[:, :COLS]
        ref[pl.ds(16 * step + 8, 8), :] = sent[:, COLS:]
    down_ref[pl.ds(EDGE_ROWS + RITZ * step, RITZ), :] = last_ref[:, 0, 7, :]
    up_ref[pl.ds(EDGE_ROWS + RITZ * step, RITZ), :] = first_ref[:, 0, 0, :]


def sides_kernel(v_ref, above_ref, below_ref, e_ref, h_ref, left_ref, right_ref, e2_ref, h2_ref):
    step = pl.program_id(0)
    square, corner = diagonal(MAIN), diagonal(8)
    lanes = iota((CHUNK, COLS), 1)
    base = pl.multiple_of(step * CHUNK, CHUNK)
    for ref, lane in ((left_ref, 0), (right_ref, COLS - 1)):
        rows = []
        for k in range(CHUNK):
            vector = v_ref[k].reshape(MAIN, COLS)
            rows.append(column_to_row(vector[:, lane : lane + 1], square))
        ref[pl.ds(base, CHUNK), :] = stack_rows(rows)
        corners = jnp.zeros((CHUNK, COLS), F32)
        for index, source in ((0, above_ref), (DEPTH, below_ref)):
            for level in range(DEPTH):
                part = source[pl.ds(EDGE_ROWS + RITZ * level + base, CHUNK), :]
                spread = jnp.broadcast_to(part[:, lane : lane + 1], (CHUNK, COLS))
                corners = jnp.where(lanes == index + level, spread, corners)
        ref[pl.ds(RITZ + base, CHUNK), :] = corners

    @pl.when(step == 0)
    def _():
        position = iota((ROWS, 2 * COLS), 0)
        packed = ([], [])
        for group in range(GROUPS):
            start = 16 * group
            above = jnp.concatenate([above_ref[start : start + 8, :], above_ref[start + 8 : start + 16, :]], axis=1)
            below = jnp.concatenate([below_ref[start : start + 8, :], below_ref[start + 8 : start + 16, :]], axis=1)
            for level in range(DEPTH):
                rows = slice(ROWS * level, ROWS * (level + 1))
                tile = e_ref[group, rows, :]
                tile = tile + jnp.where(position == 0, above[DEPTH + level : DEPTH + level + 1, :], 0.0)
                tile = tile + jnp.where(position == ROWS - 1, below[DEPTH + level : DEPTH + level + 1, :], 0.0)
                e2_ref[group, rows, :] = tile
            edge = h_ref[group] + jnp.concatenate([above[:DEPTH], below[:DEPTH]], axis=0)
            h2_ref[group] = edge
            main = e2_ref[group]
            for rows, lane, outer in ((packed[0], 0, COLS), (packed[1], COLS - 1, COLS + 1)):
                for source in (lane, outer):
                    rows.append(column_to_row(main[:, source : source + 1], square))
                    rows.append(column_to_row(edge[:, source : source + 1], corner))
        for ref, rows in ((left_ref, packed[0]), (right_ref, packed[1])):
            ref[2 * RITZ : 2 * RITZ + 8, :] = stack_rows(rows[:8])
            ref[2 * RITZ + 8 : 2 * RITZ + 16, :] = stack_rows(rows[8:])


def edge_parts(above_ref, below_ref, left_ref, right_ref, start, count):
    parts = []
    for source in (above_ref, below_ref):
        for level in range(DEPTH):
            parts.append(source[pl.ds(EDGE_ROWS + RITZ * level + start, count), :])
    for source in (left_ref, right_ref):
        parts.append(source[pl.ds(start, count), :])
        parts.append(source[pl.ds(RITZ + start, count), :])
    return parts


def project_kernel(
    where_ref, v_ref, c0_ref, c1_ref, c2_ref, c3_ref, above_ref, below_ref, left_ref, right_ref, p_ref, s_ref
):
    step = pl.program_id(0)
    base = pl.multiple_of(step * CHUNK, CHUNK)
    blocks = (c0_ref, c1_ref, c2_ref, c3_ref)
    sums = [[jnp.zeros((8, COLS), F32) for _ in range(CHUNK)] for _ in blocks]
    for tile in range(MAIN // 8):
        level, row = divmod(8 * tile, ROWS)
        fields = [block[8 * tile : 8 * tile + 8, :] for block in blocks]
        for k in range(CHUNK):
            vector = v_ref[k, level, row : row + 8, :]
            for member in range(GROUPS):
                sums[member][k] = sums[member][k] + vector * fields[member]
    parts = edge_parts(above_ref, below_ref, left_ref, right_ref, base, CHUNK)
    for member in range(GROUPS):
        total = stack_rows([jnp.sum(value, axis=0, keepdims=True) for value in sums[member]])
        for index, part in enumerate(parts):
            total = total + part * blocks[member][MAIN + index : MAIN + index + 1, :]
        s_ref[member, pl.ds(base, CHUNK), :] = total

    @pl.when(step == pl.num_programs(0) - 1)
    def _():
        ones = jnp.ones((8, COLS), F32)
        for member in range(GROUPS):
            reduced = lax.dot_general(
                ones,
                s_ref[member],
                (((1,), (1,)), ((), ())),
                precision=lax.Precision.HIGHEST,
                preferred_element_type=F32,
            )
            p_ref[pl.ds(where_ref[0] ^ member, 1), :] = reduced[0:1, :]


def update_kernel(
    where_ref, c_ref, cv_ref, v_ref, above_ref, below_ref, left_ref, right_ref, u0_ref, u1_ref, u2_ref, u3_ref, t_ref
):
    step = pl.program_id(0)
    me = where_ref[0]
    outs = (u0_ref, u1_ref, u2_ref, u3_ref)

    def body(index, sums):
        sums = list(sums)
        for offset in range(CHUNK):
            k = index * CHUNK + offset
            weights = [c_ref[me ^ member, k] for member in range(GROUPS)]
            vector = v_ref[k, 0]
            for member in range(GROUPS):
                sums[member] = sums[member] + weights[member] * vector
        return tuple(sums)

    zeros = tuple(jnp.zeros((ROWS, COLS), F32) for _ in outs)
    sums = lax.fori_loop(0, RITZ // CHUNK, body, zeros)
    for member in range(GROUPS):
        outs[member][pl.ds(pl.multiple_of(step * ROWS, ROWS), ROWS), :] = sums[member]

    @pl.when(step == 0)
    def _():
        parts = edge_parts(above_ref, below_ref, left_ref, right_ref, 0, RITZ)
        for index, part in enumerate(parts):
            t_ref[index] = jnp.dot(
                cv_ref[...], part, precision=lax.Precision.HIGHEST, preferred_element_type=F32
            )
        for member in range(GROUPS):
            for index in range(len(parts)):
                outs[member][MAIN + index : MAIN + index + 1, :] = t_ref[index, pl.ds(me ^ member, 1), :]
            outs[member][MAIN + 12 : BLOCK, :] = jnp.zeros((4, COLS), F32)


def prolong_kernel(
    where_ref, r0_ref, r1_ref, r2_ref, r3_ref, e2_ref, h2_ref, left_ref, right_ref, o_ref, r_ref, a_ref, f_ref, z_ref, m_ref
):
    step = pl.program_id(0)

    @pl.when(step == 0)
    def _():
        coarse = iota((2 * COLS, 3 * COLS), 0)
        fine = iota((2 * COLS, 3 * COLS), 1)
        tent = jnp.maximum(3 - jnp.abs(fine - 3 * coarse - 1), 0)
        left = jnp.logical_and(coarse == COLS, fine == 0)
        right = jnp.logical_and(coarse == COLS + 1, fine == 3 * COLS - 1)
        outer = jnp.where(jnp.logical_or(left, right), 1, 0)
        z_ref[...] = jnp.where(coarse < COLS, tent, outer).astype(F32).astype(BF16)

    for member, ref in enumerate((r0_ref, r1_ref, r2_ref, r3_ref)):

        @pl.when(step == member)
        def _(ref=ref):
            r_ref[...] = ref[...]

    square, corner = diagonal(MAIN), diagonal(8)
    start = 2 * RITZ + 4 * step
    halves = []
    for index, (rows, mask, edge) in enumerate(((MAIN, square, e2_ref), (8, corner, h2_ref))):
        offset = MAIN * index
        lanes = iota((rows, COLS), 1)
        value = edge[0, :, :COLS] + r_ref[offset : offset + rows, :]
        outer = edge[0, :, COLS:]
        for slot, (ref, lane) in enumerate(((left_ref, 0), (right_ref, COLS - 1))):
            beyond = ref[pl.ds(start + index, 1), :] + r_ref[MAIN + 8 + 2 * slot + index : MAIN + 9 + 2 * slot + index, :]
            inner = ref[pl.ds(start + 2 + index, 1), :]
            outer = outer + jnp.where(lanes == slot, row_to_column(beyond, mask), 0.0)
            value = value + jnp.where(lanes == lane, row_to_column(inner, mask), 0.0)
        halves.append((value, outer))
    a_ref[:MAIN, :COLS] = halves[0][0]
    a_ref[:MAIN, COLS:] = halves[0][1]
    position = iota((8, COLS), 0)
    keep_above = jnp.where(position < DEPTH, where_ref[1], where_ref[2]).astype(F32)
    a_ref[MAIN:, :COLS] = halves[1][0] * keep_above
    a_ref[MAIN:, COLS:] = halves[1][1] * keep_above
    f_ref[...] = dot_split(a_ref[...], z_ref[...])
    position = iota((ROWS, 3 * COLS), 0)
    for level in range(DEPTH):
        center = f_ref[ROWS * level : ROWS * (level + 1), :]
        above = f_ref[MAIN + level : MAIN + level + 1, :]
        below = f_ref[MAIN + DEPTH + level : MAIN + DEPTH + level + 1, :]
        before = jnp.where(position == 0, above, pltpu.roll(center, 1, 0))
        after = jnp.where(position == ROWS - 1, below, pltpu.roll(center, ROWS - 1, 0))
        fine = ((2.0 * center + before) * (1.0 / 9.0), center * (1.0 / 3.0), (2.0 * center + after) * (1.0 / 9.0))
        for part in range(3):
            lanes = slice(COLS * part, COLS * (part + 1))
            for offset, value in enumerate(fine):
                m_ref[level, part, pl.ds(offset, ROWS, stride=3), :] = value[:, lanes]
            o_ref[0, level, :, lanes] = m_ref[level, part]


def whole(shape):
    return pl.BlockSpec(shape, lambda i, *_: (0,) * len(shape))


def struct(*shape):
    return jax.ShapeDtypeStruct(shape, F32)


def params():
    return pltpu.CompilerParams(vmem_limit_bytes=VMEM_LIMIT)


def restrict(place, gradients, ritz_vectors):
    return pl.pallas_call(
        restrict_kernel,
        grid_spec=pltpu.PrefetchScalarGridSpec(
            num_scalar_prefetch=1,
            grid=(GROUPS,),
            in_specs=[
                pl.BlockSpec((1, DEPTH, 3 * ROWS, COLS), lambda i, place: (0, i ^ place[0], 0, 0)),
                pl.BlockSpec((1, DEPTH, 3 * ROWS, COLS), lambda i, place: (0, i ^ place[0], 0, 1)),
                pl.BlockSpec((1, DEPTH, 3 * ROWS, COLS), lambda i, place: (0, i ^ place[0], 0, 2)),
                pl.BlockSpec((RITZ, 1, 8, COLS), lambda i, place: (0, i, 0, 0)),
                pl.BlockSpec((RITZ, 1, 8, COLS), lambda i, place: (0, i, ROWS // 8 - 1, 0)),
            ],
            out_specs=[
                pl.BlockSpec((1, BLOCK, COLS), lambda i, place: (i, 0, 0)),
                pl.BlockSpec((1, MAIN, 2 * COLS), lambda i, place: (i, 0, 0)),
                pl.BlockSpec((1, 8, 2 * COLS), lambda i, place: (i, 0, 0)),
                whole((BAND, COLS)),
                whole((BAND, COLS)),
            ],
            scratch_shapes=[
                pltpu.VMEM((MAIN + 8, 3 * COLS), F32),
                pltpu.VMEM((3 * COLS, 2 * COLS), BF16),
            ],
        ),
        out_shape=[
            struct(GROUPS, BLOCK, COLS),
            struct(GROUPS, MAIN, 2 * COLS),
            struct(GROUPS, 8, 2 * COLS),
            struct(BAND, COLS),
            struct(BAND, COLS),
        ],
        compiler_params=params(),
        name="restrict",
    )(place, gradients, gradients, gradients, ritz_vectors, ritz_vectors)


def sides(ritz_vectors, above, below, main, edge):
    return pl.pallas_call(
        sides_kernel,
        grid=(RITZ // CHUNK,),
        in_specs=[
            pl.BlockSpec((CHUNK, DEPTH, ROWS, COLS), lambda i: (i, 0, 0, 0)),
            whole((BAND, COLS)),
            whole((BAND, COLS)),
            whole((GROUPS, MAIN, 2 * COLS)),
            whole((GROUPS, 8, 2 * COLS)),
        ],
        out_specs=[
            whole((SIDE, COLS)),
            whole((SIDE, COLS)),
            whole((GROUPS, MAIN, 2 * COLS)),
            whole((GROUPS, 8, 2 * COLS)),
        ],
        out_shape=[
            struct(SIDE, COLS),
            struct(SIDE, COLS),
            struct(GROUPS, MAIN, 2 * COLS),
            struct(GROUPS, 8, 2 * COLS),
        ],
        compiler_params=params(),
        name="sides",
    )(ritz_vectors, above, below, main, edge)


def project(place, ritz_vectors, blocks, messages):
    return pl.pallas_call(
        project_kernel,
        grid_spec=pltpu.PrefetchScalarGridSpec(
            num_scalar_prefetch=1,
            grid=(RITZ // CHUNK,),
            in_specs=[pl.BlockSpec((CHUNK, DEPTH, ROWS, COLS), lambda i, place: (i, 0, 0, 0))]
            + [whole((BLOCK, COLS))] * 4
            + [whole((BAND, COLS))] * 2
            + [whole((SIDE, COLS))] * 2,
            out_specs=whole((GROUPS, RITZ)),
            scratch_shapes=[pltpu.VMEM((GROUPS, RITZ, COLS), F32)],
        ),
        out_shape=struct(GROUPS, RITZ),
        compiler_params=params(),
        name="project",
    )(place, ritz_vectors, *blocks, *messages)


def update(place, coefficients, ritz_vectors, messages):
    return pl.pallas_call(
        update_kernel,
        grid_spec=pltpu.PrefetchScalarGridSpec(
            num_scalar_prefetch=1,
            grid=(DEPTH,),
            in_specs=[
                pl.BlockSpec(memory_space=pltpu.SMEM),
                whole((8, RITZ)),
                pl.BlockSpec((RITZ, 1, ROWS, COLS), lambda i, place: (0, i, 0, 0)),
            ]
            + [whole((BAND, COLS))] * 2
            + [whole((SIDE, COLS))] * 2,
            out_specs=[whole((BLOCK, COLS))] * 4,
            scratch_shapes=[pltpu.VMEM((12, 8, COLS), F32)],
        ),
        out_shape=[struct(BLOCK, COLS)] * 4,
        compiler_params=params(),
        name="update",
    )(place, coefficients, jnp.concatenate([coefficients, coefficients], axis=0), ritz_vectors, *messages)


def prolong(place, returned, main, edge, left, right):
    return pl.pallas_call(
        prolong_kernel,
        grid_spec=pltpu.PrefetchScalarGridSpec(
            num_scalar_prefetch=1,
            grid=(GROUPS,),
            in_specs=[whole((BLOCK, COLS))] * 4
            + [
                pl.BlockSpec((1, MAIN, 2 * COLS), lambda i, place: (i, 0, 0)),
                pl.BlockSpec((1, 8, 2 * COLS), lambda i, place: (i, 0, 0)),
                whole((SIDE, COLS)),
                whole((SIDE, COLS)),
            ],
            out_specs=pl.BlockSpec((1, DEPTH, 3 * ROWS, 3 * COLS), lambda i, place: (0, i ^ place[0], 0, 0)),
            scratch_shapes=[
                pltpu.VMEM((BLOCK, COLS), F32),
                pltpu.VMEM((MAIN + 8, 2 * COLS), F32),
                pltpu.VMEM((MAIN + 8, 3 * COLS), F32),
                pltpu.VMEM((2 * COLS, 3 * COLS), BF16),
                pltpu.VMEM((DEPTH, 3, 3 * ROWS, COLS), F32),
            ],
        ),
        out_shape=struct(1, GROUPS * DEPTH, 3 * ROWS, 3 * COLS),
        compiler_params=params(),
        name="prolong",
    )(place, *returned, main, edge, left, right)


def exchange_members(blocks):
    size = lax.axis_size("mem")
    return [blocks[0]] + [
        lax.ppermute(blocks[shift], "mem", [(i, i ^ shift) for i in range(size)]) for shift in range(1, size)
    ]


def exchange_sum(value, axes):
    size = lax.axis_size(axes)
    copies = jnp.broadcast_to(value[None], (size,) + value.shape)
    return jnp.sum(lax.all_to_all(copies, axes, 0, 0, tiled=True), axis=0)


def per_device(gradients, ritz_vectors, ritz_values):
    lats, lons = lax.axis_size("lat"), lax.axis_size("lon")
    lat, mem = lax.axis_index("lat"), lax.axis_index("mem")
    place = jnp.stack([mem, jnp.where(lat > 0, 1, 0), jnp.where(lat < lats - 1, 1, 0)]).astype(jnp.int32)

    blocks, main, edge, down, up = restrict(place, gradients, ritz_vectors)
    above = lax.ppermute(down, "lat", [(i, i + 1) for i in range(lats - 1)])
    below = lax.ppermute(up, "lat", [(i + 1, i) for i in range(lats - 1)])
    spread = exchange_members([blocks[i] for i in range(GROUPS)])
    to_left, to_right, main, edge = sides(ritz_vectors, above, below, main, edge)
    right = lax.ppermute(to_left, "lon", [((i + 1) % lons, i) for i in range(lons)])
    left = lax.ppermute(to_right, "lon", [(i, (i + 1) % lons) for i in range(lons)])
    messages = (above, below, left, right)

    partial = project(place, ritz_vectors, spread, messages)
    projections = exchange_sum(exchange_sum(partial, ("lon", "mem")), "lat")
    cells = GROUPS * DEPTH * ROWS * lats * COLS * lons
    coefficients = (1.0 / ritz_values - 1.0)[None, :] * (projections * (1.0 / cells))

    returned = exchange_members(update(place, coefficients, ritz_vectors, messages))
    preconditioned = prolong(place, returned, main, edge, left, right)
    return preconditioned, coefficients


def solution(mesh):
    placed = (P("mem", None, "lat", "lon"), P(None, "mem", "lat", "lon"), P())
    return jax.shard_map(
        per_device,
        mesh=mesh,
        in_specs=placed,
        out_specs=(P("mem", None, "lat", "lon"), P()),
        check_vma=False,
    )
```

time: 222 us -> 87.2 us (0.39)
  blocking collectives: 81.9 us -> 11.9 us
  local copies, waits for them, and re-layouts: 56.3 us -> 7.3 us
  Pallas kernels: 0 us -> 17.5 us
  matrix products: 16.7 us -> 0 us
  other arithmetic: 12.2 us -> 0.16 us
  waiting for transfers between devices: 29.7 us -> 21.4 us
  starting transfers between devices: 24.4 us -> 27.9 us
    psum x1 -> x0, blocking collectives: 72.3 us -> none  [finish_coefficients(): projections = lax.psum(partial_sums, ('lat', 'lon', 'mem')) * (1.0 / cells)]
    slice x15 -> x0, local copies, waits for them, and re-layouts: 48.2 us -> none  [the longest x4 24.8 us: restrict_padded(): result = result + TENT[offset] * along[..., offset:offset + 3 * cols - 2:3]]
    pallas_call x0 -> x5, Pallas kernels: none -> 17.5 us  [the longest x1 4.05 us: update(): pl.pallas_call(update_kernel, grid_spec=pltpu.PrefetchScalarGridSpec(num_...]
    dot_general x2 -> x0, matrix products: 16.7 us -> none  [the longest x1 9 us: levels_products(): jnp.einsum('klyx,mlyx->mk', ritz_vectors, coarse, precision=lax.Precision...]
    ppermute x8 -> x10, waiting for transfers between devices: 23.1 us -> 14.8 us  [the longest x6 8.34 us: exchange_members(): lax.ppermute(blocks[shift], 'mem', [(i, i ^ shift) for i in range(size)])]
    unnamed x7 -> x12, local copies, waits for them, and re-layouts: 2.2 us -> 6.65 us
    select_n x2 -> x0, other arithmetic: 4.03 us -> none  [clear_ends(): return jnp.where(dropped, jnp.zeros_like(padded), padded)]
    add x3 -> x0, other arithmetic: 4.03 us -> none  [the longest x1 3.15 us: restrict_padded(): along + TENT[offset] * padded[..., offset:offset + 3 * rows - 2:3, :]]
  transfers between devices with their start and end apart: 9 -> 11, of which waited for: 8 -> 7; matrix products, arithmetic and copies ran while one was open for 1% -> 0% of each run, Pallas kernels for 0% -> 0%
where the time goes in v1:
time: 87.2 us; the launch traced here: 86.9 us
  starting transfers between devices  27.9 us (32%)
  waiting for transfers between devices  21.4 us (25%)
  Pallas kernels  17.5 us (20%)
  blocking collectives  11.9 us (14%)
  local copies, waits for them, and re-layouts  7.3 us (8%)
    all_to_all x1, blocking collectives, exchange_sum(): return jnp.sum(lax.all_to_all(copies, axes, 0, 0, tiled=True), axis=0)  11.9 us
    ppermute x6, starting transfers between devices, exchange_members(): lax.ppermute(blocks[shift], 'mem', [(i, i ^ shift) for i in range(size)])  10.7 us
    ppermute x6, waiting for transfers between devices, exchange_members(): lax.ppermute(blocks[shift], 'mem', [(i, i ^ shift) for i in range(size)])  8.34 us
    all_to_all x1, starting transfers between devices, exchange_sum(): return jnp.sum(lax.all_to_all(copies, axes, 0, 0, tiled=True), axis=0)  7.85 us
    unnamed x12, local copies, waits for them, and re-layouts  6.65 us
    all_to_all x1, waiting for transfers between devices, exchange_sum(): return jnp.sum(lax.all_to_all(copies, axes, 0, 0, tiled=True), axis=0)  6.61 us
    ppermute x1, starting transfers between devices, per_device(): above = lax.ppermute(down, 'lat', [(i, i + 1) for i in range(lats - 1)])  4.38 us
    ppermute x1, waiting for transfers between devices, per_device(): below = lax.ppermute(up, 'lat', [(i + 1, i) for i in range(lats - 1)])  4.18 us
  transfers between devices with their start and end apart: 11, of which 7 were waited for; matrix products, arithmetic and copies ran while one was open for 0% of the time, Pallas kernels for 0%

profile of v1, /device:TPU:1, one launch (start us, length us, event | category | flops | bytes accessed | tf_op | source)
XLA Modules:
  0.0 86.9 jit_solution(12731421265314810642)
XLA Ops:
  0.6 0.1 pad_add_fusion.where_ref
  0.7 2.5 %copy-done = f32[80,4,32,128]{3,2,1,0:T(8,128)S(1)} copy-done((f32[80,4,32,128]{3,2,1,0:T(8,128)S(1)}, f32[80,4,32,128]{3,2,1,0:T(8,128)}, u32[]{:S(2)}) %copy-start) | copy-done | bytes 5242904
  3.2 1.7 %copy-done.3 = f32[1,16,96,384]{3,2,1,0:T(8,128)S(1)} copy-done((f32[1,16,96,384]{3,2,1,0:T(8,128)S(1)}, f32[1,16,96,384]{3,2,1,0:T(8,128)}, u32[]{:S(2)}) %copy-start.3) | copy-done | bytes 2359320
  4.9 2.8 %restrict.1 = (f32[4,144,128]{2,1,0:T(8,128)S(1)}, f32[4,128,256]{2,1,0:T(8,128)S(1)}, f32[4,8,256]{2,1,0:T(8,128)S(1)}, f32[384,128]{1,0:T(8,128)S(1)}, f32[384,128]{1,0:T(8,128)S(1)}) custom-call(s32[3]{0:T(128)S(1)} %pad_add_fusion.where_ref, f32[1,16,96,384]{3,2,1,0:T(8,128)S(1)} %copy-done.3, f32[1,16,96,384]{3,2,1,0:T(8,128)S(1)} %copy-done.3, ...), custom_call_target="tpu_custom_call" | custom-call | tf_op jit(solution)/shard_map/restrict/pallas_call | solution.py:301
  7.7 4.4 %collective-permute-start.3 = (f32[384,128]{1,0:T(8,128)S(1)}, f32[384,128]{1,0:T(8,128)S(1)}, u32[]{:S(2)}, u32[]{:S(2)}) collective-permute-start(f32[384,128]{1,0:T(8,128)S(1)} %get-tuple-element.16), channel_id=1, source_target_pairs={{0,32},{32,64},{64,96},{96,128},{128,160},{160,192},{192,224},{1,3... | collective-permute-start | bytes 589832 | tf_op jit(solution)/shard_map/ppermute | solution.py:453
  12.1 1.3 %collective-permute-start.4 = (f32[384,128]{1,0:T(8,128)S(1)}, f32[384,128]{1,0:T(8,128)S(1)}, u32[]{:S(2)}, u32[]{:S(2)}) collective-permute-start(f32[384,128]{1,0:T(8,128)S(1)} %get-tuple-element.17), channel_id=1, source_target_pairs={{32,0},{64,32},{96,64},{128,96},{160,128},{192,160},{224,192},{33,... | collective-permute-start | bytes 589832 | tf_op jit(solution)/shard_map/ppermute | solution.py:454
  13.4 2.2 %collective-permute-done.3.above_ref = f32[384,128]{1,0:T(8,128)S(1)} collective-permute-done((f32[384,128]{1,0:T(8,128)S(1)}, f32[384,128]{1,0:T(8,128)S(1)}, u32[]{:S(2)}, u32[]{:S(2)}) %collective-permute-start.3) | collective-permute-done | bytes 196640 | tf_op jit(solution)/shard_map/ppermute | solution.py:453
  15.6 4.2 %collective-permute-done.4.below_ref = f32[384,128]{1,0:T(8,128)S(1)} collective-permute-done((f32[384,128]{1,0:T(8,128)S(1)}, f32[384,128]{1,0:T(8,128)S(1)}, u32[]{:S(2)}, u32[]{:S(2)}) %collective-permute-start.4) | collective-permute-done | bytes 196640 | tf_op jit(solution)/shard_map/ppermute | solution.py:454
  19.8 4.0 %sides.1 = (f32[176,128]{1,0:T(8,128)S(1)}, f32[176,128]{1,0:T(8,128)S(1)}, f32[4,128,256]{2,1,0:T(8,128)S(1)}, f32[4,8,256]{2,1,0:T(8,128)S(1)}) custom-call(f32[80,4,32,128]{3,2,1,0:T(8,128)S(1)} %copy-done.1, f32[384,128]{1,0:T(8,128)S(1)} %collective-permute-done.3.above_ref, f32[384,128]{1,0:T(8,128)S(1)} %collective-permute-done.4.below_ref, ...), custom_call_target="tpu_custom_call" | custom-call | tf_op jit(solution)/shard_map/sides/pallas_call | solution.py:338
  23.9 1.4 %collective-permute-start.5 = (f32[176,128]{1,0:T(8,128)S(1)}, f32[176,128]{1,0:T(8,128)S(1)}, u32[]{:S(2)}, u32[]{:S(2)}) collective-permute-start(f32[176,128]{1,0:T(8,128)S(1)} %get-tuple-element.20), channel_id=1, source_target_pairs={{0,4},{4,8},{8,12},{12,16},{16,20},{20,24},{24,28},{28,0},{1,5},{5... | collective-permute-start | bytes 270344 | tf_op jit(solution)/shard_map/ppermute | solution.py:458
  25.2 2.3 %collective-permute-start.6 = (f32[176,128]{1,0:T(8,128)S(1)}, f32[176,128]{1,0:T(8,128)S(1)}, u32[]{:S(2)}, u32[]{:S(2)}) collective-permute-start(f32[176,128]{1,0:T(8,128)S(1)} %get-tuple-element.21), channel_id=1, source_target_pairs={{4,0},{8,4},{12,8},{16,12},{20,16},{24,20},{28,24},{0,28},{5,1},{9... | collective-permute-start | bytes 270344 | tf_op jit(solution)/shard_map/ppermute | solution.py:457
  27.5 5.1 %collective-permute-start.2 = (f32[144,128]{1,0:T(8,128)S(1)}, f32[144,128]{1,0:T(8,128)S(1)}, u32[]{:S(2)}, u32[]{:S(2)}) collective-permute-start(f32[144,128]{1,0:T(8,128)S(1)} %get-tuple-element.28), channel_id=1, source_target_pairs={{0,3},{1,2},{2,1},{3,0},{4,7},{5,6},{6,5},{7,4},{8,11},{9,10},{10,... | collective-permute-start | bytes 221192 | tf_op jit(solution)/shard_map/ppermute | solution.py:437
  32.6 0.1 collective-permute-start.1
  32.7 0.4 collective-permute-start
  33.1 3.2 %collective-permute-done.2.c3_ref = f32[144,128]{1,0:T(8,128)S(1)} collective-permute-done((f32[144,128]{1,0:T(8,128)S(1)}, f32[144,128]{1,0:T(8,128)S(1)}, u32[]{:S(2)}, u32[]{:S(2)}) %collective-permute-start.2) | collective-permute-done | bytes 73760 | tf_op jit(solution)/shard_map/ppermute | solution.py:437
  36.3 1.3 %collective-permute-done.1.c2_ref = f32[144,128]{1,0:T(8,128)S(1)} collective-permute-done((f32[144,128]{1,0:T(8,128)S(1)}, f32[144,128]{1,0:T(8,128)S(1)}, u32[]{:S(2)}, u32[]{:S(2)}) %collective-permute-start.1) | collective-permute-done | bytes 73760 | tf_op jit(solution)/shard_map/ppermute | solution.py:437
  37.6 0.0 copy-start.5
  37.6 3.0 %project.1 = f32[4,80]{1,0:T(4,128)S(1)} custom-call(s32[3]{0:T(128)S(1)} %pad_add_fusion.where_ref, f32[80,4,32,128]{3,2,1,0:T(8,128)S(1)} %copy-done.1, f32[144,128]{1,0:T(8,128)S(1)} %get-tuple-element.31.c0_ref, f32[144,128]{1,0:T(8,128)S(1)} %collective-permute-done.c1_ref, f32[144,128]{1,0:T(8,128)S(1)} %collective-permute-done.1.c2_ref, ...), custom_call_target="tpu_custom_call" | custom-call | tf_op jit(solution)/shard_map/project/pallas_call | solution.py:366
  40.6 11.9 %all_to_all.10 = f32[32,4,80]{2,1,0:T(4,128)S(1)} all-to-all(f32[32,4,80]{2,1,0:T(4,128)S(1)} %broadcast_in_dim.4), channel_id=1, replica_groups=mesh['lat'=8,'lon'=8,'mem'=4] {'lon','mem'}, dimensions={0} | all-to-all | bytes 81920 | tf_op jit(solution)/shard_map/all_to_all | solution.py:444
  52.6 0.6 broadcast_in_dim.5
  53.2 7.9 %all-to-all-start.1 = ((f32[8,4,80]{2,1,0:T(4,128)}), f32[8,4,80]{2,1,0:T(4,128)S(1)}, u32[]{:S(2)}, u32[]{:S(2)}) async-start(f32[8,4,80]{2,1,0:T(4,128)} %broadcast_in_dim.5), calls=%async_computation.1 | async-start | bytes 32768 | tf_op jit(solution)/shard_map/all_to_all | solution.py:444
  61.0 6.6 %all-to-all-done.1 = f32[8,4,80]{2,1,0:T(4,128)S(1)} async-done(((f32[8,4,80]{2,1,0:T(4,128)}), f32[8,4,80]{2,1,0:T(4,128)S(1)}, u32[]{:S(2)}, u32[]{:S(2)}) %all-to-all-start.1) | async-done | bytes 10272 | tf_op jit(solution)/shard_map/all_to_all | solution.py:444
  67.7 0.0 copy-start.4
  67.7 0.0 copy-start.2
  67.7 2.5 %copy-done.2 = f32[80,4,32,128]{3,2,1,0:T(8,128)S(1)} copy-done((f32[80,4,32,128]{3,2,1,0:T(8,128)S(1)}, f32[80,4,32,128]{3,2,1,0:T(8,128)}, u32[]{:S(2)}) %copy-start.2) | copy-done | bytes 5242904
  70.2 4.0 %update.1 = (f32[144,128]{1,0:T(8,128)S(1)}, f32[144,128]{1,0:T(8,128)S(1)}, f32[144,128]{1,0:T(8,128)S(1)}, f32[144,128]{1,0:T(8,128)S(1)}) custom-call(s32[3]{0:T(128)S(1)} %pad_add_fusion.where_ref, f32[4,80]{1,0:T(4,128)S(1)} %broadcast_multiply_fusion.c_ref, f32[8,80]{1,0:T(8,128)S(1)} %pad_maximum_fusion.cv_ref, f32[80,4,32,128]{3,2,1,0:T(8,128)S(1)} %copy-done.2, ...), custom_call_target="tpu_custom_call" | custom-call | tf_op jit(solution)/shard_map/update/pallas_call | solution.py:385
  74.3 1.9 %collective-permute-start.7 = (f32[144,128]{1,0:T(8,128)S(1)}, f32[144,128]{1,0:T(8,128)S(1)}, u32[]{:S(2)}, u32[]{:S(2)}) collective-permute-start(f32[144,128]{1,0:T(8,128)S(1)} %get-tuple-element.23), channel_id=1, source_target_pairs={{0,1},{1,0},{2,3},{3,2},{4,5},{5,4},{6,7},{7,6},{8,9},{9,8},{10,11... | collective-permute-start | bytes 221192 | tf_op jit(solution)/shard_map/ppermute | solution.py:437
  76.2 1.0 %collective-permute-start.8 = (f32[144,128]{1,0:T(8,128)S(1)}, f32[144,128]{1,0:T(8,128)S(1)}, u32[]{:S(2)}, u32[]{:S(2)}) collective-permute-start(f32[144,128]{1,0:T(8,128)S(1)} %get-tuple-element.24), channel_id=1, source_target_pairs={{0,2},{1,3},{2,0},{3,1},{4,6},{5,7},{6,4},{7,5},{8,10},{9,11},{10,... | collective-permute-start | bytes 221192 | tf_op jit(solution)/shard_map/ppermute | solution.py:437
  77.2 2.2 %collective-permute-start.9 = (f32[144,128]{1,0:T(8,128)S(1)}, f32[144,128]{1,0:T(8,128)S(1)}, u32[]{:S(2)}, u32[]{:S(2)}) collective-permute-start(f32[144,128]{1,0:T(8,128)S(1)} %get-tuple-element.25), channel_id=1, source_target_pairs={{0,3},{1,2},{2,1},{3,0},{4,7},{5,6},{6,5},{7,4},{8,11},{9,10},{10,... | collective-permute-start | bytes 221192 | tf_op jit(solution)/shard_map/ppermute | solution.py:437
  79.4 2.1 %collective-permute-done.8.r2_ref = f32[144,128]{1,0:T(8,128)S(1)} collective-permute-done((f32[144,128]{1,0:T(8,128)S(1)}, f32[144,128]{1,0:T(8,128)S(1)}, u32[]{:S(2)}, u32[]{:S(2)}) %collective-permute-start.8) | collective-permute-done | bytes 73760 | tf_op jit(solution)/shard_map/ppermute | solution.py:437
  81.5 1.8 %collective-permute-done.9.r3_ref = f32[144,128]{1,0:T(8,128)S(1)} collective-permute-done((f32[144,128]{1,0:T(8,128)S(1)}, f32[144,128]{1,0:T(8,128)S(1)}, u32[]{:S(2)}, u32[]{:S(2)}) %collective-permute-start.9) | collective-permute-done | bytes 73760 | tf_op jit(solution)/shard_map/ppermute | solution.py:437
  83.3 3.6 %prolong.1 = f32[1,16,96,384]{3,2,1,0:T(8,128)} custom-call(s32[3]{0:T(128)S(1)} %pad_add_fusion.where_ref, f32[144,128]{1,0:T(8,128)S(1)} %get-tuple-element.22.r0_ref, f32[144,128]{1,0:T(8,128)S(1)} %collective-permute-done.7.r1_ref, f32[144,128]{1,0:T(8,128)S(1)} %collective-permute-done.8.r2_ref, f32[144,128]{1,0:T(8,128)S(1)} %collective-permute-done.9.r3_ref, ...), custom_call_target="tpu_custom_call" | custom-call | tf_op jit(solution)/shard_map/prolong/pallas_call | solution.py:407
  (17 shorter events, 0.1 us)
Async XLA Ops:
  0.7 2.5 %copy-start = (f32[80,4,32,128]{3,2,1,0:T(8,128)S(1)}, f32[80,4,32,128]{3,2,1,0:T(8,128)}, u32[]{:S(2)}) copy-start(f32[80,4,32,128]{3,2,1,0:T(8,128)} %v_ref.5) | copy-start | bytes 15728644
  3.2 1.7 %copy-start.3 = (f32[1,16,96,384]{3,2,1,0:T(8,128)S(1)}, f32[1,16,96,384]{3,2,1,0:T(8,128)}, u32[]{:S(2)}) copy-start(f32[1,16,96,384]{3,2,1,0:T(8,128)} %g2_ref.1) | copy-start | bytes 7077892
  4.9 14.9 %copy-start.1 = (f32[80,4,32,128]{3,2,1,0:T(8,128)S(1)}, f32[80,4,32,128]{3,2,1,0:T(8,128)}, u32[]{:S(2)}) copy-start(f32[80,4,32,128]{3,2,1,0:T(8,128)} %v_ref.5) | copy-start | bytes 15728644
  7.7 7.9 %collective-permute-start.3 = (f32[384,128]{1,0:T(8,128)S(1)}, f32[384,128]{1,0:T(8,128)S(1)}, u32[]{:S(2)}, u32[]{:S(2)}) collective-permute-start(f32[384,128]{1,0:T(8,128)S(1)} %get-tuple-element.16), channel_id=1, source_target_pairs={{0,32},{32,64},{64,96},{96,128},{128,160},{160,192},{192,224},{1,3... | collective-permute-start | bytes 589832 | tf_op jit(solution)/shard_map/ppermute | solution.py:453
  12.1 7.7 %collective-permute-start.4 = (f32[384,128]{1,0:T(8,128)S(1)}, f32[384,128]{1,0:T(8,128)S(1)}, u32[]{:S(2)}, u32[]{:S(2)}) collective-permute-start(f32[384,128]{1,0:T(8,128)S(1)} %get-tuple-element.17), channel_id=1, source_target_pairs={{32,0},{64,32},{96,64},{128,96},{160,128},{192,160},{224,192},{33,... | collective-permute-start | bytes 589832 | tf_op jit(solution)/shard_map/ppermute | solution.py:454
  23.9 13.8 %collective-permute-start.5 = (f32[176,128]{1,0:T(8,128)S(1)}, f32[176,128]{1,0:T(8,128)S(1)}, u32[]{:S(2)}, u32[]{:S(2)}) collective-permute-start(f32[176,128]{1,0:T(8,128)S(1)} %get-tuple-element.20), channel_id=1, source_target_pairs={{0,4},{4,8},{8,12},{12,16},{16,20},{20,24},{24,28},{28,0},{1,5},{5... | collective-permute-start | bytes 270344 | tf_op jit(solution)/shard_map/ppermute | solution.py:458
  25.2 12.4 %collective-permute-start.6 = (f32[176,128]{1,0:T(8,128)S(1)}, f32[176,128]{1,0:T(8,128)S(1)}, u32[]{:S(2)}, u32[]{:S(2)}) collective-permute-start(f32[176,128]{1,0:T(8,128)S(1)} %get-tuple-element.21), channel_id=1, source_target_pairs={{4,0},{8,4},{12,8},{16,12},{20,16},{24,20},{28,24},{0,28},{5,1},{9... | collective-permute-start | bytes 270344 | tf_op jit(solution)/shard_map/ppermute | solution.py:457
  27.5 8.8 %collective-permute-start.2 = (f32[144,128]{1,0:T(8,128)S(1)}, f32[144,128]{1,0:T(8,128)S(1)}, u32[]{:S(2)}, u32[]{:S(2)}) collective-permute-start(f32[144,128]{1,0:T(8,128)S(1)} %get-tuple-element.28), channel_id=1, source_target_pairs={{0,3},{1,2},{2,1},{3,0},{4,7},{5,6},{6,5},{7,4},{8,11},{9,10},{10,... | collective-permute-start | bytes 221192 | tf_op jit(solution)/shard_map/ppermute | solution.py:437
  32.6 5.0 %collective-permute-start.1 = (f32[144,128]{1,0:T(8,128)S(1)}, f32[144,128]{1,0:T(8,128)S(1)}, u32[]{:S(2)}, u32[]{:S(2)}) collective-permute-start(f32[144,128]{1,0:T(8,128)S(1)} %get-tuple-element.29), channel_id=1, source_target_pairs={{0,2},{1,3},{2,0},{3,1},{4,6},{5,7},{6,4},{7,5},{8,10},{9,11},{10,... | collective-permute-start | bytes 221192 | tf_op jit(solution)/shard_map/ppermute | solution.py:437
  32.7 4.9 %collective-permute-start = (f32[144,128]{1,0:T(8,128)S(1)}, f32[144,128]{1,0:T(8,128)S(1)}, u32[]{:S(2)}, u32[]{:S(2)}) collective-permute-start(f32[144,128]{1,0:T(8,128)S(1)} %get-tuple-element.30), channel_id=1, source_target_pairs={{0,1},{1,0},{2,3},{3,2},{4,5},{5,4},{6,7},{7,6},{8,9},{9,8},{10,11... | collective-permute-start | bytes 221192 | tf_op jit(solution)/shard_map/ppermute | solution.py:437
  37.6 23.4 %copy-start.5 = (f32[80]{0:T(128)S(1)}, f32[80]{0:T(128)}, u32[]{:S(2)}) copy-start(f32[80]{0:T(128)} %param.5) | copy-start | bytes 964
  53.2 14.5 %all-to-all-start.1 = ((f32[8,4,80]{2,1,0:T(4,128)}), f32[8,4,80]{2,1,0:T(4,128)S(1)}, u32[]{:S(2)}, u32[]{:S(2)}) async-start(f32[8,4,80]{2,1,0:T(4,128)} %broadcast_in_dim.5), calls=%async_computation.1 | async-start | bytes 32768 | tf_op jit(solution)/shard_map/all_to_all | solution.py:444
  67.7 6.6 %copy-start.4 = (f32[4,80]{1,0:T(4,128)}, f32[4,80]{1,0:T(4,128)S(1)}, u32[]{:S(2)}) copy-start(f32[4,80]{1,0:T(4,128)S(1)} %broadcast_multiply_fusion.c_ref) | copy-start | bytes 3844
  67.7 2.5 %copy-start.2 = (f32[80,4,32,128]{3,2,1,0:T(8,128)S(1)}, f32[80,4,32,128]{3,2,1,0:T(8,128)}, u32[]{:S(2)}) copy-start(f32[80,4,32,128]{3,2,1,0:T(8,128)} %v_ref.5) | copy-start | bytes 15728644
  74.3 5.2 %collective-permute-start.7 = (f32[144,128]{1,0:T(8,128)S(1)}, f32[144,128]{1,0:T(8,128)S(1)}, u32[]{:S(2)}, u32[]{:S(2)}) collective-permute-start(f32[144,128]{1,0:T(8,128)S(1)} %get-tuple-element.23), channel_id=1, source_target_pairs={{0,1},{1,0},{2,3},{3,2},{4,5},{5,4},{6,7},{7,6},{8,9},{9,8},{10,11... | collective-permute-start | bytes 221192 | tf_op jit(solution)/shard_map/ppermute | solution.py:437
  76.2 5.3 %collective-permute-start.8 = (f32[144,128]{1,0:T(8,128)S(1)}, f32[144,128]{1,0:T(8,128)S(1)}, u32[]{:S(2)}, u32[]{:S(2)}) collective-permute-start(f32[144,128]{1,0:T(8,128)S(1)} %get-tuple-element.24), channel_id=1, source_target_pairs={{0,2},{1,3},{2,0},{3,1},{4,6},{5,7},{6,4},{7,5},{8,10},{9,11},{10,... | collective-permute-start | bytes 221192 | tf_op jit(solution)/shard_map/ppermute | solution.py:437
  77.2 6.1 %collective-permute-start.9 = (f32[144,128]{1,0:T(8,128)S(1)}, f32[144,128]{1,0:T(8,128)S(1)}, u32[]{:S(2)}, u32[]{:S(2)}) collective-permute-start(f32[144,128]{1,0:T(8,128)S(1)} %get-tuple-element.25), channel_id=1, source_target_pairs={{0,3},{1,2},{2,1},{3,0},{4,7},{5,6},{6,5},{7,4},{8,11},{9,10},{10,... | collective-permute-start | bytes 221192 | tf_op jit(solution)/shard_map/ppermute | solution.py:437

commit v2 on v0

v2 whole, which is shorter than its diff:
```python
import functools

import jax
import jax.numpy as jnp
from jax import lax
from jax.experimental import pallas as pl
from jax.experimental.pallas import tpu as pltpu
from jax.sharding import PartitionSpec as P

F32 = jnp.float32
BF16 = jnp.bfloat16
RITZ = 80
GROUPS = 4
DEPTH = 4
ROWS = 32
COLS = 128
MAIN = DEPTH * ROWS
HALO = 16
BLOCK = MAIN + HALO
LEVELS = GROUPS * DEPTH
BAND = 2 * 3 * LEVELS
EDGE = DEPTH * RITZ
SIDE = RITZ + 4 * GROUPS
CHUNK = 8
PIECES = 4
EARLY = (0, 2)
LATE = (3, 1)
MIB = 1024 * 1024
VMEM_LIMIT = 24 * MIB


def iota(shape, dim):
    return lax.broadcasted_iota(jnp.int32, shape, dim)


def diagonal(rows):
    return iota((rows, COLS), 0) == iota((rows, COLS), 1)


def column_to_row(column, mask):
    spread = jnp.broadcast_to(column, mask.shape)
    return jnp.sum(jnp.where(mask, spread, 0.0), axis=0, keepdims=True)


def stack_rows(rows):
    position = iota((8, COLS), 0)
    result = jnp.zeros((8, COLS), F32)
    for index, row in enumerate(rows):
        result = jnp.where(position == index, jnp.broadcast_to(row, (8, COLS)), result)
    return result


def split(value):
    high = value.astype(BF16)
    return high, (value - high.astype(F32)).astype(BF16)


def dot_split(value, weights):
    rows = value.shape[0]
    both = jnp.dot(jnp.concatenate(split(value), axis=0), weights, preferred_element_type=F32)
    return both[:rows] + both[rows:]


def tent_weights(coarse, fine):
    tent = jnp.maximum(3 - jnp.abs(fine - 3 * coarse - 1), 0)
    left = jnp.logical_and(coarse == COLS, fine == 0)
    right = jnp.logical_and(coarse == COLS + 1, fine == 3 * COLS - 1)
    outer = jnp.where(jnp.logical_or(left, right), 1, 0)
    return jnp.where(coarse < COLS, tent, outer)


def edges_kernel(g_ref, f_ref, down_ref, up_ref, sem):
    copies = []
    for part in range(3):
        source = g_ref.at[:, :, pl.ds(COLS * part, COLS)]
        copy = pltpu.make_async_copy(source, f_ref.at[part], sem.at[part])
        copy.start()
        copies.append(copy)
    row = iota((1, 8, COLS), 1)
    plans = (
        (up_ref, 0, jnp.where(row < 4, jnp.where(row == 1, 3, jnp.where(row == 3, 1, 2)), 0), row == 0),
        (
            down_ref,
            3 * ROWS - 8,
            jnp.where(row > 3, jnp.where(row == 6, 3, jnp.where(row == 4, 1, 2)), 0),
            row == 7,
        ),
    )
    for part in range(3):
        copies[part].wait()
        for ref, start, weights, outer in plans:
            fine = f_ref[part, :, start : start + 8, :]
            place = 2 * LEVELS * part
            ref[place : place + LEVELS, :] = jnp.sum(fine * weights.astype(F32), axis=1)
            ref[place + LEVELS : place + 2 * LEVELS, :] = jnp.sum(jnp.where(outer, fine, 0.0), axis=1)


def restrict_kernel(f_ref, v_ref, copy_ref, e_ref, h_ref, first_ref, last_ref, w_ref, a_ref, o_ref, m_ref, sem):
    rows = RITZ * MAIN // PIECES
    copies = []
    for piece in range(PIECES):
        place = pl.ds(rows * piece, rows)
        copy = pltpu.make_async_copy(v_ref.at[place, :], copy_ref.at[place, :], sem.at[piece])
        copy.start()
        copies.append(copy)
    fine = iota((3 * COLS, 2 * COLS), 0)
    coarse = iota((3 * COLS, 2 * COLS), 1)
    w_ref[...] = tent_weights(coarse, fine).astype(F32).astype(BF16)
    position = iota((ROWS, COLS), 0)
    o_ref[...] = jnp.zeros_like(o_ref)

    def body(group, carry):
        for part in range(3):
            lanes = slice(COLS * part, COLS * (part + 1))
            for level in range(DEPTH):
                first = f_ref[part, DEPTH * group + level, pl.ds(0, ROWS, stride=3), :]
                middle = f_ref[part, DEPTH * group + level, pl.ds(1, ROWS, stride=3), :]
                third = f_ref[part, DEPTH * group + level, pl.ds(2, ROWS, stride=3), :]
                before = jnp.where(position == 0, 0.0, pltpu.roll(third, 1, 0))
                after = jnp.where(position == ROWS - 1, 0.0, pltpu.roll(first, ROWS - 1, 0))
                high, low = split(before + after + 2.0 * (first + third) + 3.0 * middle)
                start = ROWS * level
                a_ref[start : start + ROWS, lanes] = high
                a_ref[BLOCK + start : BLOCK + start + ROWS, lanes] = low
                o_ref[level : level + 1, lanes] = first[0:1]
                o_ref[DEPTH + level : DEPTH + level + 1, lanes] = third[ROWS - 1 : ROWS]
        high, low = split(o_ref[...])
        a_ref[MAIN:BLOCK, :] = high
        a_ref[BLOCK + MAIN :, :] = low
        both = jnp.dot(a_ref[...], w_ref[...], preferred_element_type=F32)
        coarse = (both[:BLOCK] + both[BLOCK:]) * (1.0 / 81.0)
        e_ref[group] = coarse[:MAIN]
        h_ref[group] = coarse[MAIN : MAIN + 8]
        return carry

    lax.fori_loop(0, GROUPS, body, 0)
    lanes = iota((MAIN, COLS), 1) // 2
    half = RITZ // 2
    for part in range(2):
        packed = jnp.zeros((MAIN, COLS), F32)
        for index in range(half):
            k = half * part + index
            if k % (RITZ // PIECES) == 0:
                copies[k // (RITZ // PIECES)].wait()
            turned = pltpu.roll(copy_ref[MAIN * k : MAIN * (k + 1), :], 2 * index + 1, 1)
            packed = jnp.where(lanes == index, turned, packed)
        m_ref[...] = jnp.transpose(packed)
        place = slice(half * part, half * (part + 1))
        last_ref[place, :] = m_ref[pl.ds(0, half, stride=2), :]
        first_ref[place, :] = m_ref[pl.ds(1, half, stride=2), :]


def sides_kernel(
    where_ref, above_ref, below_ref, e_ref, h_ref, first_ref, last_ref, w_ref,
    left_ref, right_ref, e2_ref, h2_ref, x0_ref, x1_ref, x2_ref, x3_ref, m_ref
):
    corner = diagonal(8)
    left_ref[:RITZ, :] = first_ref[...]
    right_ref[:RITZ, :] = last_ref[...]
    position = iota((ROWS, 2 * COLS), 0)
    lanes = iota((MAIN, COLS), 1)
    packed = jnp.zeros((MAIN, COLS), F32)
    corners = ([], [])
    received = []
    for index, ref in enumerate((above_ref, below_ref)):
        keep = where_ref[1 + index].astype(F32)
        parts = [keep * ref[2 * LEVELS * part : 2 * LEVELS * (part + 1), :] for part in range(3)]
        received.append(jnp.concatenate(parts, axis=1))
    received = dot_split(jnp.concatenate(received, axis=0), w_ref[...]) * (1.0 / 81.0)
    for group in range(GROUPS):
        place = slice(DEPTH * group, DEPTH * (group + 1))
        over, above, under, below = [received[LEVELS * i : LEVELS * (i + 1)][place] for i in range(4)]
        for level in range(DEPTH):
            rows = slice(ROWS * level, ROWS * (level + 1))
            tile = e_ref[group, rows, :]
            tile = tile + jnp.where(position == 0, above[level : level + 1, :], 0.0)
            tile = tile + jnp.where(position == ROWS - 1, below[level : level + 1, :], 0.0)
            e2_ref[group, rows, :] = tile
        edge = h_ref[group] + jnp.concatenate([over, under], axis=0)
        h2_ref[group] = edge
        for rows, lane, outer in ((corners[0], 0, COLS), (corners[1], COLS - 1, COLS + 1)):
            for source in (lane, outer):
                rows.append(column_to_row(edge[:, source : source + 1], corner))
        inner = pltpu.roll(e2_ref[group, :, :COLS], 4 * group + 1, 1)
        outer = pltpu.roll(e2_ref[group, :, COLS:], 4 * group + 2, 1)
        packed = jnp.where(lanes // 2 == 2 * group, inner, packed)
        packed = jnp.where(lanes // 2 == 2 * group + 1, outer, packed)
    m_ref[...] = jnp.transpose(packed)
    for ref, row, outer, extra in ((left_ref, 1, 2, corners[0]), (right_ref, 0, 3, corners[1])):
        for pair in range(2):
            rows = []
            for group in (2 * pair, 2 * pair + 1):
                rows.append(m_ref[4 * group + row : 4 * group + row + 1, :])
                rows.append(extra[2 * group])
                rows.append(m_ref[4 * group + outer : 4 * group + outer + 1, :])
                rows.append(extra[2 * group + 1])
            ref[RITZ + 8 * pair : RITZ + 8 * pair + 8, :] = stack_rows(rows)
    for slot, ref in enumerate((x0_ref, x1_ref, x2_ref, x3_ref)):
        group = where_ref[0] ^ slot
        ref[:MAIN] = e2_ref[group, :, :COLS]
        ref[MAIN:] = stack_rows([m_ref[pl.ds(4 * group + 2 + side, 1), :] for side in range(2)])


def bands_kernel(v_ref, left_ref, right_ref, down_ref, up_ref):
    lanes = iota((RITZ, COLS), 1)
    for ref, row in ((up_ref, 0), (down_ref, ROWS - 1)):
        corners = jnp.zeros((RITZ, COLS), F32)
        for level in range(DEPTH):
            source = ROWS * level + row
            ref[RITZ * level : RITZ * (level + 1), :] = v_ref[pl.ds(source, RITZ, stride=MAIN), :]
            for side, columns in enumerate((left_ref, right_ref)):
                target = DEPTH * side + level
                turned = pltpu.roll(columns[:RITZ, :], (target - source) % COLS, 1)
                corners = jnp.where(lanes == target, turned, corners)
        ref[EDGE:, :] = corners


def edge_parts(where_ref, above_ref, below_ref, left_ref, right_ref):
    keep = [where_ref[1 + index].astype(F32) for index in range(2)]
    parts = []
    for index, source in enumerate((above_ref, below_ref)):
        for level in range(DEPTH):
            parts.append(keep[index] * source[RITZ * level : RITZ * (level + 1), :])
    parts += [left_ref[:RITZ, :], keep[0] * above_ref[EDGE:, :], right_ref[:RITZ, :], keep[1] * below_ref[EDGE:, :]]
    return parts


def accumulate(v_ref, blocks, base):
    sums = [[jnp.zeros((8, COLS), F32) for _ in range(CHUNK)] for _ in blocks]
    for tile in range(MAIN // 8):
        fields = [block[8 * tile : 8 * tile + 8, :] for block in blocks]
        for k in range(CHUNK):
            vector = v_ref[pl.ds(pl.multiple_of((base + k) * MAIN + 8 * tile, 8), 8), :]
            for member, field in enumerate(fields):
                sums[member][k] = sums[member][k] + vector * field
    return [stack_rows([jnp.sum(value, axis=0, keepdims=True) for value in member]) for member in sums]


def near_kernel(v_ref, c0_ref, c2_ref, s_ref):
    def body(step, carry):
        base = pl.multiple_of(step * CHUNK, CHUNK)
        for member, total in enumerate(accumulate(v_ref, (c0_ref, c2_ref), base)):
            s_ref[member, pl.ds(base, CHUNK), :] = total
        return carry

    lax.fori_loop(0, RITZ // CHUNK, body, 0)


def far_kernel(
    where_ref, near_ref, v_ref, c0_ref, c1_ref, c2_ref, c3_ref, left_ref, right_ref, p_ref, s_ref
):
    blocks = (c0_ref, c2_ref, c3_ref, c1_ref)

    def body(step, carry):
        base = pl.multiple_of(step * CHUNK, CHUNK)
        totals = [near_ref[member, pl.ds(base, CHUNK), :] for member in range(2)]
        totals += accumulate(v_ref, (c3_ref, c1_ref), base)
        parts = [ref[pl.ds(base, CHUNK), :] for ref in (left_ref, right_ref)]
        for member, total in enumerate(totals):
            for index, part in enumerate(parts):
                total = total + part * blocks[member][MAIN + index : MAIN + index + 1, :]
            s_ref[member, pl.ds(base, CHUNK), :] = total
        return carry

    lax.fori_loop(0, RITZ // CHUNK, body, 0)
    ones = jnp.ones((8, COLS), F32)
    for index, slot in enumerate((0, 2, 3, 1)):
        reduced = exact_dot(ones, s_ref[index], ((1,), (1,)))
        p_ref[pl.ds(where_ref[0] ^ slot, 1), :] = reduced[0:1, :]


def exact_dot(left, right, dims):
    return lax.dot_general(
        left, right, (dims, ((), ())), precision=lax.Precision.HIGHEST, preferred_element_type=F32
    )


def weighted_sums(v_ref, b_ref, slots, prepare):
    half = MAIN // 2
    results = []
    for part in range(2):

        def body(index, sums, part=part):
            sums = list(sums)
            prepare(part, index)
            for offset in range(CHUNK):
                k = index * CHUNK + offset
                vector = v_ref[k, part]
                for position, member in enumerate(slots):
                    sums[position] = sums[position] + b_ref[pl.ds(RITZ * member + k, 1), :] * vector
            return tuple(sums)

        zeros = tuple(jnp.zeros((half, COLS), F32) for _ in slots)
        results.append(lax.fori_loop(0, RITZ // CHUNK, body, zeros))
    return results


def update_kernel(
    where_ref, c_ref, v_hbm_ref, above_ref, below_ref, left_ref, right_ref,
    v_ref, b_ref, edge_ref, u1_ref, u2_ref, u3_ref, sem
):
    me = where_ref[0]
    outs = (None, u1_ref, u2_ref, u3_ref)
    pieces = RITZ // CHUNK

    def copy(part, piece):
        place = pl.ds(piece * CHUNK, CHUNK)
        return pltpu.make_async_copy(v_hbm_ref.at[place, part], v_ref.at[place, part], sem.at[part, piece])

    for part in range(2):
        for piece in range(pieces):
            copy(part, piece).start()
    coefficients = c_ref[...]
    for member in range(GROUPS):
        chosen = jnp.where(iota((8, COLS), 0) == (me ^ member), 1.0, 0.0)
        b_ref[RITZ * member : RITZ * (member + 1), :] = exact_dot(coefficients, chosen, ((0,), (0,)))
    swap = jnp.where(iota((8, 8), 1) == (me ^ iota((8, 8), 0)), 1.0, 0.0)
    ordered = exact_dot(swap, coefficients, ((1,), (0,)))
    parts = edge_parts(where_ref, above_ref, below_ref, left_ref, right_ref)
    edge = exact_dot(ordered, jnp.concatenate(parts, axis=1), ((1,), (0,)))
    for member in range(GROUPS):
        ref, start = (outs[member], MAIN) if member else (edge_ref, 0)
        for index in range(len(parts)):
            row = edge[member : member + 1, COLS * index : COLS * (index + 1)]
            ref[start + index : start + index + 1, :] = row
        ref[start + 12 : start + HALO, :] = jnp.zeros((4, COLS), F32)

    def prepare(part, index):
        copy(part, index).wait()

    half = MAIN // 2
    for part, sums in enumerate(weighted_sums(v_ref, b_ref, (1, 2, 3), prepare)):
        for member, value in zip((1, 2, 3), sums):
            outs[member][half * part : half * (part + 1), :] = value


def own_kernel(v_ref, b_ref, edge_ref, u0_ref):
    half = MAIN // 2
    for part, sums in enumerate(weighted_sums(v_ref, b_ref, (0,), lambda part, index: None)):
        u0_ref[half * part : half * (part + 1), :] = sums[0]
    u0_ref[MAIN:, :] = edge_ref[...]


def write_group(o_ref, m_ref, group, index, sem):
    copies = []
    for part in range(3):
        target = o_ref.at[pl.ds(DEPTH * group, DEPTH), :, pl.ds(COLS * part, COLS)]
        copy = pltpu.make_async_copy(m_ref.at[index, part], target, sem.at[index, part])
        copy.start()
        copies.append(copy)
    return copies


def prolong_kernel(slots, where_ref, ra_ref, rb_ref, e2_ref, h2_ref, left_ref, right_ref, *refs):
    early_ref = None
    copies = []
    if len(refs) == 4:
        m_ref, a_ref, f_ref, z_ref = refs
    else:
        early_ref, o_ref, a_ref, f_ref, z_ref, m_ref, early_sem, sem = refs
        for index, slot in enumerate(EARLY):
            copies += write_group(o_ref, early_ref, where_ref[0] ^ slot, index, early_sem)
    coarse = iota((2 * COLS, 3 * COLS), 0)
    fine = iota((2 * COLS, 3 * COLS), 1)
    coarse = jnp.where(coarse == COLS + 2, 0, jnp.where(coarse == COLS + 3, COLS - 1, coarse))
    z_ref[...] = tent_weights(coarse, fine).astype(F32).astype(BF16)
    row = iota((8, COLS), 0)
    keep = jnp.where(row < DEPTH, where_ref[1], where_ref[2]).astype(F32)
    outer_lanes = iota((MAIN, COLS), 1) < 4
    position = iota((ROWS, 3 * COLS), 0)
    for index, (slot, r_ref) in enumerate(zip(slots, (ra_ref, rb_ref))):
        group = where_ref[0] ^ slot
        start = RITZ + 4 * group
        outer = [r_ref[MAIN + 8 + kind : MAIN + 9 + kind, :] for kind in range(4)]
        first_half = iota((1, COLS), 1) < DEPTH
        beyond = (
            (outer[0], outer[2]),
            (
                jnp.where(first_half, outer[1], pltpu.roll(outer[3], DEPTH, 1)),
                jnp.where(first_half, pltpu.roll(outer[1], COLS - DEPTH, 1), outer[3]),
            ),
        )
        rows = []
        for kind in range(2):
            for ref, value in zip((left_ref, right_ref), beyond[kind]):
                rows.append(ref[pl.ds(start + kind, 1), :] + value)
            for ref in (left_ref, right_ref):
                rows.append(ref[pl.ds(start + 2 + kind, 1), :])
        stacked = jnp.concatenate([stack_rows(rows), jnp.zeros((COLS - 8, COLS), F32)], axis=0)
        turned = jnp.transpose(stacked)
        corners = pltpu.roll(turned[:8], COLS - 4, 1)
        a_ref[:MAIN, :COLS] = e2_ref[group, :, :COLS] + r_ref[:MAIN, :]
        a_ref[:MAIN, COLS:] = e2_ref[group, :, COLS:] + jnp.where(outer_lanes, turned, 0.0)
        a_ref[MAIN:, :COLS] = (h2_ref[group, :, :COLS] + r_ref[MAIN : MAIN + 8, :]) * keep
        a_ref[MAIN:, COLS:] = (h2_ref[group, :, COLS:] + jnp.where(outer_lanes[:8], corners, 0.0)) * keep
        f_ref[...] = dot_split(a_ref[...], z_ref[...])
        for level in range(DEPTH):
            center = f_ref[ROWS * level : ROWS * (level + 1), :]
            above = f_ref[MAIN + level : MAIN + level + 1, :]
            below = f_ref[MAIN + DEPTH + level : MAIN + DEPTH + level + 1, :]
            before = jnp.where(position == 0, above, pltpu.roll(center, 1, 0))
            after = jnp.where(position == ROWS - 1, below, pltpu.roll(center, ROWS - 1, 0))
            fine = ((2.0 * center + before) * (1.0 / 9.0), center * (1.0 / 3.0), (2.0 * center + after) * (1.0 / 9.0))
            for part in range(3):
                lanes = slice(COLS * part, COLS * (part + 1))
                for offset, value in enumerate(fine):
                    m_ref[index, part, level, pl.ds(offset, ROWS, stride=3), :] = value[:, lanes]
        if early_ref is not None:
            copies += write_group(o_ref, m_ref, group, index, sem)
    for copy in copies:
        copy.wait()


def struct(*shape):
    return jax.ShapeDtypeStruct(shape, F32)


SMEM = pl.BlockSpec(memory_space=pltpu.SMEM)
VMEM = pl.BlockSpec(memory_space=pltpu.VMEM)
HBM = pl.BlockSpec(memory_space=pltpu.HBM)
FIELD = (GROUPS, MAIN, 2 * COLS)
RIM = (GROUPS, 8, 2 * COLS)


def call(kernel, name, ins, outs, scratch, out_specs=None, limit=VMEM_LIMIT, aliases=None):
    return pl.pallas_call(
        kernel,
        in_specs=ins,
        out_specs=out_specs or [VMEM] * len(outs),
        out_shape=outs,
        scratch_shapes=scratch,
        input_output_aliases=aliases or {},
        compiler_params=pltpu.CompilerParams(vmem_limit_bytes=limit),
        name=name,
    )


def edges(gradients):
    scratch = [pltpu.SemaphoreType.DMA((3,))]
    outs = [pltpu.VMEM((3, LEVELS, 3 * ROWS, COLS), F32)] + [struct(BAND, COLS)] * 2
    gradients = pltpu.with_memory_space_constraint(gradients, pltpu.HBM)
    return call(edges_kernel, "edges", [HBM], outs, scratch, limit=VMEM_LIMIT)(gradients)


def restrict(fine, ritz_vectors):
    scratch = [
        pltpu.VMEM((2 * BLOCK, 3 * COLS), BF16),
        pltpu.VMEM((HALO, 3 * COLS), F32),
        pltpu.VMEM((COLS, COLS), F32),
        pltpu.SemaphoreType.DMA((PIECES,)),
    ]
    outs = [pltpu.VMEM((RITZ * MAIN, COLS), F32), struct(*FIELD), struct(*RIM)] + [struct(RITZ, COLS)] * 2
    outs += [jax.ShapeDtypeStruct((3 * COLS, 2 * COLS), BF16)]
    flat = ritz_vectors.reshape(RITZ * MAIN, COLS)
    flat = pltpu.with_memory_space_constraint(flat, pltpu.HBM)
    return call(restrict_kernel, "restrict", [VMEM, HBM], outs, scratch, limit=VMEM_LIMIT)(fine, flat)


def sides(*args):
    outs = [struct(SIDE, COLS)] * 2 + [struct(*FIELD), struct(*RIM)] + [struct(MAIN + 8, COLS)] * 4
    return call(sides_kernel, "sides", [SMEM] + [VMEM] * 7, outs, [pltpu.VMEM((COLS, COLS), F32)])(*args)


def bands(*args):
    return call(bands_kernel, "bands", [VMEM] * 3, [struct(EDGE + RITZ, COLS)] * 2, [])(*args)


def near(ritz_vectors, blocks):
    return call(near_kernel, "near", [VMEM] * 3, [struct(2, RITZ, COLS)], [])(ritz_vectors, *blocks)[0]


def far(place, sums, ritz_vectors, blocks, messages):
    outs = [struct(GROUPS, RITZ)]
    scratch = [pltpu.VMEM((GROUPS, RITZ, COLS), F32)]
    return call(far_kernel, "far", [SMEM] + [VMEM] * 8, outs, scratch)(
        place, sums, ritz_vectors, *blocks, *messages
    )[0]


def update(place, coefficients, ritz_vectors, messages):
    outs = [pltpu.VMEM((RITZ, 2, MAIN // 2, COLS), F32), struct(GROUPS * RITZ, COLS), struct(HALO, COLS)]
    outs += [struct(BLOCK, COLS)] * 3
    scratch = [pltpu.SemaphoreType.DMA((2, RITZ // CHUNK))]
    doubled = jnp.concatenate([coefficients, coefficients], axis=0)
    return call(update_kernel, "update", [SMEM, VMEM, HBM] + [VMEM] * 4, outs, scratch, limit=VMEM_LIMIT)(
        place, doubled, pltpu.with_memory_space_constraint(ritz_vectors.reshape(RITZ, 2, MAIN // 2, COLS), pltpu.HBM), *messages
    )


def own(ritz_vectors, weights, edge):
    return call(own_kernel, "own", [VMEM] * 3, [struct(BLOCK, COLS)], [])(ritz_vectors, weights, edge)[0]


def prolong(place, slots, returned, main, edge, left, right, early=None):
    scratch = [
        pltpu.VMEM((MAIN + 8, 2 * COLS), F32),
        pltpu.VMEM((MAIN + 8, 3 * COLS), F32),
        pltpu.VMEM((2 * COLS, 3 * COLS), BF16),
    ]
    stage = (2, 3, DEPTH, 3 * ROWS, COLS)
    args = (place, *returned, main, edge, left, right)
    specs = [SMEM] + [VMEM] * 6
    kernel = functools.partial(prolong_kernel, slots)
    if early is None:
        return call(kernel, "prolong_early", specs, [pltpu.VMEM(stage, F32)], scratch)(*args)[0]
    scratch += [pltpu.VMEM(stage, F32), pltpu.SemaphoreType.DMA((2, 3)), pltpu.SemaphoreType.DMA((2, 3))]
    outs = [struct(GROUPS * DEPTH, 3 * ROWS, 3 * COLS)]
    return call(kernel, "prolong_late", specs + [VMEM], outs, scratch, [HBM])(*args, early)[0]


def exchange_members(blocks):
    size = lax.axis_size("mem")
    order = (2, 3, 1)
    sent = {shift: lax.ppermute(blocks[shift], "mem", [(i, i ^ shift) for i in range(size)]) for shift in order}
    return [sent[shift] for shift in range(1, size)]


def exchange_sum(value, axes):
    size = lax.axis_size(axes)
    copies = jnp.broadcast_to(value[None], (size,) + value.shape)
    return jnp.sum(lax.all_to_all(copies, axes, 0, 0, tiled=True), axis=0)


def per_device(gradients, ritz_vectors, ritz_values):
    lats, lons = lax.axis_size("lat"), lax.axis_size("lon")
    lat, mem = lax.axis_index("lat"), lax.axis_index("mem")
    place = jnp.stack([mem, jnp.where(lat > 0, 1, 0), jnp.where(lat < lats - 1, 1, 0)]).astype(jnp.int32)

    gradients = gradients.reshape(gradients.shape[1:])
    fine, down, up = edges(gradients)
    over = [(i, (i + 1) % lats) for i in range(lats)]
    under = [((i + 1) % lats, i) for i in range(lats)]
    above = lax.ppermute(down, "lat", over)
    below = lax.ppermute(up, "lat", under)
    held, main, edge, first, last, weights = restrict(fine, ritz_vectors)
    to_left, to_right, main, edge, *blocks = sides(place, above, below, main, edge, first, last, weights)
    right = lax.ppermute(to_left, "lon", [((i + 1) % lons, i) for i in range(lons)])
    left = lax.ppermute(to_right, "lon", [(i, (i + 1) % lons) for i in range(lons)])
    spread = [blocks[0]] + exchange_members(blocks)
    near_sums = near(held, (spread[0], spread[2]))
    left, right, near_sums, *spread = lax.optimization_barrier((left, right, near_sums, *spread))
    down, up = bands(held, left, right)
    above = lax.ppermute(down, "lat", over)
    below = lax.ppermute(up, "lat", under)
    *spread, _, _ = lax.optimization_barrier((*spread, down, up))
    partial = far(place, near_sums, held, spread, (left, right))
    partial = exchange_sum(partial, ("lon", "mem"))
    partial, above, below = lax.optimization_barrier((partial, above, below))
    projections = exchange_sum(partial, "lat")
    cells = GROUPS * DEPTH * ROWS * lats * COLS * lons
    coefficients = (1.0 / ritz_values - 1.0)[None, :] * (projections * (1.0 / cells))

    messages = (above, below, left, right)
    held, weights, own_edge, *sent = update(place, coefficients, ritz_vectors, messages)
    returned = exchange_members([None] + sent)
    mine = own(held, weights, own_edge)
    returned = [mine] + returned
    early = prolong(place, EARLY, [returned[slot] for slot in EARLY], main, edge, left, right)
    output = prolong(place, LATE, [returned[slot] for slot in LATE], main, edge, left, right, early)
    preconditioned = output[None]
    return preconditioned, coefficients


def solution(mesh):
    placed = (P("mem", None, "lat", "lon"), P(None, "mem", "lat", "lon"), P())
    return jax.shard_map(
        per_device,
        mesh=mesh,
        in_specs=placed,
        out_specs=(P("mem", None, "lat", "lon"), P()),
        check_vma=False,
    )
```

time: 222 us -> 71.8 us (0.32)
  blocking collectives: 81.9 us -> 15.5 us
  local copies, waits for them, and re-layouts: 56.3 us -> 0.64 us
  waiting for transfers between devices: 29.7 us -> 10.4 us
  matrix products: 16.7 us -> 0 us
  Pallas kernels: 0 us -> 16.5 us
  other arithmetic: 12.2 us -> 0.16 us
  starting transfers between devices: 24.4 us -> 27.6 us
    psum x1 -> x0, blocking collectives: 72.3 us -> none  [finish_coefficients(): projections = lax.psum(partial_sums, ('lat', 'lon', 'mem')) * (1.0 / cells)]
    slice x15 -> x0, local copies, waits for them, and re-layouts: 48.2 us -> none  [the longest x4 24.8 us: restrict_padded(): result = result + TENT[offset] * along[..., offset:offset + 3 * cols - 2:3]]
    ppermute x8 -> x12, waiting for transfers between devices: 23.1 us -> 3.81 us  [the longest x6 3.22 us: exchange_members(): lax.ppermute(blocks[shift], 'mem', [(i, i ^ shift) for i in range(size)])]
    dot_general x2 -> x0, matrix products: 16.7 us -> none  [the longest x1 9 us: levels_products(): jnp.einsum('klyx,mlyx->mk', ritz_vectors, coarse, precision=lax.Precision...]
    pallas_call x0 -> x10, Pallas kernels: none -> 16.5 us  [the longest x1 3.6 us: update(): call(update_kernel, 'update', [SMEM, VMEM, HBM] + [VMEM] * 4, outs, scrat...]
    all_to_all x1, blocking collectives: 9.63 us -> 15.5 us  [exchange_sum(): return jnp.sum(lax.all_to_all(copies, axes, 0, 0, tiled=True), axis=0)]
    ppermute x8 -> x12, starting transfers between devices: 16.7 us -> 22.2 us  [the longest x6 9.29 us: exchange_members(): lax.ppermute(blocks[shift], 'mem', [(i, i ^ shift) for i in range(size)])]
    select_n x2 -> x0, other arithmetic: 4.03 us -> none  [clear_ends(): return jnp.where(dropped, jnp.zeros_like(padded), padded)]
  transfers between devices with their start and end apart: 9 -> 13, of which waited for: 8 -> 4; matrix products, arithmetic and copies ran while one was open for 1% -> 0% of each run, Pallas kernels for 0% -> 10%
where the time goes in v2:
time: 71.8 us; the launch traced here: 71.6 us
  starting transfers between devices  27.6 us (38%)
  Pallas kernels  16.5 us (23%)
  blocking collectives  15.5 us (22%)
  waiting for transfers between devices  10.4 us (14%)
  between operations  0.78 us (1%)
    all_to_all x1, blocking collectives, exchange_sum(): return jnp.sum(lax.all_to_all(copies, axes, 0, 0, tiled=True), axis=0)  15.5 us
    ppermute x6, starting transfers between devices, exchange_members(): lax.ppermute(blocks[shift], 'mem', [(i, i ^ shift) for i in range(size)])  9.29 us
    ppermute x2, starting transfers between devices, per_device(): below = lax.ppermute(up, 'lat', under)  6.68 us
    all_to_all x1, waiting for transfers between devices, exchange_sum(): return jnp.sum(lax.all_to_all(copies, axes, 0, 0, tiled=True), axis=0)  6.61 us
    all_to_all x1, starting transfers between devices, exchange_sum(): return jnp.sum(lax.all_to_all(copies, axes, 0, 0, tiled=True), axis=0)  5.48 us
    pallas_call x1, Pallas kernels, update(): call(update_kernel, 'update', [SMEM, VMEM, HBM] + [VMEM] * 4, outs, scrat...  3.6 us
    ppermute x6, waiting for transfers between devices, exchange_members(): lax.ppermute(blocks[shift], 'mem', [(i, i ^ shift) for i in range(size)])  3.22 us
    pallas_call x1, Pallas kernels, restrict(): call(restrict_kernel, 'restrict', [VMEM, HBM], outs, scratch, limit=VMEM_...  3.18 us
  transfers between devices with their start and end apart: 13, of which 4 were waited for; matrix products, arithmetic and copies ran while one was open for 0% of the time, Pallas kernels for 10%

profile of v2, /device:TPU:1, one launch (start us, length us, event | category | flops | bytes accessed | tf_op | source)
XLA Modules:
  0.0 71.6 jit_solution(12740116218988692169)
XLA Ops:
  0.6 1.7 %edges.1 = (f32[3,16,96,128]{3,2,1,0:T(8,128)S(1)}, f32[96,128]{1,0:T(8,128)S(1)}, f32[96,128]{1,0:T(8,128)S(1)}) custom-call(f32[16,96,384]{2,1,0:T(8,128)} %bitcast.9), custom_call_target="tpu_custom_call" | custom-call | tf_op jit(solution)/shard_map/edges/pallas_call | solution.py:442
  2.4 2.5 %collective-permute-start = (f32[96,128]{1,0:T(8,128)S(1)}, f32[96,128]{1,0:T(8,128)S(1)}, u32[]{:S(2)}, u32[]{:S(2)}) collective-permute-start(f32[96,128]{1,0:T(8,128)S(1)} %get-tuple-element.41), channel_id=1, source_target_pairs={{0,32},{32,64},{64,96},{96,128},{128,160},{160,192},{192,224},{224... | collective-permute-start | bytes 147464 | tf_op jit(solution)/shard_map/ppermute | solution.py:533
  4.9 4.0 %collective-permute-start.1 = (f32[96,128]{1,0:T(8,128)S(1)}, f32[96,128]{1,0:T(8,128)S(1)}, u32[]{:S(2)}, u32[]{:S(2)}) collective-permute-start(f32[96,128]{1,0:T(8,128)S(1)} %get-tuple-element.42), channel_id=1, source_target_pairs={{32,0},{64,32},{96,64},{128,96},{160,128},{192,160},{224,192},{0,2... | collective-permute-start | bytes 147464 | tf_op jit(solution)/shard_map/ppermute | solution.py:534
  8.9 0.1 pad_add_fusion.where_ref
  9.0 3.2 %restrict.1 = (f32[10240,128]{1,0:T(8,128)S(1)}, f32[4,128,256]{2,1,0:T(8,128)S(1)}, f32[4,8,256]{2,1,0:T(8,128)S(1)}, f32[80,128]{1,0:T(8,128)S(1)}, f32[80,128...) custom-call(f32[3,16,96,128]{3,2,1,0:T(8,128)S(1)} %get-tuple-element.43.f_ref, f32[10240,128]{1,0:T(8,128)} %bitcast.7), custom_call_target="tpu_custom_call" | custom-call | tf_op jit(solution)/shard_map/restrict/pallas_call | solution.py:456
  12.2 0.0 collective-permute-done.above_ref
  12.2 1.0 %sides.1 = (f32[96,128]{1,0:T(8,128)S(1)}, f32[96,128]{1,0:T(8,128)S(1)}, f32[4,128,256]{2,1,0:T(8,128)S(1)}, f32[4,8,256]{2,1,0:T(8,128)S(1)}, f32[136,128]{1,0...) custom-call(s32[3]{0:T(128)S(1)} %pad_add_fusion.where_ref, ...), custom_call_target="tpu_custom_call" | custom-call | tf_op jit(solution)/shard_map/sides/pallas_call | solution.py:461
  13.2 3.0 %collective-permute-start.4 = (f32[136,128]{1,0:T(8,128)S(1)}, f32[136,128]{1,0:T(8,128)S(1)}, u32[]{:S(2)}, u32[]{:S(2)}) collective-permute-start(f32[136,128]{1,0:T(8,128)S(1)} %get-tuple-element.53), channel_id=1, source_target_pairs={{0,2},{1,3},{2,0},{3,1},{4,6},{5,7},{6,4},{7,5},{8,10},{9,11},{10,... | collective-permute-start | bytes 208904 | tf_op jit(solution)/shard_map/ppermute | solution.py:514
  16.2 1.2 %collective-permute-start.5 = (f32[136,128]{1,0:T(8,128)S(1)}, f32[136,128]{1,0:T(8,128)S(1)}, u32[]{:S(2)}, u32[]{:S(2)}) collective-permute-start(f32[136,128]{1,0:T(8,128)S(1)} %get-tuple-element.54), channel_id=1, source_target_pairs={{0,1},{1,0},{2,3},{3,2},{4,5},{5,4},{6,7},{7,6},{8,9},{9,8},{10,11... | collective-permute-start | bytes 208904 | tf_op jit(solution)/shard_map/ppermute | solution.py:514
  17.5 1.2 %collective-permute-start.2 = (f32[96,128]{1,0:T(8,128)S(1)}, f32[96,128]{1,0:T(8,128)S(1)}, u32[]{:S(2)}, u32[]{:S(2)}) collective-permute-start(f32[96,128]{1,0:T(8,128)S(1)} %get-tuple-element.49), channel_id=1, source_target_pairs={{0,4},{4,8},{8,12},{12,16},{16,20},{20,24},{24,28},{28,0},{1,5},{5... | collective-permute-start | bytes 147464 | tf_op jit(solution)/shard_map/ppermute | solution.py:538
  18.7 2.3 %collective-permute-start.3 = (f32[96,128]{1,0:T(8,128)S(1)}, f32[96,128]{1,0:T(8,128)S(1)}, u32[]{:S(2)}, u32[]{:S(2)}) collective-permute-start(f32[96,128]{1,0:T(8,128)S(1)} %get-tuple-element.50), channel_id=1, source_target_pairs={{4,0},{8,4},{12,8},{16,12},{20,16},{24,20},{28,24},{0,28},{5,1},{9... | collective-permute-start | bytes 147464 | tf_op jit(solution)/shard_map/ppermute | solution.py:537
  21.0 0.9 %near.1.near_ref = f32[2,80,128]{2,1,0:T(8,128)S(1)} custom-call(f32[10240,128]{1,0:T(8,128)S(1)} %get-tuple-element.51.v_ref, f32[136,128]{1,0:T(8,128)S(1)} %get-tuple-element.65.c0_ref, f32[136,128]{1,0:T(8,128)S(1)} %collective-permute-done.4.c2_ref), custom_call_target="tpu_custom_call" | custom-call | tf_op jit(solution)/shard_map/near/pallas_call | solution.py:469
  22.0 0.6 collective-permute-done.2.left_ref
  22.5 1.0 %collective-permute-done.6.c3_ref = f32[136,128]{1,0:T(8,128)S(1)} collective-permute-done((f32[136,128]{1,0:T(8,128)S(1)}, f32[136,128]{1,0:T(8,128)S(1)}, u32[]{:S(2)}, u32[]{:S(2)}) %collective-permute-start.6) | collective-permute-done | bytes 69664 | tf_op jit(solution)/shard_map/ppermute | solution.py:514
  23.5 0.4 bands.1
  23.9 0.1 collective-permute-start.7
  24.0 0.0 copy-start.1
  24.0 2.7 %collective-permute-start.8 = (f32[400,128]{1,0:T(8,128)S(1)}, f32[400,128]{1,0:T(8,128)S(1)}, u32[]{:S(2)}, u32[]{:S(2)}) collective-permute-start(f32[400,128]{1,0:T(8,128)S(1)} %get-tuple-element.64), channel_id=1, source_target_pairs={{32,0},{64,32},{96,64},{128,96},{160,128},{192,160},{224,192},{0,2... | collective-permute-start | bytes 614408 | tf_op jit(solution)/shard_map/ppermute | solution.py:544
  26.7 1.9 %far.1 = f32[4,80]{1,0:T(4,128)S(1)} custom-call(s32[3]{0:T(128)S(1)} %pad_add_fusion.where_ref, f32[2,80,128]{2,1,0:T(8,128)S(1)} %near.1.near_ref, f32[10240,128]{1,0:T(8,128)S(1)} %get-tuple-element.51.v_ref, f32[136,128]{1,0:T(8,128)S(1)} %get-tuple-element.65.c0_ref, f32[136,128]{1,0:T(8,128)S(1)} %collective-permute-done.5.c1_ref, ...), custom_call_target="tpu_custom_call" | custom-call | tf_op jit(solution)/shard_map/far/pallas_call | solution.py:475
  28.6 15.5 %all_to_all.10 = f32[32,4,80]{2,1,0:T(4,128)S(1)} all-to-all(f32[32,4,80]{2,1,0:T(4,128)S(1)} %broadcast_in_dim.6), channel_id=1, replica_groups=mesh['lat'=8,'lon'=8,'mem'=4] {'lon','mem'}, dimensions={0} | all-to-all | bytes 81920 | tf_op jit(solution)/shard_map/all_to_all | solution.py:521
  44.2 0.0 collective-permute-done.7.above_ref
  44.2 0.6 broadcast_in_dim.7
  44.8 5.5 %all-to-all-start.1 = ((f32[8,4,80]{2,1,0:T(4,128)}), f32[8,4,80]{2,1,0:T(4,128)S(1)}, u32[]{:S(2)}, u32[]{:S(2)}) async-start(f32[8,4,80]{2,1,0:T(4,128)} %broadcast_in_dim.7), calls=%async_computation.1 | async-start | bytes 32768 | tf_op jit(solution)/shard_map/all_to_all | solution.py:521
  50.3 6.6 %all-to-all-done.1 = f32[8,4,80]{2,1,0:T(4,128)S(1)} async-done(((f32[8,4,80]{2,1,0:T(4,128)}), f32[8,4,80]{2,1,0:T(4,128)S(1)}, u32[]{:S(2)}, u32[]{:S(2)}) %all-to-all-start.1) | async-done | bytes 10272 | tf_op jit(solution)/shard_map/all_to_all | solution.py:521
  56.9 0.0 copy-start
  56.9 3.6 %update.1 = (f32[80,2,64,128]{3,2,1,0:T(8,128)S(1)}, f32[320,128]{1,0:T(8,128)S(1)}, f32[16,128]{1,0:T(8,128)S(1)}, f32[144,128]{1,0:T(8,128)S(1)}, f32[144,128]{1,0:T(8,128)S(1)}, /*index=5*/f32[144,128]{1,0:T(8,128)S(1)}) custom-call(s32[3]{0:T(128)S(1)} %pad_add_fusion.where_ref, f32[8,80]{1,0:T(8,128)S(1)} %pad_maximum_fusion.c_ref, ...), custom_call_target="tpu_custom_call" | custom-call | tf_op jit(solution)/shard_map/update/pallas_call | solution.py:485
  60.6 1.1 %collective-permute-start.11 = (f32[144,128]{1,0:T(8,128)S(1)}, f32[144,128]{1,0:T(8,128)S(1)}, u32[]{:S(2)}, u32[]{:S(2)}) collective-permute-start(f32[144,128]{1,0:T(8,128)S(1)} %get-tuple-element.79), channel_id=1, source_target_pairs={{0,2},{1,3},{2,0},{3,1},{4,6},{5,7},{6,4},{7,5},{8,10},{9,11},{10,... | collective-permute-start | bytes 221192 | tf_op jit(solution)/shard_map/ppermute | solution.py:514
  61.6 4.0 %collective-permute-start.9 = (f32[144,128]{1,0:T(8,128)S(1)}, f32[144,128]{1,0:T(8,128)S(1)}, u32[]{:S(2)}, u32[]{:S(2)}) collective-permute-start(f32[144,128]{1,0:T(8,128)S(1)} %get-tuple-element.72), channel_id=1, source_target_pairs={{0,3},{1,2},{2,1},{3,0},{4,7},{5,6},{6,5},{7,4},{8,11},{9,10},{10,... | collective-permute-start | bytes 221192 | tf_op jit(solution)/shard_map/ppermute | solution.py:514
  65.6 0.4 own.1.ra_ref
  66.1 1.1 %prolong_early.1.refs_0_ = f32[2,3,4,96,128]{4,3,2,1,0:T(8,128)S(1)} custom-call(s32[3]{0:T(128)S(1)} %pad_add_fusion.where_ref, f32[144,128]{1,0:T(8,128)S(1)} %own.1.ra_ref, f32[144,128]{1,0:T(8,128)S(1)} %collective-permute-done.11.rb_ref, f32[4,128,256]{2,1,0:T(8,128)S(1)} %get-tuple-element.74.e2_ref, f32[4,8,256]{2,1,0:T(8,128)S(1)} %get-tuple-element.75.h2_ref, ...), custom_call_target="tpu_custom_call" | custom-call | tf_op jit(solution)/shard_map/prolong_early/pallas_call | solution.py:505
  67.2 2.2 %collective-permute-done.9.ra_ref = f32[144,128]{1,0:T(8,128)S(1)} collective-permute-done((f32[144,128]{1,0:T(8,128)S(1)}, f32[144,128]{1,0:T(8,128)S(1)}, u32[]{:S(2)}, u32[]{:S(2)}) %collective-permute-start.9) | collective-permute-done | bytes 73760 | tf_op jit(solution)/shard_map/ppermute | solution.py:514
  69.4 2.2 %prolong_late.1 = f32[16,96,384]{2,1,0:T(8,128)} custom-call(s32[3]{0:T(128)S(1)} %pad_add_fusion.where_ref, f32[144,128]{1,0:T(8,128)S(1)} %collective-permute-done.9.ra_ref, f32[144,128]{1,0:T(8,128)S(1)} %collective-permute-done.10.rb_ref, f32[4,128,256]{2,1,0:T(8,128)S(1)} %get-tuple-element.74.e2_ref, f32[4,8,256]{2,1,0:T(8,128)S(1)} %get-tuple-element.75.h2_ref, ...), custom_call_target="tpu_custom_call" | custom-call | tf_op jit(solution)/shard_map/prolong_late/pallas_call | solution.py:508
  (17 shorter events, 0.1 us)
Async XLA Ops:
  2.4 9.8 %collective-permute-start = (f32[96,128]{1,0:T(8,128)S(1)}, f32[96,128]{1,0:T(8,128)S(1)}, u32[]{:S(2)}, u32[]{:S(2)}) collective-permute-start(f32[96,128]{1,0:T(8,128)S(1)} %get-tuple-element.41), channel_id=1, source_target_pairs={{0,32},{32,64},{64,96},{96,128},{128,160},{160,192},{192,224},{224... | collective-permute-start | bytes 147464 | tf_op jit(solution)/shard_map/ppermute | solution.py:533
  4.9 7.3 %collective-permute-start.1 = (f32[96,128]{1,0:T(8,128)S(1)}, f32[96,128]{1,0:T(8,128)S(1)}, u32[]{:S(2)}, u32[]{:S(2)}) collective-permute-start(f32[96,128]{1,0:T(8,128)S(1)} %get-tuple-element.42), channel_id=1, source_target_pairs={{32,0},{64,32},{96,64},{128,96},{160,128},{192,160},{224,192},{0,2... | collective-permute-start | bytes 147464 | tf_op jit(solution)/shard_map/ppermute | solution.py:534
  13.2 7.8 %collective-permute-start.4 = (f32[136,128]{1,0:T(8,128)S(1)}, f32[136,128]{1,0:T(8,128)S(1)}, u32[]{:S(2)}, u32[]{:S(2)}) collective-permute-start(f32[136,128]{1,0:T(8,128)S(1)} %get-tuple-element.53), channel_id=1, source_target_pairs={{0,2},{1,3},{2,0},{3,1},{4,6},{5,7},{6,4},{7,5},{8,10},{9,11},{10,... | collective-permute-start | bytes 208904 | tf_op jit(solution)/shard_map/ppermute | solution.py:514
  16.2 6.3 %collective-permute-start.5 = (f32[136,128]{1,0:T(8,128)S(1)}, f32[136,128]{1,0:T(8,128)S(1)}, u32[]{:S(2)}, u32[]{:S(2)}) collective-permute-start(f32[136,128]{1,0:T(8,128)S(1)} %get-tuple-element.54), channel_id=1, source_target_pairs={{0,1},{1,0},{2,3},{3,2},{4,5},{5,4},{6,7},{7,6},{8,9},{9,8},{10,11... | collective-permute-start | bytes 208904 | tf_op jit(solution)/shard_map/ppermute | solution.py:514
  17.5 6.1 %collective-permute-start.6 = (f32[136,128]{1,0:T(8,128)S(1)}, f32[136,128]{1,0:T(8,128)S(1)}, u32[]{:S(2)}, u32[]{:S(2)}) collective-permute-start(f32[136,128]{1,0:T(8,128)S(1)} %get-tuple-element.55), channel_id=1, source_target_pairs={{0,3},{1,2},{2,1},{3,0},{4,7},{5,6},{6,5},{7,4},{8,11},{9,10},{10,... | collective-permute-start | bytes 208904 | tf_op jit(solution)/shard_map/ppermute | solution.py:514
  17.5 5.1 %collective-permute-start.2 = (f32[96,128]{1,0:T(8,128)S(1)}, f32[96,128]{1,0:T(8,128)S(1)}, u32[]{:S(2)}, u32[]{:S(2)}) collective-permute-start(f32[96,128]{1,0:T(8,128)S(1)} %get-tuple-element.49), channel_id=1, source_target_pairs={{0,4},{4,8},{8,12},{12,16},{16,20},{20,24},{24,28},{28,0},{1,5},{5... | collective-permute-start | bytes 147464 | tf_op jit(solution)/shard_map/ppermute | solution.py:538
  18.7 3.8 %collective-permute-start.3 = (f32[96,128]{1,0:T(8,128)S(1)}, f32[96,128]{1,0:T(8,128)S(1)}, u32[]{:S(2)}, u32[]{:S(2)}) collective-permute-start(f32[96,128]{1,0:T(8,128)S(1)} %get-tuple-element.50), channel_id=1, source_target_pairs={{4,0},{8,4},{12,8},{16,12},{20,16},{24,20},{28,24},{0,28},{5,1},{9... | collective-permute-start | bytes 147464 | tf_op jit(solution)/shard_map/ppermute | solution.py:537
  23.9 20.2 %collective-permute-start.7 = (f32[400,128]{1,0:T(8,128)S(1)}, f32[400,128]{1,0:T(8,128)S(1)}, u32[]{:S(2)}, u32[]{:S(2)}) collective-permute-start(f32[400,128]{1,0:T(8,128)S(1)} %get-tuple-element.63), channel_id=1, source_target_pairs={{0,32},{32,64},{64,96},{96,128},{128,160},{160,192},{192,224},{224... | collective-permute-start | bytes 614408 | tf_op jit(solution)/shard_map/ppermute | solution.py:543
  24.0 26.2 %copy-start.1 = (f32[80]{0:T(128)S(1)}, f32[80]{0:T(128)}, u32[]{:S(2)}) copy-start(f32[80]{0:T(128)} %param.5) | copy-start | bytes 964
  24.0 20.1 %collective-permute-start.8 = (f32[400,128]{1,0:T(8,128)S(1)}, f32[400,128]{1,0:T(8,128)S(1)}, u32[]{:S(2)}, u32[]{:S(2)}) collective-permute-start(f32[400,128]{1,0:T(8,128)S(1)} %get-tuple-element.64), channel_id=1, source_target_pairs={{32,0},{64,32},{96,64},{128,96},{160,128},{192,160},{224,192},{0,2... | collective-permute-start | bytes 614408 | tf_op jit(solution)/shard_map/ppermute | solution.py:544
  44.8 12.1 %all-to-all-start.1 = ((f32[8,4,80]{2,1,0:T(4,128)}), f32[8,4,80]{2,1,0:T(4,128)S(1)}, u32[]{:S(2)}, u32[]{:S(2)}) async-start(f32[8,4,80]{2,1,0:T(4,128)} %broadcast_in_dim.7), calls=%async_computation.1 | async-start | bytes 32768 | tf_op jit(solution)/shard_map/all_to_all | solution.py:521
  56.9 3.6 %copy-start = (f32[4,80]{1,0:T(4,128)}, f32[4,80]{1,0:T(4,128)S(1)}, u32[]{:S(2)}) copy-start(f32[4,80]{1,0:T(4,128)S(1)} %broadcast_multiply_fusion) | copy-start | bytes 3844
  60.6 5.5 %collective-permute-start.11 = (f32[144,128]{1,0:T(8,128)S(1)}, f32[144,128]{1,0:T(8,128)S(1)}, u32[]{:S(2)}, u32[]{:S(2)}) collective-permute-start(f32[144,128]{1,0:T(8,128)S(1)} %get-tuple-element.79), channel_id=1, source_target_pairs={{0,2},{1,3},{2,0},{3,1},{4,6},{5,7},{6,4},{7,5},{8,10},{9,11},{10,... | collective-permute-start | bytes 221192 | tf_op jit(solution)/shard_map/ppermute | solution.py:514
  61.6 7.7 %collective-permute-start.9 = (f32[144,128]{1,0:T(8,128)S(1)}, f32[144,128]{1,0:T(8,128)S(1)}, u32[]{:S(2)}, u32[]{:S(2)}) collective-permute-start(f32[144,128]{1,0:T(8,128)S(1)} %get-tuple-element.72), channel_id=1, source_target_pairs={{0,3},{1,2},{2,1},{3,0},{4,7},{5,6},{6,5},{7,4},{8,11},{9,10},{10,... | collective-permute-start | bytes 221192 | tf_op jit(solution)/shard_map/ppermute | solution.py:514
  65.6 3.8 %collective-permute-start.10 = (f32[144,128]{1,0:T(8,128)S(1)}, f32[144,128]{1,0:T(8,128)S(1)}, u32[]{:S(2)}, u32[]{:S(2)}) collective-permute-start(f32[144,128]{1,0:T(8,128)S(1)} %get-tuple-element.73), channel_id=1, source_target_pairs={{0,1},{1,0},{2,3},{3,2},{4,5},{5,4},{6,7},{7,6},{8,9},{9,8},{10,11... | collective-permute-start | bytes 221192 | tf_op jit(solution)/shard_map/ppermute | solution.py:514

commit v3 on v2

--- a/solution.py
+++ b/solution.py
@@ -22,11 +22,20 @@
 EDGE = DEPTH * RITZ
 SIDE = RITZ + 4 * GROUPS
 CHUNK = 8
-PIECES = 4
+PIECE = 16
 EARLY = (0, 2)
 LATE = (3, 1)
 MIB = 1024 * 1024
 VMEM_LIMIT = 24 * MIB
+
+
+def member_index():
+    return lax.axis_index("mem")
+
+
+def has_rows():
+    lat = lax.axis_index("lat")
+    return [jnp.where(lat > 0, 1.0, 0.0), jnp.where(lat < lax.axis_size("lat") - 1, 1.0, 0.0)]
 
 
 def iota(shape, dim):
@@ -95,12 +104,13 @@
             ref[place + LEVELS : place + 2 * LEVELS, :] = jnp.sum(jnp.where(outer, fine, 0.0), axis=1)
 
 
-def restrict_kernel(f_ref, v_ref, copy_ref, e_ref, h_ref, first_ref, last_ref, w_ref, a_ref, o_ref, m_ref, sem):
-    rows = RITZ * MAIN // PIECES
+def restrict_kernel(
+    f_ref, v_ref, copy_ref, e_ref, h_ref, first_ref, last_ref, w_ref, a_ref, o_ref, m_ref, sem
+):
     copies = []
-    for piece in range(PIECES):
-        place = pl.ds(rows * piece, rows)
-        copy = pltpu.make_async_copy(v_ref.at[place, :], copy_ref.at[place, :], sem.at[piece])
+    for start in range(0, RITZ, PIECE):
+        place = pl.ds(MAIN * start, MAIN * PIECE)
+        copy = pltpu.make_async_copy(v_ref.at[place, :], copy_ref.at[place, :], sem.at[start // PIECE])
         copy.start()
         copies.append(copy)
     fine = iota((3 * COLS, 2 * COLS), 0)
@@ -140,8 +150,8 @@
         packed = jnp.zeros((MAIN, COLS), F32)
         for index in range(half):
             k = half * part + index
-            if k % (RITZ // PIECES) == 0:
-                copies[k // (RITZ // PIECES)].wait()
+            if k % PIECE == 0:
+                copies[k // PIECE].wait()
             turned = pltpu.roll(copy_ref[MAIN * k : MAIN * (k + 1), :], 2 * index + 1, 1)
             packed = jnp.where(lanes == index, turned, packed)
         m_ref[...] = jnp.transpose(packed)
@@ -151,7 +161,7 @@
 
 
 def sides_kernel(
-    where_ref, above_ref, below_ref, e_ref, h_ref, first_ref, last_ref, w_ref,
+    above_ref, below_ref, e_ref, h_ref, first_ref, last_ref, w_ref,
     left_ref, right_ref, e2_ref, h2_ref, x0_ref, x1_ref, x2_ref, x3_ref, m_ref
 ):
     corner = diagonal(8)
@@ -163,8 +173,7 @@
     corners = ([], [])
     received = []
     for index, ref in enumerate((above_ref, below_ref)):
-        keep = where_ref[1 + index].astype(F32)
-        parts = [keep * ref[2 * LEVELS * part : 2 * LEVELS * (part + 1), :] for part in range(3)]
+        parts = [has_rows()[index] * ref[2 * LEVELS * part : 2 * LEVELS * (part + 1), :] for part in range(3)]
         received.append(jnp.concatenate(parts, axis=1))
     received = dot_split(jnp.concatenate(received, axis=0), w_ref[...]) * (1.0 / 81.0)
     for group in range(GROUPS):
@@ -196,77 +205,73 @@
                 rows.append(extra[2 * group + 1])
             ref[RITZ + 8 * pair : RITZ + 8 * pair + 8, :] = stack_rows(rows)
     for slot, ref in enumerate((x0_ref, x1_ref, x2_ref, x3_ref)):
-        group = where_ref[0] ^ slot
+        group = member_index() ^ slot
         ref[:MAIN] = e2_ref[group, :, :COLS]
         ref[MAIN:] = stack_rows([m_ref[pl.ds(4 * group + 2 + side, 1), :] for side in range(2)])
 
 
 def bands_kernel(v_ref, left_ref, right_ref, down_ref, up_ref):
-    lanes = iota((RITZ, COLS), 1)
+    lanes = iota((COLS, COLS), 1)
     for ref, row in ((up_ref, 0), (down_ref, ROWS - 1)):
-        corners = jnp.zeros((RITZ, COLS), F32)
+        corners = jnp.zeros((COLS, COLS), F32)
         for level in range(DEPTH):
             source = ROWS * level + row
-            ref[RITZ * level : RITZ * (level + 1), :] = v_ref[pl.ds(source, RITZ, stride=MAIN), :]
+            start = RITZ * level
+            ref[start : start + RITZ, :] = v_ref[pl.ds(source, RITZ, stride=MAIN), :]
             for side, columns in enumerate((left_ref, right_ref)):
                 target = DEPTH * side + level
-                turned = pltpu.roll(columns[:RITZ, :], (target - source) % COLS, 1)
+                column = jnp.concatenate([columns[:RITZ, :], jnp.zeros((COLS - RITZ, COLS), F32)], axis=0)
+                turned = pltpu.roll(column, (target - source) % COLS, 1)
                 corners = jnp.where(lanes == target, turned, corners)
-        ref[EDGE:, :] = corners
-
-
-def edge_parts(where_ref, above_ref, below_ref, left_ref, right_ref):
-    keep = [where_ref[1 + index].astype(F32) for index in range(2)]
+        ref[EDGE:, :] = jnp.transpose(corners)[:8]
+
+
+def edge_parts(above_ref, below_ref, left_ref, right_ref):
+    keep = has_rows()
     parts = []
     for index, source in enumerate((above_ref, below_ref)):
         for level in range(DEPTH):
             parts.append(keep[index] * source[RITZ * level : RITZ * (level + 1), :])
-    parts += [left_ref[:RITZ, :], keep[0] * above_ref[EDGE:, :], right_ref[:RITZ, :], keep[1] * below_ref[EDGE:, :]]
-    return parts
-
-
-def accumulate(v_ref, blocks, base):
-    sums = [[jnp.zeros((8, COLS), F32) for _ in range(CHUNK)] for _ in blocks]
-    for tile in range(MAIN // 8):
-        fields = [block[8 * tile : 8 * tile + 8, :] for block in blocks]
-        for k in range(CHUNK):
-            vector = v_ref[pl.ds(pl.multiple_of((base + k) * MAIN + 8 * tile, 8), 8), :]
-            for member, field in enumerate(fields):
-                sums[member][k] = sums[member][k] + vector * field
-    return [stack_rows([jnp.sum(value, axis=0, keepdims=True) for value in member]) for member in sums]
-
-
-def near_kernel(v_ref, c0_ref, c2_ref, s_ref):
+    parts += [left_ref[:RITZ, :], right_ref[:RITZ, :]]
+    corners = [keep[index] * source[EDGE:, :RITZ] for index, source in enumerate((above_ref, below_ref))]
+    return parts, corners
+
+
+def lane_sums(v_ref, blocks, left_ref, right_ref, s_ref):
     def body(step, carry):
         base = pl.multiple_of(step * CHUNK, CHUNK)
-        for member, total in enumerate(accumulate(v_ref, (c0_ref, c2_ref), base)):
-            s_ref[member, pl.ds(base, CHUNK), :] = total
+        sums = [[jnp.zeros((8, COLS), F32) for _ in range(CHUNK)] for _ in blocks]
+        for tile in range(MAIN // 8):
+            fields = [block[8 * tile : 8 * tile + 8, :] for block in blocks]
+            for k in range(CHUNK):
+                vector = v_ref[pl.ds(pl.multiple_of((base + k) * MAIN + 8 * tile, 8), 8), :]
+                for member, field in enumerate(fields):
+                    sums[member][k] = sums[member][k] + vector * field
+        for member, block in enumerate(blocks):
+            total = stack_rows([jnp.sum(value, axis=0, keepdims=True) for value in sums[member]])
+            for side, column_ref in enumerate((left_ref, right_ref)):
+                total = total + column_ref[pl.ds(base, CHUNK), :] * block[MAIN + side : MAIN + side + 1, :]
+            s_ref[pl.ds(COLS * member + base, CHUNK), :] = total
         return carry
 
     lax.fori_loop(0, RITZ // CHUNK, body, 0)
-
-
-def far_kernel(
-    where_ref, near_ref, v_ref, c0_ref, c1_ref, c2_ref, c3_ref, left_ref, right_ref, p_ref, s_ref
-):
-    blocks = (c0_ref, c2_ref, c3_ref, c1_ref)
-
-    def body(step, carry):
-        base = pl.multiple_of(step * CHUNK, CHUNK)
-        totals = [near_ref[member, pl.ds(base, CHUNK), :] for member in range(2)]
-        totals += accumulate(v_ref, (c3_ref, c1_ref), base)
-        parts = [ref[pl.ds(base, CHUNK), :] for ref in (left_ref, right_ref)]
-        for member, total in enumerate(totals):
-            for index, part in enumerate(parts):
-                total = total + part * blocks[member][MAIN + index : MAIN + index + 1, :]
-            s_ref[member, pl.ds(base, CHUNK), :] = total
-        return carry
-
-    lax.fori_loop(0, RITZ // CHUNK, body, 0)
-    ones = jnp.ones((8, COLS), F32)
-    for index, slot in enumerate((0, 2, 3, 1)):
-        reduced = exact_dot(ones, s_ref[index], ((1,), (1,)))
-        p_ref[pl.ds(where_ref[0] ^ slot, 1), :] = reduced[0:1, :]
+    high, low = split(s_ref[...])
+    rest = (s_ref[...] - high.astype(F32) - low.astype(F32)).astype(BF16)
+    ones = jnp.ones((8, 3 * COLS), BF16)
+    parts = jnp.concatenate([high, low, rest], axis=1)
+    sums = lax.dot_general(ones, parts, (((1,), (1,)), ((), ())), preferred_element_type=F32)
+    return [sums[0:1, COLS * member : COLS * member + RITZ] for member in range(len(blocks))]
+
+
+def near_kernel(v_ref, c0_ref, c2_ref, left_ref, right_ref, p_ref, s_ref):
+    for index, row in enumerate(lane_sums(v_ref, (c0_ref, c2_ref), left_ref, right_ref, s_ref)):
+        p_ref[index : index + 1, :] = row
+
+
+def far_kernel(near_ref, v_ref, c3_ref, c1_ref, left_ref, right_ref, p_ref, s_ref):
+    rows = lane_sums(v_ref, (c3_ref, c1_ref), left_ref, right_ref, s_ref)
+    for slot, row in zip((0, 2, 3, 1), [near_ref[0:1, :], near_ref[1:2, :]] + rows):
+        p_ref[pl.ds(member_index() ^ slot, 1), :] = row
 
 
 def exact_dot(left, right, dims):
@@ -281,13 +286,13 @@
     for part in range(2):
 
         def body(index, sums, part=part):
-            sums = list(sums)
             prepare(part, index)
             for offset in range(CHUNK):
                 k = index * CHUNK + offset
                 vector = v_ref[k, part]
-                for position, member in enumerate(slots):
-                    sums[position] = sums[position] + b_ref[pl.ds(RITZ * member + k, 1), :] * vector
+                sums = [
+                    value + b_ref[pl.ds(RITZ * member + k, 1), :] * vector for value, member in zip(sums, slots)
+                ]
             return tuple(sums)
 
         zeros = tuple(jnp.zeros((half, COLS), F32) for _ in slots)
@@ -296,16 +301,16 @@
 
 
 def update_kernel(
-    where_ref, c_ref, v_hbm_ref, above_ref, below_ref, left_ref, right_ref,
+    c_ref, v_hbm_ref, above_ref, below_ref, left_ref, right_ref,
     v_ref, b_ref, edge_ref, u1_ref, u2_ref, u3_ref, sem
 ):
-    me = where_ref[0]
+    me = member_index()
     outs = (None, u1_ref, u2_ref, u3_ref)
     pieces = RITZ // CHUNK
 
     def copy(part, piece):
-        place = pl.ds(piece * CHUNK, CHUNK)
-        return pltpu.make_async_copy(v_hbm_ref.at[place, part], v_ref.at[place, part], sem.at[part, piece])
+        source = v_hbm_ref.at[pl.ds(piece * CHUNK, CHUNK), part]
+        return pltpu.make_async_copy(source, v_ref.at[pl.ds(piece * CHUNK, CHUNK), part], sem.at[part, piece])
 
     for part in range(2):
         for piece in range(pieces):
@@ -316,14 +321,18 @@
         b_ref[RITZ * member : RITZ * (member + 1), :] = exact_dot(coefficients, chosen, ((0,), (0,)))
     swap = jnp.where(iota((8, 8), 1) == (me ^ iota((8, 8), 0)), 1.0, 0.0)
     ordered = exact_dot(swap, coefficients, ((1,), (0,)))
-    parts = edge_parts(where_ref, above_ref, below_ref, left_ref, right_ref)
+    parts, corners = edge_parts(above_ref, below_ref, left_ref, right_ref)
     edge = exact_dot(ordered, jnp.concatenate(parts, axis=1), ((1,), (0,)))
+    corners = [exact_dot(ordered, corner, ((1,), (1,))) for corner in corners]
+    places = list(range(2 * DEPTH)) + [8, 10]
     for member in range(GROUPS):
         ref, start = (outs[member], MAIN) if member else (edge_ref, 0)
-        for index in range(len(parts)):
+        ref[start + 8 : start + HALO, :] = jnp.zeros((HALO - 8, COLS), F32)
+        for index, place in enumerate(places):
             row = edge[member : member + 1, COLS * index : COLS * (index + 1)]
-            ref[start + index : start + index + 1, :] = row
-        ref[start + 12 : start + HALO, :] = jnp.zeros((4, COLS), F32)
+            ref[start + place : start + place + 1, :] = row
+        for index, place in enumerate((9, 11)):
+            ref[start + place : start + place + 1, :8] = corners[index][member : member + 1, :]
 
     def prepare(part, index):
         copy(part, index).wait()
@@ -351,7 +360,7 @@
     return copies
 
 
-def prolong_kernel(slots, where_ref, ra_ref, rb_ref, e2_ref, h2_ref, left_ref, right_ref, *refs):
+def prolong_kernel(slots, ra_ref, rb_ref, e2_ref, h2_ref, left_ref, right_ref, *refs):
     early_ref = None
     copies = []
     if len(refs) == 4:
@@ -359,17 +368,17 @@
     else:
         early_ref, o_ref, a_ref, f_ref, z_ref, m_ref, early_sem, sem = refs
         for index, slot in enumerate(EARLY):
-            copies += write_group(o_ref, early_ref, where_ref[0] ^ slot, index, early_sem)
+            copies += write_group(o_ref, early_ref, member_index() ^ slot, index, early_sem)
     coarse = iota((2 * COLS, 3 * COLS), 0)
     fine = iota((2 * COLS, 3 * COLS), 1)
     coarse = jnp.where(coarse == COLS + 2, 0, jnp.where(coarse == COLS + 3, COLS - 1, coarse))
     z_ref[...] = tent_weights(coarse, fine).astype(F32).astype(BF16)
     row = iota((8, COLS), 0)
-    keep = jnp.where(row < DEPTH, where_ref[1], where_ref[2]).astype(F32)
+    keep = jnp.where(row < DEPTH, *has_rows())
     outer_lanes = iota((MAIN, COLS), 1) < 4
     position = iota((ROWS, 3 * COLS), 0)
     for index, (slot, r_ref) in enumerate(zip(slots, (ra_ref, rb_ref))):
-        group = where_ref[0] ^ slot
+        group = member_index() ^ slot
         start = RITZ + 4 * group
         outer = [r_ref[MAIN + 8 + kind : MAIN + 9 + kind, :] for kind in range(4)]
         first_half = iota((1, COLS), 1) < DEPTH
@@ -415,31 +424,33 @@
     return jax.ShapeDtypeStruct(shape, F32)
 
 
-SMEM = pl.BlockSpec(memory_space=pltpu.SMEM)
 VMEM = pl.BlockSpec(memory_space=pltpu.VMEM)
 HBM = pl.BlockSpec(memory_space=pltpu.HBM)
 FIELD = (GROUPS, MAIN, 2 * COLS)
 RIM = (GROUPS, 8, 2 * COLS)
 
 
-def call(kernel, name, ins, outs, scratch, out_specs=None, limit=VMEM_LIMIT, aliases=None):
+def call(kernel, name, ins, outs, scratch, out_specs=None):
     return pl.pallas_call(
         kernel,
         in_specs=ins,
         out_specs=out_specs or [VMEM] * len(outs),
         out_shape=outs,
         scratch_shapes=scratch,
-        input_output_aliases=aliases or {},
-        compiler_params=pltpu.CompilerParams(vmem_limit_bytes=limit),
+        compiler_params=pltpu.CompilerParams(vmem_limit_bytes=VMEM_LIMIT),
         name=name,
     )
+
+
+def pinned(value):
+    return pltpu.with_memory_space_constraint(value, pltpu.HBM)
 
 
 def edges(gradients):
     scratch = [pltpu.SemaphoreType.DMA((3,))]
     outs = [pltpu.VMEM((3, LEVELS, 3 * ROWS, COLS), F32)] + [struct(BAND, COLS)] * 2
-    gradients = pltpu.with_memory_space_constraint(gradients, pltpu.HBM)
-    return call(edges_kernel, "edges", [HBM], outs, scratch, limit=VMEM_LIMIT)(gradients)
+    gradients = pinned(gradients)
+    return call(edges_kernel, "edges", [HBM], outs, scratch)(gradients)
 
 
 def restrict(fine, ritz_vectors):
@@ -447,64 +458,62 @@
         pltpu.VMEM((2 * BLOCK, 3 * COLS), BF16),
         pltpu.VMEM((HALO, 3 * COLS), F32),
         pltpu.VMEM((COLS, COLS), F32),
-        pltpu.SemaphoreType.DMA((PIECES,)),
+        pltpu.SemaphoreType.DMA((RITZ // PIECE,)),
     ]
-    outs = [pltpu.VMEM((RITZ * MAIN, COLS), F32), struct(*FIELD), struct(*RIM)] + [struct(RITZ, COLS)] * 2
-    outs += [jax.ShapeDtypeStruct((3 * COLS, 2 * COLS), BF16)]
-    flat = ritz_vectors.reshape(RITZ * MAIN, COLS)
-    flat = pltpu.with_memory_space_constraint(flat, pltpu.HBM)
-    return call(restrict_kernel, "restrict", [VMEM, HBM], outs, scratch, limit=VMEM_LIMIT)(fine, flat)
+    outs = [pltpu.VMEM((RITZ * MAIN, COLS), F32)]
+    outs += [struct(*FIELD), struct(*RIM)] + [struct(RITZ, COLS)] * 2
+    outs += [pltpu.VMEM((3 * COLS, 2 * COLS), BF16)]
+    flat = pinned(ritz_vectors.reshape(RITZ * MAIN, COLS))
+    return call(restrict_kernel, "restrict", [VMEM, HBM], outs, scratch)(fine, flat)
 
 
 def sides(*args):
     outs = [struct(SIDE, COLS)] * 2 + [struct(*FIELD), struct(*RIM)] + [struct(MAIN + 8, COLS)] * 4
-    return call(sides_kernel, "sides", [SMEM] + [VMEM] * 7, outs, [pltpu.VMEM((COLS, COLS), F32)])(*args)
+    return call(sides_kernel, "sides", [VMEM] * 7, outs, [pltpu.VMEM((COLS, COLS), F32)])(*args)
 
 
 def bands(*args):
-    return call(bands_kernel, "bands", [VMEM] * 3, [struct(EDGE + RITZ, COLS)] * 2, [])(*args)
-
-
-def near(ritz_vectors, blocks):
-    return call(near_kernel, "near", [VMEM] * 3, [struct(2, RITZ, COLS)], [])(ritz_vectors, *blocks)[0]
-
-
-def far(place, sums, ritz_vectors, blocks, messages):
-    outs = [struct(GROUPS, RITZ)]
-    scratch = [pltpu.VMEM((GROUPS, RITZ, COLS), F32)]
-    return call(far_kernel, "far", [SMEM] + [VMEM] * 8, outs, scratch)(
-        place, sums, ritz_vectors, *blocks, *messages
-    )[0]
-
-
-def update(place, coefficients, ritz_vectors, messages):
+    return call(bands_kernel, "bands", [VMEM] * 3, [struct(EDGE + 8, COLS)] * 2, [])(*args)
+
+
+def near(held, blocks, columns):
+    outs, scratch = [struct(2, RITZ)], [pltpu.VMEM((2 * COLS, COLS), F32)]
+    return call(near_kernel, "near", [VMEM] * 5, outs, scratch)(held, *blocks, *columns)[0]
+
+
+def far(sums, held, blocks, columns):
+    outs, scratch = [struct(GROUPS, RITZ)], [pltpu.VMEM((2 * COLS, COLS), F32)]
+    return call(far_kernel, "far", [VMEM] * 6, outs, scratch)(sums, held, *blocks, *columns)[0]
+
+
+def update(coefficients, ritz_vectors, messages):
     outs = [pltpu.VMEM((RITZ, 2, MAIN // 2, COLS), F32), struct(GROUPS * RITZ, COLS), struct(HALO, COLS)]
     outs += [struct(BLOCK, COLS)] * 3
     scratch = [pltpu.SemaphoreType.DMA((2, RITZ // CHUNK))]
     doubled = jnp.concatenate([coefficients, coefficients], axis=0)
-    return call(update_kernel, "update", [SMEM, VMEM, HBM] + [VMEM] * 4, outs, scratch, limit=VMEM_LIMIT)(
-        place, doubled, pltpu.with_memory_space_constraint(ritz_vectors.reshape(RITZ, 2, MAIN // 2, COLS), pltpu.HBM), *messages
+    return call(update_kernel, "update", [VMEM, HBM] + [VMEM] * 4, outs, scratch)(
+        doubled, pinned(ritz_vectors.reshape(RITZ, 2, MAIN // 2, COLS)), *messages
     )
 
 
-def own(ritz_vectors, weights, edge):
-    return call(own_kernel, "own", [VMEM] * 3, [struct(BLOCK, COLS)], [])(ritz_vectors, weights, edge)[0]
-
-
-def prolong(place, slots, returned, main, edge, left, right, early=None):
+def own(*args):
+    return call(own_kernel, "own", [VMEM] * 3, [struct(BLOCK, COLS)], [])(*args)[0]
+
+
+def prolong(slots, returned, main, edge, left, right, early=None):
     scratch = [
         pltpu.VMEM((MAIN + 8, 2 * COLS), F32),
         pltpu.VMEM((MAIN + 8, 3 * COLS), F32),
         pltpu.VMEM((2 * COLS, 3 * COLS), BF16),
     ]
     stage = (2, 3, DEPTH, 3 * ROWS, COLS)
-    args = (place, *returned, main, edge, left, right)
-    specs = [SMEM] + [VMEM] * 6
+    args = (*returned, main, edge, left, right)
+    specs = [VMEM] * 6
     kernel = functools.partial(prolong_kernel, slots)
     if early is None:
         return call(kernel, "prolong_early", specs, [pltpu.VMEM(stage, F32)], scratch)(*args)[0]
     scratch += [pltpu.VMEM(stage, F32), pltpu.SemaphoreType.DMA((2, 3)), pltpu.SemaphoreType.DMA((2, 3))]
-    outs = [struct(GROUPS * DEPTH, 3 * ROWS, 3 * COLS)]
+    outs = [jax.ShapeDtypeStruct((GROUPS * DEPTH, 3 * ROWS, 3 * COLS), F32)]
     return call(kernel, "prolong_late", specs + [VMEM], outs, scratch, [HBM])(*args, early)[0]
 
 
@@ -523,8 +532,6 @@
 
 def per_device(gradients, ritz_vectors, ritz_values):
     lats, lons = lax.axis_size("lat"), lax.axis_size("lon")
-    lat, mem = lax.axis_index("lat"), lax.axis_index("mem")
-    place = jnp.stack([mem, jnp.where(lat > 0, 1, 0), jnp.where(lat < lats - 1, 1, 0)]).astype(jnp.int32)
 
     gradients = gradients.reshape(gradients.shape[1:])
     fine, down, up = edges(gradients)
@@ -533,30 +540,30 @@
     above = lax.ppermute(down, "lat", over)
     below = lax.ppermute(up, "lat", under)
     held, main, edge, first, last, weights = restrict(fine, ritz_vectors)
-    to_left, to_right, main, edge, *blocks = sides(place, above, below, main, edge, first, last, weights)
+    to_left, to_right, main, edge, *blocks = sides(above, below, main, edge, first, last, weights)
     right = lax.ppermute(to_left, "lon", [((i + 1) % lons, i) for i in range(lons)])
     left = lax.ppermute(to_right, "lon", [(i, (i + 1) % lons) for i in range(lons)])
     spread = [blocks[0]] + exchange_members(blocks)
-    near_sums = near(held, (spread[0], spread[2]))
+    near_sums = near(held, (spread[0], spread[2]), (left, right))
     left, right, near_sums, *spread = lax.optimization_barrier((left, right, near_sums, *spread))
     down, up = bands(held, left, right)
     above = lax.ppermute(down, "lat", over)
     below = lax.ppermute(up, "lat", under)
     *spread, _, _ = lax.optimization_barrier((*spread, down, up))
-    partial = far(place, near_sums, held, spread, (left, right))
-    partial = exchange_sum(partial, ("lon", "mem"))
-    partial, above, below = lax.optimization_barrier((partial, above, below))
-    projections = exchange_sum(partial, "lat")
+    partial = far(near_sums, held, (spread[3], spread[1]), (left, right))
     cells = GROUPS * DEPTH * ROWS * lats * COLS * lons
-    coefficients = (1.0 / ritz_values - 1.0)[None, :] * (projections * (1.0 / cells))
-
+    factors = (1.0 / ritz_values - 1.0) * (1.0 / cells)
+    partial, factors = lax.optimization_barrier((partial, factors))
+    for shift in (1, 2):
+        partial = partial + lax.ppermute(partial, "mem", [(i, i ^ shift) for i in range(4)])
+    coefficients = factors[None, :] * exchange_sum(partial, ("lat", "lon"))
     messages = (above, below, left, right)
-    held, weights, own_edge, *sent = update(place, coefficients, ritz_vectors, messages)
+    held, weights, own_edge, *sent = update(coefficients, ritz_vectors, messages)
     returned = exchange_members([None] + sent)
     mine = own(held, weights, own_edge)
     returned = [mine] + returned
-    early = prolong(place, EARLY, [returned[slot] for slot in EARLY], main, edge, left, right)
-    output = prolong(place, LATE, [returned[slot] for slot in LATE], main, edge, left, right, early)
+    early = prolong(EARLY, [returned[slot] for slot in EARLY], main, edge, left, right)
+    output = prolong(LATE, [returned[slot] for slot in LATE], main, edge, left, right, early)
     preconditioned = output[None]
     return preconditioned, coefficients
 

time: 71.8 us -> 66.4 us (0.925)
  blocking collectives: 15.5 us -> 0 us
  waiting for transfers between devices: 10.4 us -> 16.8 us
  starting transfers between devices: 27.6 us -> 33.9 us
  Pallas kernels: 16.5 us -> 14 us
    all_to_all x1 -> x0, blocking collectives: 15.5 us -> none  [exchange_sum(): return jnp.sum(lax.all_to_all(copies, axes, 0, 0, tiled=True), axis=0)]
    ppermute x0 -> x2, waiting for transfers between devices: none -> 3.43 us  [per_device(): lax.ppermute(partial, 'mem', [(i, i ^ shift) for i in range(4)])]
    ppermute x6, waiting for transfers between devices: 3.22 us -> 6.31 us  [exchange_members(): lax.ppermute(blocks[shift], 'mem', [(i, i ^ shift) for i in range(size)])]
    all_to_all x1, starting transfers between devices: 5.48 us -> 7.74 us  [exchange_sum(): return jnp.sum(lax.all_to_all(copies, axes, 0, 0, tiled=True), axis=0)]
    ppermute x6, starting transfers between devices: 9.29 us -> 11.5 us  [exchange_members(): lax.ppermute(blocks[shift], 'mem', [(i, i ^ shift) for i in range(size)])]
    ppermute x0 -> x2, starting transfers between devices: none -> 1.71 us  [per_device(): lax.ppermute(partial, 'mem', [(i, i ^ shift) for i in range(4)])]
    pallas_call x8, Pallas kernels: 13.1 us -> 11.6 us  [the longest x1 3.17 us: update(): call(update_kernel, 'update', [VMEM, HBM] + [VMEM] * 4, outs, scratch)]
    ppermute x2, starting transfers between devices: 2.63 us -> 3.63 us  [per_device(): above = lax.ppermute(down, 'lat', over)]
  transfers between devices with their start and end apart: 13 -> 15, of which waited for: 4 -> 6; matrix products, arithmetic and copies ran while one was open for 0% -> 0% of each run, Pallas kernels for 10% -> 8%
where the time goes in v3:
time: 66.4 us; the launch traced here: 66.3 us
  starting transfers between devices  33.9 us (51%)
  waiting for transfers between devices  16.8 us (25%)
  Pallas kernels  14 us (21%)
  between operations  0.78 us (1%)
  local copies, waits for them, and re-layouts  0.68 us (1%)
    ppermute x6, starting transfers between devices, exchange_members(): lax.ppermute(blocks[shift], 'mem', [(i, i ^ shift) for i in range(size)])  11.5 us
    all_to_all x1, starting transfers between devices, exchange_sum(): return jnp.sum(lax.all_to_all(copies, axes, 0, 0, tiled=True), axis=0)  7.74 us
    all_to_all x1, waiting for transfers between devices, exchange_sum(): return jnp.sum(lax.all_to_all(copies, axes, 0, 0, tiled=True), axis=0)  7.06 us
    ppermute x6, waiting for transfers between devices, exchange_members(): lax.ppermute(blocks[shift], 'mem', [(i, i ^ shift) for i in range(size)])  6.31 us
    ppermute x2, starting transfers between devices, per_device(): below = lax.ppermute(up, 'lat', under)  5.69 us
    ppermute x2, starting transfers between devices, per_device(): above = lax.ppermute(down, 'lat', over)  3.63 us
    ppermute x2, waiting for transfers between devices, per_device(): lax.ppermute(partial, 'mem', [(i, i ^ shift) for i in range(4)])  3.43 us
    pallas_call x1, Pallas kernels, update(): call(update_kernel, 'update', [VMEM, HBM] + [VMEM] * 4, outs, scratch)  3.17 us
  transfers between devices with their start and end apart: 15, of which 6 were waited for; matrix products, arithmetic and copies ran while one was open for 0% of the time, Pallas kernels for 8%

profile of v3, /device:TPU:1, one launch (start us, length us, event | category | flops | bytes accessed | tf_op | source)
XLA Modules:
  0.0 66.3 jit_solution(15205839934467684964)
XLA Ops:
  0.6 1.7 %edges.1 = (f32[3,16,96,128]{3,2,1,0:T(8,128)S(1)}, f32[96,128]{1,0:T(8,128)S(1)}, f32[96,128]{1,0:T(8,128)S(1)}) custom-call(f32[16,96,384]{2,1,0:T(8,128)} %bitcast.6), custom_call_target="tpu_custom_call" | custom-call | tf_op jit(solution)/shard_map/edges/pallas_call | solution.py:453
  2.4 2.5 %collective-permute-start = (f32[96,128]{1,0:T(8,128)S(1)}, f32[96,128]{1,0:T(8,128)S(1)}, u32[]{:S(2)}, u32[]{:S(2)}) collective-permute-start(f32[96,128]{1,0:T(8,128)S(1)} %get-tuple-element.36), channel_id=1, source_target_pairs={{0,32},{32,64},{64,96},{96,128},{128,160},{160,192},{192,224},{224... | collective-permute-start | bytes 147464 | tf_op jit(solution)/shard_map/ppermute | solution.py:540
  4.9 4.0 %collective-permute-start.1 = (f32[96,128]{1,0:T(8,128)S(1)}, f32[96,128]{1,0:T(8,128)S(1)}, u32[]{:S(2)}, u32[]{:S(2)}) collective-permute-start(f32[96,128]{1,0:T(8,128)S(1)} %get-tuple-element.37), channel_id=1, source_target_pairs={{32,0},{64,32},{96,64},{128,96},{160,128},{192,160},{224,192},{0,2... | collective-permute-start | bytes 147464 | tf_op jit(solution)/shard_map/ppermute | solution.py:541
  8.9 3.2 %restrict.1 = (f32[10240,128]{1,0:T(8,128)S(1)}, f32[4,128,256]{2,1,0:T(8,128)S(1)}, f32[4,8,256]{2,1,0:T(8,128)S(1)}, f32[80,128]{1,0:T(8,128)S(1)}, f32[80,128...) custom-call(f32[3,16,96,128]{3,2,1,0:T(8,128)S(1)} %get-tuple-element.38.f_ref, f32[10240,128]{1,0:T(8,128)} %bitcast.4), custom_call_target="tpu_custom_call" | custom-call | tf_op jit(solution)/shard_map/restrict/pallas_call | solution.py:467
  12.1 0.0 collective-permute-done.above_ref
  12.1 0.5 sides.1
  12.6 1.4 %collective-permute-start.2 = (f32[96,128]{1,0:T(8,128)S(1)}, f32[96,128]{1,0:T(8,128)S(1)}, u32[]{:S(2)}, u32[]{:S(2)}) collective-permute-start(f32[96,128]{1,0:T(8,128)S(1)} %get-tuple-element.44), channel_id=1, source_target_pairs={{0,4},{4,8},{8,12},{12,16},{16,20},{20,24},{24,28},{28,0},{1,5},{5... | collective-permute-start | bytes 147464 | tf_op jit(solution)/shard_map/ppermute | solution.py:545
  14.0 2.3 %collective-permute-start.3 = (f32[96,128]{1,0:T(8,128)S(1)}, f32[96,128]{1,0:T(8,128)S(1)}, u32[]{:S(2)}, u32[]{:S(2)}) collective-permute-start(f32[96,128]{1,0:T(8,128)S(1)} %get-tuple-element.45), channel_id=1, source_target_pairs={{4,0},{8,4},{12,8},{16,12},{20,16},{24,20},{28,24},{0,28},{5,1},{9... | collective-permute-start | bytes 147464 | tf_op jit(solution)/shard_map/ppermute | solution.py:544
  16.3 2.9 %collective-permute-start.4 = (f32[136,128]{1,0:T(8,128)S(1)}, f32[136,128]{1,0:T(8,128)S(1)}, u32[]{:S(2)}, u32[]{:S(2)}) collective-permute-start(f32[136,128]{1,0:T(8,128)S(1)} %get-tuple-element.48), channel_id=1, source_target_pairs={{0,2},{1,3},{2,0},{3,1},{4,6},{5,7},{6,4},{7,5},{8,10},{9,11},{10,... | collective-permute-start | bytes 208904 | tf_op jit(solution)/shard_map/ppermute | solution.py:523
  19.2 1.8 %collective-permute-start.5 = (f32[136,128]{1,0:T(8,128)S(1)}, f32[136,128]{1,0:T(8,128)S(1)}, u32[]{:S(2)}, u32[]{:S(2)}) collective-permute-start(f32[136,128]{1,0:T(8,128)S(1)} %get-tuple-element.49), channel_id=1, source_target_pairs={{0,1},{1,0},{2,3},{3,2},{4,5},{5,4},{6,7},{7,6},{8,9},{9,8},{10,11... | collective-permute-start | bytes 208904 | tf_op jit(solution)/shard_map/ppermute | solution.py:523
  21.0 0.1 collective-permute-done.4.c2_ref
  21.1 1.1 %near.1.near_ref = f32[2,80]{1,0:T(2,128)S(1)} custom-call(f32[10240,128]{1,0:T(8,128)S(1)} %get-tuple-element.46.v_ref, f32[136,128]{1,0:T(8,128)S(1)} %get-tuple-element.47.c0_ref, f32[136,128]{1,0:T(8,128)S(1)} %collective-permute-done.4.c2_ref, f32[96,128]{1,0:T(8,128)S(1)} %collective-permute-done.2.left_ref, f32[96,128]{1,0:T(8,128)S(1)} %collective-permute-done.3.right_ref), custom_call_target="tpu_custom_call" | custom-call | tf_op jit(solution)/shard_map/near/pallas_call | solution.py:481
  22.2 4.1 %collective-permute-done.6.c3_ref = f32[136,128]{1,0:T(8,128)S(1)} collective-permute-done((f32[136,128]{1,0:T(8,128)S(1)}, f32[136,128]{1,0:T(8,128)S(1)}, u32[]{:S(2)}, u32[]{:S(2)}) %collective-permute-start.6) | collective-permute-done | bytes 69664 | tf_op jit(solution)/shard_map/ppermute | solution.py:523
  26.3 0.5 bands.1
  26.8 1.1 %far.1 = f32[4,80]{1,0:T(4,128)S(1)} custom-call(f32[2,80]{1,0:T(2,128)S(1)} %near.1.near_ref, f32[10240,128]{1,0:T(8,128)S(1)} %get-tuple-element.46.v_ref, f32[136,128]{1,0:T(8,128)S(1)} %collective-permute-done.6.c3_ref, f32[136,128]{1,0:T(8,128)S(1)} %collective-permute-done.5.c1_ref, f32[96,128]{1,0:T(8,128)S(1)} %collective-permute-done.2.left_ref, ...), custom_call_target="tpu_custom_call" | custom-call | tf_op jit(solution)/shard_map/far/pallas_call | solution.py:486
  27.9 0.1 collective-permute-start.7
  28.0 1.1 %collective-permute-done.7 = f32[4,80]{1,0:T(4,128)S(1)} collective-permute-done((f32[4,80]{1,0:T(4,128)S(1)}, f32[4,80]{1,0:T(4,128)S(1)}, u32[]{:S(2)}, u32[]{:S(2)}) %collective-permute-start.7) | collective-permute-done | bytes 1312 | tf_op jit(solution)/shard_map/ppermute | solution.py:558
  29.1 1.6 %collective-permute-start.8 = (f32[4,80]{1,0:T(4,128)S(1)}, f32[4,80]{1,0:T(4,128)S(1)}, u32[]{:S(2)}, u32[]{:S(2)}) collective-permute-start(f32[4,80]{1,0:T(4,128)S(1)} %add.7), channel_id=1, source_target_pairs={{0,2},{1,3},{2,0},{3,1},{4,6},{5,7},{6,4},{7,5},{8,10},{9,11},{10,... | collective-permute-start | bytes 3848 | tf_op jit(solution)/shard_map/ppermute | solution.py:558
  30.7 2.3 %collective-permute-done.8 = f32[4,80]{1,0:T(4,128)S(1)} collective-permute-done((f32[4,80]{1,0:T(4,128)S(1)}, f32[4,80]{1,0:T(4,128)S(1)}, u32[]{:S(2)}, u32[]{:S(2)}) %collective-permute-start.8) | collective-permute-done | bytes 1312 | tf_op jit(solution)/shard_map/ppermute | solution.py:558
  33.0 0.7 %broadcast_in_dim.4 = f32[64,4,80]{2,1,0:T(4,128)} broadcast(f32[4,80]{1,0:T(4,128)S(1)} %add.8), dimensions={1,2} | broadcast | bytes 83200 | tf_op jit(solution)/shard_map/broadcast_in_dim | solution.py:529
  33.7 7.7 %all-to-all-start = ((f32[64,4,80]{2,1,0:T(4,128)}), f32[64,4,80]{2,1,0:T(4,128)S(1)}, u32[]{:S(2)}, u32[]{:S(2)}) async-start(f32[64,4,80]{2,1,0:T(4,128)} %broadcast_in_dim.4), calls=%async_computation | async-start | bytes 262144 | tf_op jit(solution)/shard_map/all_to_all | solution.py:530
  41.4 1.1 %collective-permute-start.9 = (f32[328,128]{1,0:T(8,128)S(1)}, f32[328,128]{1,0:T(8,128)S(1)}, u32[]{:S(2)}, u32[]{:S(2)}) collective-permute-start(f32[328,128]{1,0:T(8,128)S(1)} %get-tuple-element.56), channel_id=1, source_target_pairs={{0,32},{32,64},{64,96},{96,128},{128,160},{160,192},{192,224},{224... | collective-permute-start | bytes 503816 | tf_op jit(solution)/shard_map/ppermute | solution.py:550
  42.5 1.7 %collective-permute-start.10 = (f32[328,128]{1,0:T(8,128)S(1)}, f32[328,128]{1,0:T(8,128)S(1)}, u32[]{:S(2)}, u32[]{:S(2)}) collective-permute-start(f32[328,128]{1,0:T(8,128)S(1)} %get-tuple-element.57), channel_id=1, source_target_pairs={{32,0},{64,32},{96,64},{128,96},{160,128},{192,160},{224,192},{0,2... | collective-permute-start | bytes 503816 | tf_op jit(solution)/shard_map/ppermute | solution.py:551
  44.2 7.1 %all-to-all-done = f32[64,4,80]{2,1,0:T(4,128)S(1)} async-done(((f32[64,4,80]{2,1,0:T(4,128)}), f32[64,4,80]{2,1,0:T(4,128)S(1)}, u32[]{:S(2)}, u32[]{:S(2)}) %all-to-all-start) | async-done | bytes 81952 | tf_op jit(solution)/shard_map/all_to_all | solution.py:530
  51.3 0.1 reduce_sum.9
  51.4 3.2 %update.1 = (f32[80,2,64,128]{3,2,1,0:T(8,128)S(1)}, f32[320,128]{1,0:T(8,128)S(1)}, f32[16,128]{1,0:T(8,128)S(1)}, f32[144,128]{1,0:T(8,128)S(1)}, f32[144,128]{1,0:T(8,128)S(1)}, /*index=5*/f32[144,128]{1,0:T(8,128)S(1)}) custom-call(f32[8,80]{1,0:T(8,128)S(1)} %pad_maximum_fusion.c_ref, f32[80,2,64,128]{3,2,1,0:T(8,128)} %bitcast.5, ...), custom_call_target="tpu_custom_call" | custom-call | tf_op jit(solution)/shard_map/update/pallas_call | solution.py:494
  54.6 1.7 %collective-permute-start.13 = (f32[144,128]{1,0:T(8,128)S(1)}, f32[144,128]{1,0:T(8,128)S(1)}, u32[]{:S(2)}, u32[]{:S(2)}) collective-permute-start(f32[144,128]{1,0:T(8,128)S(1)} %get-tuple-element.69), channel_id=1, source_target_pairs={{0,2},{1,3},{2,0},{3,1},{4,6},{5,7},{6,4},{7,5},{8,10},{9,11},{10,... | collective-permute-start | bytes 221192 | tf_op jit(solution)/shard_map/ppermute | solution.py:523
  56.3 5.1 %collective-permute-start.11 = (f32[144,128]{1,0:T(8,128)S(1)}, f32[144,128]{1,0:T(8,128)S(1)}, u32[]{:S(2)}, u32[]{:S(2)}) collective-permute-start(f32[144,128]{1,0:T(8,128)S(1)} %get-tuple-element.62), channel_id=1, source_target_pairs={{0,3},{1,2},{2,1},{3,0},{4,7},{5,6},{6,5},{7,4},{8,11},{9,10},{10,... | collective-permute-start | bytes 221192 | tf_op jit(solution)/shard_map/ppermute | solution.py:523
  61.3 0.4 own.1.ra_ref
  61.8 0.6 prolong_early.1.refs_0_
  62.4 2.1 %collective-permute-done.11.ra_ref = f32[144,128]{1,0:T(8,128)S(1)} collective-permute-done((f32[144,128]{1,0:T(8,128)S(1)}, f32[144,128]{1,0:T(8,128)S(1)}, u32[]{:S(2)}, u32[]{:S(2)}) %collective-permute-start.11) | collective-permute-done | bytes 73760 | tf_op jit(solution)/shard_map/ppermute | solution.py:523
  64.5 1.8 %prolong_late.1 = f32[16,96,384]{2,1,0:T(8,128)} custom-call(f32[144,128]{1,0:T(8,128)S(1)} %collective-permute-done.11.ra_ref, f32[144,128]{1,0:T(8,128)S(1)} %collective-permute-done.12.rb_ref, f32[4,128,256]{2,1,0:T(8,128)S(1)} %get-tuple-element.64.e2_ref, f32[4,8,256]{2,1,0:T(8,128)S(1)} %get-tuple-element.65.h2_ref, ...), custom_call_target="tpu_custom_call" | custom-call | tf_op jit(solution)/shard_map/prolong_late/pallas_call | solution.py:517
  (19 shorter events, 0.1 us)
Async XLA Ops:
  2.4 9.7 %collective-permute-start = (f32[96,128]{1,0:T(8,128)S(1)}, f32[96,128]{1,0:T(8,128)S(1)}, u32[]{:S(2)}, u32[]{:S(2)}) collective-permute-start(f32[96,128]{1,0:T(8,128)S(1)} %get-tuple-element.36), channel_id=1, source_target_pairs={{0,32},{32,64},{64,96},{96,128},{128,160},{160,192},{192,224},{224... | collective-permute-start | bytes 147464 | tf_op jit(solution)/shard_map/ppermute | solution.py:540
  4.9 7.2 %collective-permute-start.1 = (f32[96,128]{1,0:T(8,128)S(1)}, f32[96,128]{1,0:T(8,128)S(1)}, u32[]{:S(2)}, u32[]{:S(2)}) collective-permute-start(f32[96,128]{1,0:T(8,128)S(1)} %get-tuple-element.37), channel_id=1, source_target_pairs={{32,0},{64,32},{96,64},{128,96},{160,128},{192,160},{224,192},{0,2... | collective-permute-start | bytes 147464 | tf_op jit(solution)/shard_map/ppermute | solution.py:541
  8.9 12.0 %copy-start.1 = (f32[80]{0:T(128)S(1)}, f32[80]{0:T(128)}, u32[]{:S(2)}) copy-start(f32[80]{0:T(128)} %param.5) | copy-start | bytes 964
  12.6 8.4 %collective-permute-start.2 = (f32[96,128]{1,0:T(8,128)S(1)}, f32[96,128]{1,0:T(8,128)S(1)}, u32[]{:S(2)}, u32[]{:S(2)}) collective-permute-start(f32[96,128]{1,0:T(8,128)S(1)} %get-tuple-element.44), channel_id=1, source_target_pairs={{0,4},{4,8},{8,12},{12,16},{16,20},{20,24},{24,28},{28,0},{1,5},{5... | collective-permute-start | bytes 147464 | tf_op jit(solution)/shard_map/ppermute | solution.py:545
  14.0 7.0 %collective-permute-start.3 = (f32[96,128]{1,0:T(8,128)S(1)}, f32[96,128]{1,0:T(8,128)S(1)}, u32[]{:S(2)}, u32[]{:S(2)}) collective-permute-start(f32[96,128]{1,0:T(8,128)S(1)} %get-tuple-element.45), channel_id=1, source_target_pairs={{4,0},{8,4},{12,8},{16,12},{20,16},{24,20},{28,24},{0,28},{5,1},{9... | collective-permute-start | bytes 147464 | tf_op jit(solution)/shard_map/ppermute | solution.py:544
  16.3 4.8 %collective-permute-start.4 = (f32[136,128]{1,0:T(8,128)S(1)}, f32[136,128]{1,0:T(8,128)S(1)}, u32[]{:S(2)}, u32[]{:S(2)}) collective-permute-start(f32[136,128]{1,0:T(8,128)S(1)} %get-tuple-element.48), channel_id=1, source_target_pairs={{0,2},{1,3},{2,0},{3,1},{4,6},{5,7},{6,4},{7,5},{8,10},{9,11},{10,... | collective-permute-start | bytes 208904 | tf_op jit(solution)/shard_map/ppermute | solution.py:523
  19.2 3.0 %collective-permute-start.5 = (f32[136,128]{1,0:T(8,128)S(1)}, f32[136,128]{1,0:T(8,128)S(1)}, u32[]{:S(2)}, u32[]{:S(2)}) collective-permute-start(f32[136,128]{1,0:T(8,128)S(1)} %get-tuple-element.49), channel_id=1, source_target_pairs={{0,1},{1,0},{2,3},{3,2},{4,5},{5,4},{6,7},{7,6},{8,9},{9,8},{10,11... | collective-permute-start | bytes 208904 | tf_op jit(solution)/shard_map/ppermute | solution.py:523
  21.0 5.3 %collective-permute-start.6 = (f32[136,128]{1,0:T(8,128)S(1)}, f32[136,128]{1,0:T(8,128)S(1)}, u32[]{:S(2)}, u32[]{:S(2)}) collective-permute-start(f32[136,128]{1,0:T(8,128)S(1)} %get-tuple-element.50), channel_id=1, source_target_pairs={{0,3},{1,2},{2,1},{3,0},{4,7},{5,6},{6,5},{7,4},{8,11},{9,10},{10,... | collective-permute-start | bytes 208904 | tf_op jit(solution)/shard_map/ppermute | solution.py:523
  27.9 1.2 %collective-permute-start.7 = (f32[4,80]{1,0:T(4,128)S(1)}, f32[4,80]{1,0:T(4,128)S(1)}, u32[]{:S(2)}, u32[]{:S(2)}) collective-permute-start(f32[4,80]{1,0:T(4,128)S(1)} %far.1), channel_id=1, source_target_pairs={{0,1},{1,0},{2,3},{3,2},{4,5},{5,4},{6,7},{7,6},{8,9},{9,8},{10,11... | collective-permute-start | bytes 3848 | tf_op jit(solution)/shard_map/ppermute | solution.py:558
  29.1 3.9 %collective-permute-start.8 = (f32[4,80]{1,0:T(4,128)S(1)}, f32[4,80]{1,0:T(4,128)S(1)}, u32[]{:S(2)}, u32[]{:S(2)}) collective-permute-start(f32[4,80]{1,0:T(4,128)S(1)} %add.7), channel_id=1, source_target_pairs={{0,2},{1,3},{2,0},{3,1},{4,6},{5,7},{6,4},{7,5},{8,10},{9,11},{10,... | collective-permute-start | bytes 3848 | tf_op jit(solution)/shard_map/ppermute | solution.py:558
  33.7 17.6 %all-to-all-start = ((f32[64,4,80]{2,1,0:T(4,128)}), f32[64,4,80]{2,1,0:T(4,128)S(1)}, u32[]{:S(2)}, u32[]{:S(2)}) async-start(f32[64,4,80]{2,1,0:T(4,128)} %broadcast_in_dim.4), calls=%async_computation | async-start | bytes 262144 | tf_op jit(solution)/shard_map/all_to_all | solution.py:530
  41.4 9.9 %collective-permute-start.9 = (f32[328,128]{1,0:T(8,128)S(1)}, f32[328,128]{1,0:T(8,128)S(1)}, u32[]{:S(2)}, u32[]{:S(2)}) collective-permute-start(f32[328,128]{1,0:T(8,128)S(1)} %get-tuple-element.56), channel_id=1, source_target_pairs={{0,32},{32,64},{64,96},{96,128},{128,160},{160,192},{192,224},{224... | collective-permute-start | bytes 503816 | tf_op jit(solution)/shard_map/ppermute | solution.py:550
  42.5 8.8 %collective-permute-start.10 = (f32[328,128]{1,0:T(8,128)S(1)}, f32[328,128]{1,0:T(8,128)S(1)}, u32[]{:S(2)}, u32[]{:S(2)}) collective-permute-start(f32[328,128]{1,0:T(8,128)S(1)} %get-tuple-element.57), channel_id=1, source_target_pairs={{32,0},{64,32},{96,64},{128,96},{160,128},{192,160},{224,192},{0,2... | collective-permute-start | bytes 503816 | tf_op jit(solution)/shard_map/ppermute | solution.py:551
  51.3 3.2 %copy-start = (f32[4,80]{1,0:T(4,128)}, f32[4,80]{1,0:T(4,128)S(1)}, u32[]{:S(2)}) copy-start(f32[4,80]{1,0:T(4,128)S(1)} %broadcast_multiply_fusion) | copy-start | bytes 3844
  54.6 7.2 %collective-permute-start.13 = (f32[144,128]{1,0:T(8,128)S(1)}, f32[144,128]{1,0:T(8,128)S(1)}, u32[]{:S(2)}, u32[]{:S(2)}) collective-permute-start(f32[144,128]{1,0:T(8,128)S(1)} %get-tuple-element.69), channel_id=1, source_target_pairs={{0,2},{1,3},{2,0},{3,1},{4,6},{5,7},{6,4},{7,5},{8,10},{9,11},{10,... | collective-permute-start | bytes 221192 | tf_op jit(solution)/shard_map/ppermute | solution.py:523
  56.3 8.2 %collective-permute-start.11 = (f32[144,128]{1,0:T(8,128)S(1)}, f32[144,128]{1,0:T(8,128)S(1)}, u32[]{:S(2)}, u32[]{:S(2)}) collective-permute-start(f32[144,128]{1,0:T(8,128)S(1)} %get-tuple-element.62), channel_id=1, source_target_pairs={{0,3},{1,2},{2,1},{3,0},{4,7},{5,6},{6,5},{7,4},{8,11},{9,10},{10,... | collective-permute-start | bytes 221192 | tf_op jit(solution)/shard_map/ppermute | solution.py:523
  61.3 3.1 %collective-permute-start.12 = (f32[144,128]{1,0:T(8,128)S(1)}, f32[144,128]{1,0:T(8,128)S(1)}, u32[]{:S(2)}, u32[]{:S(2)}) collective-permute-start(f32[144,128]{1,0:T(8,128)S(1)} %get-tuple-element.63), channel_id=1, source_target_pairs={{0,1},{1,0},{2,3},{3,2},{4,5},{5,4},{6,7},{7,6},{8,9},{9,8},{10,11... | collective-permute-start | bytes 221192 | tf_op jit(solution)/shard_map/ppermute | solution.py:523

commit v4 on v3

--- a/solution.py
+++ b/solution.py
@@ -316,9 +316,11 @@
         for piece in range(pieces):
             copy(part, piece).start()
     coefficients = c_ref[...]
+    places = [iota((8, COLS), 0) == (me ^ member) for member in range(GROUPS)]
+    chosen = jnp.concatenate([jnp.where(place, 1.0, 0.0) for place in places], axis=1)
+    spread = exact_dot(coefficients, chosen, ((0,), (0,)))
     for member in range(GROUPS):
-        chosen = jnp.where(iota((8, COLS), 0) == (me ^ member), 1.0, 0.0)
-        b_ref[RITZ * member : RITZ * (member + 1), :] = exact_dot(coefficients, chosen, ((0,), (0,)))
+        b_ref[RITZ * member : RITZ * (member + 1), :] = spread[:, COLS * member : COLS * (member + 1)]
     swap = jnp.where(iota((8, 8), 1) == (me ^ iota((8, 8), 0)), 1.0, 0.0)
     ordered = exact_dot(swap, coefficients, ((1,), (0,)))
     parts, corners = edge_parts(above_ref, below_ref, left_ref, right_ref)
@@ -372,6 +374,7 @@
     coarse = iota((2 * COLS, 3 * COLS), 0)
     fine = iota((2 * COLS, 3 * COLS), 1)
     coarse = jnp.where(coarse == COLS + 2, 0, jnp.where(coarse == COLS + 3, COLS - 1, coarse))
+    a_ref[MAIN + 8 :, :] = jnp.zeros((BLOCK - MAIN - 8, 2 * COLS), F32)
     z_ref[...] = tent_weights(coarse, fine).astype(F32).astype(BF16)
     row = iota((8, COLS), 0)
     keep = jnp.where(row < DEPTH, *has_rows())
@@ -400,8 +403,8 @@
         corners = pltpu.roll(turned[:8], COLS - 4, 1)
         a_ref[:MAIN, :COLS] = e2_ref[group, :, :COLS] + r_ref[:MAIN, :]
         a_ref[:MAIN, COLS:] = e2_ref[group, :, COLS:] + jnp.where(outer_lanes, turned, 0.0)
-        a_ref[MAIN:, :COLS] = (h2_ref[group, :, :COLS] + r_ref[MAIN : MAIN + 8, :]) * keep
-        a_ref[MAIN:, COLS:] = (h2_ref[group, :, COLS:] + jnp.where(outer_lanes[:8], corners, 0.0)) * keep
+        a_ref[MAIN : MAIN + 8, :COLS] = (h2_ref[group, :, :COLS] + r_ref[MAIN : MAIN + 8, :]) * keep
+        a_ref[MAIN : MAIN + 8, COLS:] = (h2_ref[group, :, COLS:] + jnp.where(outer_lanes[:8], corners, 0.0)) * keep
         f_ref[...] = dot_split(a_ref[...], z_ref[...])
         for level in range(DEPTH):
             center = f_ref[ROWS * level : ROWS * (level + 1), :]
@@ -502,8 +505,8 @@
 
 def prolong(slots, returned, main, edge, left, right, early=None):
     scratch = [
-        pltpu.VMEM((MAIN + 8, 2 * COLS), F32),
-        pltpu.VMEM((MAIN + 8, 3 * COLS), F32),
+        pltpu.VMEM((BLOCK, 2 * COLS), F32),
+        pltpu.VMEM((BLOCK, 3 * COLS), F32),
         pltpu.VMEM((2 * COLS, 3 * COLS), BF16),
     ]
     stage = (2, 3, DEPTH, 3 * ROWS, COLS)

time: 66.4 us -> 66.5 us (level)
  no operation moved by 1% of the time
where the time goes in v4:
time: 66.5 us; the launch traced here: 66.3 us
  starting transfers between devices  33.9 us (51%)
  waiting for transfers between devices  16.8 us (25%)
  Pallas kernels  14 us (21%)
  between operations  0.78 us (1%)
  local copies, waits for them, and re-layouts  0.68 us (1%)
    ppermute x6, starting transfers between devices, exchange_members(): lax.ppermute(blocks[shift], 'mem', [(i, i ^ shift) for i in range(size)])  11.5 us
    all_to_all x1, starting transfers between devices, exchange_sum(): return jnp.sum(lax.all_to_all(copies, axes, 0, 0, tiled=True), axis=0)  7.74 us
    all_to_all x1, waiting for transfers between devices, exchange_sum(): return jnp.sum(lax.all_to_all(copies, axes, 0, 0, tiled=True), axis=0)  7.06 us
    ppermute x6, waiting for transfers between devices, exchange_members(): lax.ppermute(blocks[shift], 'mem', [(i, i ^ shift) for i in range(size)])  6.32 us
    ppermute x2, starting transfers between devices, per_device(): below = lax.ppermute(up, 'lat', under)  5.69 us
    ppermute x2, starting transfers between devices, per_device(): above = lax.ppermute(down, 'lat', over)  3.63 us
    ppermute x2, waiting for transfers between devices, per_device(): lax.ppermute(partial, 'mem', [(i, i ^ shift) for i in range(4)])  3.43 us
    pallas_call x1, Pallas kernels, update(): call(update_kernel, 'update', [VMEM, HBM] + [VMEM] * 4, outs, scratch)  3.17 us
  transfers between devices with their start and end apart: 15, of which 6 were waited for; matrix products, arithmetic and copies ran while one was open for 0% of the time, Pallas kernels for 8%

profile of v4, /device:TPU:1, one launch (start us, length us, event | category | flops | bytes accessed | tf_op | source)
XLA Modules:
  0.0 66.3 jit_solution(14022112695770197469)
XLA Ops:
  0.6 1.7 %edges.1 = (f32[3,16,96,128]{3,2,1,0:T(8,128)S(1)}, f32[96,128]{1,0:T(8,128)S(1)}, f32[96,128]{1,0:T(8,128)S(1)}) custom-call(f32[16,96,384]{2,1,0:T(8,128)} %bitcast.6), custom_call_target="tpu_custom_call" | custom-call | tf_op jit(solution)/shard_map/edges/pallas_call | solution.py:456
  2.4 2.5 %collective-permute-start = (f32[96,128]{1,0:T(8,128)S(1)}, f32[96,128]{1,0:T(8,128)S(1)}, u32[]{:S(2)}, u32[]{:S(2)}) collective-permute-start(f32[96,128]{1,0:T(8,128)S(1)} %get-tuple-element.36), channel_id=1, source_target_pairs={{0,32},{32,64},{64,96},{96,128},{128,160},{160,192},{192,224},{224... | collective-permute-start | bytes 147464 | tf_op jit(solution)/shard_map/ppermute | solution.py:543
  4.9 4.0 %collective-permute-start.1 = (f32[96,128]{1,0:T(8,128)S(1)}, f32[96,128]{1,0:T(8,128)S(1)}, u32[]{:S(2)}, u32[]{:S(2)}) collective-permute-start(f32[96,128]{1,0:T(8,128)S(1)} %get-tuple-element.37), channel_id=1, source_target_pairs={{32,0},{64,32},{96,64},{128,96},{160,128},{192,160},{224,192},{0,2... | collective-permute-start | bytes 147464 | tf_op jit(solution)/shard_map/ppermute | solution.py:544
  8.9 3.2 %restrict.1 = (f32[10240,128]{1,0:T(8,128)S(1)}, f32[4,128,256]{2,1,0:T(8,128)S(1)}, f32[4,8,256]{2,1,0:T(8,128)S(1)}, f32[80,128]{1,0:T(8,128)S(1)}, f32[80,128...) custom-call(f32[3,16,96,128]{3,2,1,0:T(8,128)S(1)} %get-tuple-element.38.f_ref, f32[10240,128]{1,0:T(8,128)} %bitcast.4), custom_call_target="tpu_custom_call" | custom-call | tf_op jit(solution)/shard_map/restrict/pallas_call | solution.py:470
  12.1 0.0 collective-permute-done.above_ref
  12.1 0.5 sides.1
  12.6 1.4 %collective-permute-start.2 = (f32[96,128]{1,0:T(8,128)S(1)}, f32[96,128]{1,0:T(8,128)S(1)}, u32[]{:S(2)}, u32[]{:S(2)}) collective-permute-start(f32[96,128]{1,0:T(8,128)S(1)} %get-tuple-element.44), channel_id=1, source_target_pairs={{0,4},{4,8},{8,12},{12,16},{16,20},{20,24},{24,28},{28,0},{1,5},{5... | collective-permute-start | bytes 147464 | tf_op jit(solution)/shard_map/ppermute | solution.py:548
  14.0 2.3 %collective-permute-start.3 = (f32[96,128]{1,0:T(8,128)S(1)}, f32[96,128]{1,0:T(8,128)S(1)}, u32[]{:S(2)}, u32[]{:S(2)}) collective-permute-start(f32[96,128]{1,0:T(8,128)S(1)} %get-tuple-element.45), channel_id=1, source_target_pairs={{4,0},{8,4},{12,8},{16,12},{20,16},{24,20},{28,24},{0,28},{5,1},{9... | collective-permute-start | bytes 147464 | tf_op jit(solution)/shard_map/ppermute | solution.py:547
  16.3 2.9 %collective-permute-start.4 = (f32[136,128]{1,0:T(8,128)S(1)}, f32[136,128]{1,0:T(8,128)S(1)}, u32[]{:S(2)}, u32[]{:S(2)}) collective-permute-start(f32[136,128]{1,0:T(8,128)S(1)} %get-tuple-element.48), channel_id=1, source_target_pairs={{0,2},{1,3},{2,0},{3,1},{4,6},{5,7},{6,4},{7,5},{8,10},{9,11},{10,... | collective-permute-start | bytes 208904 | tf_op jit(solution)/shard_map/ppermute | solution.py:526
  19.2 1.8 %collective-permute-start.5 = (f32[136,128]{1,0:T(8,128)S(1)}, f32[136,128]{1,0:T(8,128)S(1)}, u32[]{:S(2)}, u32[]{:S(2)}) collective-permute-start(f32[136,128]{1,0:T(8,128)S(1)} %get-tuple-element.49), channel_id=1, source_target_pairs={{0,1},{1,0},{2,3},{3,2},{4,5},{5,4},{6,7},{7,6},{8,9},{9,8},{10,11... | collective-permute-start | bytes 208904 | tf_op jit(solution)/shard_map/ppermute | solution.py:526
  21.0 0.1 collective-permute-done.4.c2_ref
  21.1 1.1 %near.1.near_ref = f32[2,80]{1,0:T(2,128)S(1)} custom-call(f32[10240,128]{1,0:T(8,128)S(1)} %get-tuple-element.46.v_ref, f32[136,128]{1,0:T(8,128)S(1)} %get-tuple-element.47.c0_ref, f32[136,128]{1,0:T(8,128)S(1)} %collective-permute-done.4.c2_ref, f32[96,128]{1,0:T(8,128)S(1)} %collective-permute-done.2.left_ref, f32[96,128]{1,0:T(8,128)S(1)} %collective-permute-done.3.right_ref), custom_call_target="tpu_custom_call" | custom-call | tf_op jit(solution)/shard_map/near/pallas_call | solution.py:484
  22.2 4.1 %collective-permute-done.6.c3_ref = f32[136,128]{1,0:T(8,128)S(1)} collective-permute-done((f32[136,128]{1,0:T(8,128)S(1)}, f32[136,128]{1,0:T(8,128)S(1)}, u32[]{:S(2)}, u32[]{:S(2)}) %collective-permute-start.6) | collective-permute-done | bytes 69664 | tf_op jit(solution)/shard_map/ppermute | solution.py:526
  26.3 0.5 bands.1
  26.8 1.1 %far.1 = f32[4,80]{1,0:T(4,128)S(1)} custom-call(f32[2,80]{1,0:T(2,128)S(1)} %near.1.near_ref, f32[10240,128]{1,0:T(8,128)S(1)} %get-tuple-element.46.v_ref, f32[136,128]{1,0:T(8,128)S(1)} %collective-permute-done.6.c3_ref, f32[136,128]{1,0:T(8,128)S(1)} %collective-permute-done.5.c1_ref, f32[96,128]{1,0:T(8,128)S(1)} %collective-permute-done.2.left_ref, ...), custom_call_target="tpu_custom_call" | custom-call | tf_op jit(solution)/shard_map/far/pallas_call | solution.py:489
  27.9 0.1 collective-permute-start.7
  28.0 1.1 %collective-permute-done.7 = f32[4,80]{1,0:T(4,128)S(1)} collective-permute-done((f32[4,80]{1,0:T(4,128)S(1)}, f32[4,80]{1,0:T(4,128)S(1)}, u32[]{:S(2)}, u32[]{:S(2)}) %collective-permute-start.7) | collective-permute-done | bytes 1312 | tf_op jit(solution)/shard_map/ppermute | solution.py:561
  29.1 1.6 %collective-permute-start.8 = (f32[4,80]{1,0:T(4,128)S(1)}, f32[4,80]{1,0:T(4,128)S(1)}, u32[]{:S(2)}, u32[]{:S(2)}) collective-permute-start(f32[4,80]{1,0:T(4,128)S(1)} %add.7), channel_id=1, source_target_pairs={{0,2},{1,3},{2,0},{3,1},{4,6},{5,7},{6,4},{7,5},{8,10},{9,11},{10,... | collective-permute-start | bytes 3848 | tf_op jit(solution)/shard_map/ppermute | solution.py:561
  30.7 2.3 %collective-permute-done.8 = f32[4,80]{1,0:T(4,128)S(1)} collective-permute-done((f32[4,80]{1,0:T(4,128)S(1)}, f32[4,80]{1,0:T(4,128)S(1)}, u32[]{:S(2)}, u32[]{:S(2)}) %collective-permute-start.8) | collective-permute-done | bytes 1312 | tf_op jit(solution)/shard_map/ppermute | solution.py:561
  33.0 0.7 %broadcast_in_dim.4 = f32[64,4,80]{2,1,0:T(4,128)} broadcast(f32[4,80]{1,0:T(4,128)S(1)} %add.8), dimensions={1,2} | broadcast | bytes 83200 | tf_op jit(solution)/shard_map/broadcast_in_dim | solution.py:532
  33.7 7.7 %all-to-all-start = ((f32[64,4,80]{2,1,0:T(4,128)}), f32[64,4,80]{2,1,0:T(4,128)S(1)}, u32[]{:S(2)}, u32[]{:S(2)}) async-start(f32[64,4,80]{2,1,0:T(4,128)} %broadcast_in_dim.4), calls=%async_computation | async-start | bytes 262144 | tf_op jit(solution)/shard_map/all_to_all | solution.py:533
  41.4 1.1 %collective-permute-start.9 = (f32[328,128]{1,0:T(8,128)S(1)}, f32[328,128]{1,0:T(8,128)S(1)}, u32[]{:S(2)}, u32[]{:S(2)}) collective-permute-start(f32[328,128]{1,0:T(8,128)S(1)} %get-tuple-element.56), channel_id=1, source_target_pairs={{0,32},{32,64},{64,96},{96,128},{128,160},{160,192},{192,224},{224... | collective-permute-start | bytes 503816 | tf_op jit(solution)/shard_map/ppermute | solution.py:553
  42.5 1.7 %collective-permute-start.10 = (f32[328,128]{1,0:T(8,128)S(1)}, f32[328,128]{1,0:T(8,128)S(1)}, u32[]{:S(2)}, u32[]{:S(2)}) collective-permute-start(f32[328,128]{1,0:T(8,128)S(1)} %get-tuple-element.57), channel_id=1, source_target_pairs={{32,0},{64,32},{96,64},{128,96},{160,128},{192,160},{224,192},{0,2... | collective-permute-start | bytes 503816 | tf_op jit(solution)/shard_map/ppermute | solution.py:554
  44.2 7.1 %all-to-all-done = f32[64,4,80]{2,1,0:T(4,128)S(1)} async-done(((f32[64,4,80]{2,1,0:T(4,128)}), f32[64,4,80]{2,1,0:T(4,128)S(1)}, u32[]{:S(2)}, u32[]{:S(2)}) %all-to-all-start) | async-done | bytes 81952 | tf_op jit(solution)/shard_map/all_to_all | solution.py:533
  51.3 0.1 reduce_sum.9
  51.4 3.2 %update.1 = (f32[80,2,64,128]{3,2,1,0:T(8,128)S(1)}, f32[320,128]{1,0:T(8,128)S(1)}, f32[16,128]{1,0:T(8,128)S(1)}, f32[144,128]{1,0:T(8,128)S(1)}, f32[144,128]{1,0:T(8,128)S(1)}, /*index=5*/f32[144,128]{1,0:T(8,128)S(1)}) custom-call(f32[8,80]{1,0:T(8,128)S(1)} %pad_maximum_fusion.c_ref, f32[80,2,64,128]{3,2,1,0:T(8,128)} %bitcast.5, ...), custom_call_target="tpu_custom_call" | custom-call | tf_op jit(solution)/shard_map/update/pallas_call | solution.py:497
  54.6 1.7 %collective-permute-start.13 = (f32[144,128]{1,0:T(8,128)S(1)}, f32[144,128]{1,0:T(8,128)S(1)}, u32[]{:S(2)}, u32[]{:S(2)}) collective-permute-start(f32[144,128]{1,0:T(8,128)S(1)} %get-tuple-element.69), channel_id=1, source_target_pairs={{0,2},{1,3},{2,0},{3,1},{4,6},{5,7},{6,4},{7,5},{8,10},{9,11},{10,... | collective-permute-start | bytes 221192 | tf_op jit(solution)/shard_map/ppermute | solution.py:526
  56.3 5.1 %collective-permute-start.11 = (f32[144,128]{1,0:T(8,128)S(1)}, f32[144,128]{1,0:T(8,128)S(1)}, u32[]{:S(2)}, u32[]{:S(2)}) collective-permute-start(f32[144,128]{1,0:T(8,128)S(1)} %get-tuple-element.62), channel_id=1, source_target_pairs={{0,3},{1,2},{2,1},{3,0},{4,7},{5,6},{6,5},{7,4},{8,11},{9,10},{10,... | collective-permute-start | bytes 221192 | tf_op jit(solution)/shard_map/ppermute | solution.py:526
  61.3 0.4 own.1.ra_ref
  61.8 0.5 prolong_early.1.refs_0_
  62.3 2.1 %collective-permute-done.11.ra_ref = f32[144,128]{1,0:T(8,128)S(1)} collective-permute-done((f32[144,128]{1,0:T(8,128)S(1)}, f32[144,128]{1,0:T(8,128)S(1)}, u32[]{:S(2)}, u32[]{:S(2)}) %collective-permute-start.11) | collective-permute-done | bytes 73760 | tf_op jit(solution)/shard_map/ppermute | solution.py:526
  64.5 1.8 %prolong_late.1 = f32[16,96,384]{2,1,0:T(8,128)} custom-call(f32[144,128]{1,0:T(8,128)S(1)} %collective-permute-done.11.ra_ref, f32[144,128]{1,0:T(8,128)S(1)} %collective-permute-done.12.rb_ref, f32[4,128,256]{2,1,0:T(8,128)S(1)} %get-tuple-element.64.e2_ref, f32[4,8,256]{2,1,0:T(8,128)S(1)} %get-tuple-element.65.h2_ref, ...), custom_call_target="tpu_custom_call" | custom-call | tf_op jit(solution)/shard_map/prolong_late/pallas_call | solution.py:520
  (19 shorter events, 0.1 us)
Async XLA Ops:
  2.4 9.7 %collective-permute-start = (f32[96,128]{1,0:T(8,128)S(1)}, f32[96,128]{1,0:T(8,128)S(1)}, u32[]{:S(2)}, u32[]{:S(2)}) collective-permute-start(f32[96,128]{1,0:T(8,128)S(1)} %get-tuple-element.36), channel_id=1, source_target_pairs={{0,32},{32,64},{64,96},{96,128},{128,160},{160,192},{192,224},{224... | collective-permute-start | bytes 147464 | tf_op jit(solution)/shard_map/ppermute | solution.py:543
  4.9 7.2 %collective-permute-start.1 = (f32[96,128]{1,0:T(8,128)S(1)}, f32[96,128]{1,0:T(8,128)S(1)}, u32[]{:S(2)}, u32[]{:S(2)}) collective-permute-start(f32[96,128]{1,0:T(8,128)S(1)} %get-tuple-element.37), channel_id=1, source_target_pairs={{32,0},{64,32},{96,64},{128,96},{160,128},{192,160},{224,192},{0,2... | collective-permute-start | bytes 147464 | tf_op jit(solution)/shard_map/ppermute | solution.py:544
  8.9 12.0 %copy-start.1 = (f32[80]{0:T(128)S(1)}, f32[80]{0:T(128)}, u32[]{:S(2)}) copy-start(f32[80]{0:T(128)} %param.5) | copy-start | bytes 964
  12.6 8.4 %collective-permute-start.2 = (f32[96,128]{1,0:T(8,128)S(1)}, f32[96,128]{1,0:T(8,128)S(1)}, u32[]{:S(2)}, u32[]{:S(2)}) collective-permute-start(f32[96,128]{1,0:T(8,128)S(1)} %get-tuple-element.44), channel_id=1, source_target_pairs={{0,4},{4,8},{8,12},{12,16},{16,20},{20,24},{24,28},{28,0},{1,5},{5... | collective-permute-start | bytes 147464 | tf_op jit(solution)/shard_map/ppermute | solution.py:548
  14.0 7.0 %collective-permute-start.3 = (f32[96,128]{1,0:T(8,128)S(1)}, f32[96,128]{1,0:T(8,128)S(1)}, u32[]{:S(2)}, u32[]{:S(2)}) collective-permute-start(f32[96,128]{1,0:T(8,128)S(1)} %get-tuple-element.45), channel_id=1, source_target_pairs={{4,0},{8,4},{12,8},{16,12},{20,16},{24,20},{28,24},{0,28},{5,1},{9... | collective-permute-start | bytes 147464 | tf_op jit(solution)/shard_map/ppermute | solution.py:547
  16.3 4.8 %collective-permute-start.4 = (f32[136,128]{1,0:T(8,128)S(1)}, f32[136,128]{1,0:T(8,128)S(1)}, u32[]{:S(2)}, u32[]{:S(2)}) collective-permute-start(f32[136,128]{1,0:T(8,128)S(1)} %get-tuple-element.48), channel_id=1, source_target_pairs={{0,2},{1,3},{2,0},{3,1},{4,6},{5,7},{6,4},{7,5},{8,10},{9,11},{10,... | collective-permute-start | bytes 208904 | tf_op jit(solution)/shard_map/ppermute | solution.py:526
  19.2 3.0 %collective-permute-start.5 = (f32[136,128]{1,0:T(8,128)S(1)}, f32[136,128]{1,0:T(8,128)S(1)}, u32[]{:S(2)}, u32[]{:S(2)}) collective-permute-start(f32[136,128]{1,0:T(8,128)S(1)} %get-tuple-element.49), channel_id=1, source_target_pairs={{0,1},{1,0},{2,3},{3,2},{4,5},{5,4},{6,7},{7,6},{8,9},{9,8},{10,11... | collective-permute-start | bytes 208904 | tf_op jit(solution)/shard_map/ppermute | solution.py:526
  21.0 5.3 %collective-permute-start.6 = (f32[136,128]{1,0:T(8,128)S(1)}, f32[136,128]{1,0:T(8,128)S(1)}, u32[]{:S(2)}, u32[]{:S(2)}) collective-permute-start(f32[136,128]{1,0:T(8,128)S(1)} %get-tuple-element.50), channel_id=1, source_target_pairs={{0,3},{1,2},{2,1},{3,0},{4,7},{5,6},{6,5},{7,4},{8,11},{9,10},{10,... | collective-permute-start | bytes 208904 | tf_op jit(solution)/shard_map/ppermute | solution.py:526
  27.9 1.2 %collective-permute-start.7 = (f32[4,80]{1,0:T(4,128)S(1)}, f32[4,80]{1,0:T(4,128)S(1)}, u32[]{:S(2)}, u32[]{:S(2)}) collective-permute-start(f32[4,80]{1,0:T(4,128)S(1)} %far.1), channel_id=1, source_target_pairs={{0,1},{1,0},{2,3},{3,2},{4,5},{5,4},{6,7},{7,6},{8,9},{9,8},{10,11... | collective-permute-start | bytes 3848 | tf_op jit(solution)/shard_map/ppermute | solution.py:561
  29.1 3.9 %collective-permute-start.8 = (f32[4,80]{1,0:T(4,128)S(1)}, f32[4,80]{1,0:T(4,128)S(1)}, u32[]{:S(2)}, u32[]{:S(2)}) collective-permute-start(f32[4,80]{1,0:T(4,128)S(1)} %add.7), channel_id=1, source_target_pairs={{0,2},{1,3},{2,0},{3,1},{4,6},{5,7},{6,4},{7,5},{8,10},{9,11},{10,... | collective-permute-start | bytes 3848 | tf_op jit(solution)/shard_map/ppermute | solution.py:561
  33.7 17.6 %all-to-all-start = ((f32[64,4,80]{2,1,0:T(4,128)}), f32[64,4,80]{2,1,0:T(4,128)S(1)}, u32[]{:S(2)}, u32[]{:S(2)}) async-start(f32[64,4,80]{2,1,0:T(4,128)} %broadcast_in_dim.4), calls=%async_computation | async-start | bytes 262144 | tf_op jit(solution)/shard_map/all_to_all | solution.py:533
  41.4 9.9 %collective-permute-start.9 = (f32[328,128]{1,0:T(8,128)S(1)}, f32[328,128]{1,0:T(8,128)S(1)}, u32[]{:S(2)}, u32[]{:S(2)}) collective-permute-start(f32[328,128]{1,0:T(8,128)S(1)} %get-tuple-element.56), channel_id=1, source_target_pairs={{0,32},{32,64},{64,96},{96,128},{128,160},{160,192},{192,224},{224... | collective-permute-start | bytes 503816 | tf_op jit(solution)/shard_map/ppermute | solution.py:553
  42.5 8.8 %collective-permute-start.10 = (f32[328,128]{1,0:T(8,128)S(1)}, f32[328,128]{1,0:T(8,128)S(1)}, u32[]{:S(2)}, u32[]{:S(2)}) collective-permute-start(f32[328,128]{1,0:T(8,128)S(1)} %get-tuple-element.57), channel_id=1, source_target_pairs={{32,0},{64,32},{96,64},{128,96},{160,128},{192,160},{224,192},{0,2... | collective-permute-start | bytes 503816 | tf_op jit(solution)/shard_map/ppermute | solution.py:554
  51.3 3.2 %copy-start = (f32[4,80]{1,0:T(4,128)}, f32[4,80]{1,0:T(4,128)S(1)}, u32[]{:S(2)}) copy-start(f32[4,80]{1,0:T(4,128)S(1)} %broadcast_multiply_fusion) | copy-start | bytes 3844
  54.6 7.2 %collective-permute-start.13 = (f32[144,128]{1,0:T(8,128)S(1)}, f32[144,128]{1,0:T(8,128)S(1)}, u32[]{:S(2)}, u32[]{:S(2)}) collective-permute-start(f32[144,128]{1,0:T(8,128)S(1)} %get-tuple-element.69), channel_id=1, source_target_pairs={{0,2},{1,3},{2,0},{3,1},{4,6},{5,7},{6,4},{7,5},{8,10},{9,11},{10,... | collective-permute-start | bytes 221192 | tf_op jit(solution)/shard_map/ppermute | solution.py:526
  56.3 8.2 %collective-permute-start.11 = (f32[144,128]{1,0:T(8,128)S(1)}, f32[144,128]{1,0:T(8,128)S(1)}, u32[]{:S(2)}, u32[]{:S(2)}) collective-permute-start(f32[144,128]{1,0:T(8,128)S(1)} %get-tuple-element.62), channel_id=1, source_target_pairs={{0,3},{1,2},{2,1},{3,0},{4,7},{5,6},{6,5},{7,4},{8,11},{9,10},{10,... | collective-permute-start | bytes 221192 | tf_op jit(solution)/shard_map/ppermute | solution.py:526
  61.3 3.1 %collective-permute-start.12 = (f32[144,128]{1,0:T(8,128)S(1)}, f32[144,128]{1,0:T(8,128)S(1)}, u32[]{:S(2)}, u32[]{:S(2)}) collective-permute-start(f32[144,128]{1,0:T(8,128)S(1)} %get-tuple-element.63), channel_id=1, source_target_pairs={{0,1},{1,0},{2,3},{3,2},{4,5},{5,4},{6,7},{7,6},{8,9},{9,8},{10,11... | collective-permute-start | bytes 221192 | tf_op jit(solution)/shard_map/ppermute | solution.py:526

commit v5 on v4

--- a/solution.py
+++ b/solution.py
@@ -23,6 +23,7 @@
 SIDE = RITZ + 4 * GROUPS
 CHUNK = 8
 PIECE = 16
+KEPT = 24
 EARLY = (0, 2)
 LATE = (3, 1)
 MIB = 1024 * 1024
@@ -280,36 +281,40 @@
     )
 
 
-def weighted_sums(v_ref, b_ref, slots, prepare):
+def weighted_sums(kept_ref, rest_ref, b_ref, slots, prepare):
     half = MAIN // 2
     results = []
     for part in range(2):
 
-        def body(index, sums, part=part):
-            prepare(part, index)
+        def body(index, sums, ref, first, part=part):
+            if first:
+                prepare(part, index)
             for offset in range(CHUNK):
                 k = index * CHUNK + offset
-                vector = v_ref[k, part]
+                vector = ref[k, part]
                 sums = [
-                    value + b_ref[pl.ds(RITZ * member + k, 1), :] * vector for value, member in zip(sums, slots)
+                    value + b_ref[pl.ds(RITZ * member + first + k, 1), :] * vector
+                    for value, member in zip(sums, slots)
                 ]
             return tuple(sums)
 
-        zeros = tuple(jnp.zeros((half, COLS), F32) for _ in slots)
-        results.append(lax.fori_loop(0, RITZ // CHUNK, body, zeros))
+        sums = tuple(jnp.zeros((half, COLS), F32) for _ in slots)
+        sums = lax.fori_loop(0, KEPT // CHUNK, functools.partial(body, ref=kept_ref, first=0), sums)
+        rest = functools.partial(body, ref=rest_ref, first=KEPT)
+        results.append(lax.fori_loop(0, (RITZ - KEPT) // CHUNK, rest, sums))
     return results
 
 
 def update_kernel(
-    c_ref, v_hbm_ref, above_ref, below_ref, left_ref, right_ref,
+    c_ref, kept_ref, v_hbm_ref, above_ref, below_ref, left_ref, right_ref,
     v_ref, b_ref, edge_ref, u1_ref, u2_ref, u3_ref, sem
 ):
     me = member_index()
     outs = (None, u1_ref, u2_ref, u3_ref)
-    pieces = RITZ // CHUNK
+    pieces = (RITZ - KEPT) // CHUNK
 
     def copy(part, piece):
-        source = v_hbm_ref.at[pl.ds(piece * CHUNK, CHUNK), part]
+        source = v_hbm_ref.at[pl.ds(KEPT + piece * CHUNK, CHUNK), part]
         return pltpu.make_async_copy(source, v_ref.at[pl.ds(piece * CHUNK, CHUNK), part], sem.at[part, piece])
 
     for part in range(2):
@@ -340,14 +345,20 @@
         copy(part, index).wait()
 
     half = MAIN // 2
-    for part, sums in enumerate(weighted_sums(v_ref, b_ref, (1, 2, 3), prepare)):
+    for part, sums in enumerate(weighted_sums(kept_ref, v_ref, b_ref, (1, 2, 3), prepare)):
         for member, value in zip((1, 2, 3), sums):
             outs[member][half * part : half * (part + 1), :] = value
 
 
-def own_kernel(v_ref, b_ref, edge_ref, u0_ref):
+def keep_kernel(v_ref, kept_ref, sem):
+    copy = pltpu.make_async_copy(v_ref.at[pl.ds(0, KEPT)], kept_ref, sem.at[0])
+    copy.start()
+    copy.wait()
+
+
+def own_kernel(kept_ref, v_ref, b_ref, edge_ref, u0_ref):
     half = MAIN // 2
-    for part, sums in enumerate(weighted_sums(v_ref, b_ref, (0,), lambda part, index: None)):
+    for part, sums in enumerate(weighted_sums(kept_ref, v_ref, b_ref, (0,), lambda part, index: None)):
         u0_ref[half * part : half * (part + 1), :] = sums[0]
     u0_ref[MAIN:, :] = edge_ref[...]
 
@@ -489,18 +500,24 @@
     return call(far_kernel, "far", [VMEM] * 6, outs, scratch)(sums, held, *blocks, *columns)[0]
 
 
-def update(coefficients, ritz_vectors, messages):
-    outs = [pltpu.VMEM((RITZ, 2, MAIN // 2, COLS), F32), struct(GROUPS * RITZ, COLS), struct(HALO, COLS)]
+def update(coefficients, kept, ritz_vectors, messages):
+    outs = [pltpu.VMEM((RITZ - KEPT, 2, MAIN // 2, COLS), F32), struct(GROUPS * RITZ, COLS), struct(HALO, COLS)]
     outs += [struct(BLOCK, COLS)] * 3
-    scratch = [pltpu.SemaphoreType.DMA((2, RITZ // CHUNK))]
+    scratch = [pltpu.SemaphoreType.DMA((2, (RITZ - KEPT) // CHUNK))]
     doubled = jnp.concatenate([coefficients, coefficients], axis=0)
-    return call(update_kernel, "update", [VMEM, HBM] + [VMEM] * 4, outs, scratch)(
-        doubled, pinned(ritz_vectors.reshape(RITZ, 2, MAIN // 2, COLS)), *messages
+    return call(update_kernel, "update", [VMEM, VMEM, HBM] + [VMEM] * 4, outs, scratch)(
+        doubled, kept, pinned(ritz_vectors.reshape(RITZ, 2, MAIN // 2, COLS)), *messages
     )
 
 
+def keep(ritz_vectors):
+    outs = [pltpu.VMEM((KEPT, 2, MAIN // 2, COLS), F32)]
+    tiles = pinned(ritz_vectors.reshape(RITZ, 2, MAIN // 2, COLS))
+    return call(keep_kernel, "keep", [HBM], outs, [pltpu.SemaphoreType.DMA((1,))])(tiles)[0]
+
+
 def own(*args):
-    return call(own_kernel, "own", [VMEM] * 3, [struct(BLOCK, COLS)], [])(*args)[0]
+    return call(own_kernel, "own", [VMEM] * 4, [struct(BLOCK, COLS)], [])(*args)[0]
 
 
 def prolong(slots, returned, main, edge, left, right, early=None):
@@ -556,14 +573,15 @@
     partial = far(near_sums, held, (spread[3], spread[1]), (left, right))
     cells = GROUPS * DEPTH * ROWS * lats * COLS * lons
     factors = (1.0 / ritz_values - 1.0) * (1.0 / cells)
-    partial, factors = lax.optimization_barrier((partial, factors))
+    partial, factors, stored = lax.optimization_barrier((partial, factors, ritz_vectors))
+    kept = keep(stored)
     for shift in (1, 2):
         partial = partial + lax.ppermute(partial, "mem", [(i, i ^ shift) for i in range(4)])
     coefficients = factors[None, :] * exchange_sum(partial, ("lat", "lon"))
     messages = (above, below, left, right)
-    held, weights, own_edge, *sent = update(coefficients, ritz_vectors, messages)
+    held, weights, own_edge, *sent = update(coefficients, kept, ritz_vectors, messages)
     returned = exchange_members([None] + sent)
-    mine = own(held, weights, own_edge)
+    mine = own(kept, held, weights, own_edge)
     returned = [mine] + returned
     early = prolong(EARLY, [returned[slot] for slot in EARLY], main, edge, left, right)
     output = prolong(LATE, [returned[slot] for slot in LATE], main, edge, left, right, early)

time: 66.5 us -> 66.1 us (level)
  waiting for transfers between devices: 16.8 us -> 15.4 us
  Pallas kernels: 14 us -> 15 us
    all_to_all x1, waiting for transfers between devices: 7.06 us -> 5.64 us  [exchange_sum(): return jnp.sum(lax.all_to_all(copies, axes, 0, 0, tiled=True), axis=0)]
    pallas_call x2 -> x3, Pallas kernels: 3.6 us -> 4.57 us  [the longest x1 2.7 us: update(): call(update_kernel, 'update', [VMEM, VMEM, HBM] + [VMEM] * 4, outs, scratch)]
  transfers between devices with their start and end apart: 15 -> 15, of which waited for: 6 -> 6; matrix products, arithmetic and copies ran while one was open for 0% -> 0% of each run, Pallas kernels for 8% -> 10%
where the time goes in v5:
time: 66.1 us; the launch traced here: 65.8 us
  starting transfers between devices  33.9 us (51%)
  waiting for transfers between devices  15.4 us (23%)
  Pallas kernels  15 us (23%)
  between operations  0.78 us (1%)
  local copies, waits for them, and re-layouts  0.68 us (1%)
    ppermute x6, starting transfers between devices, exchange_members(): lax.ppermute(blocks[shift], 'mem', [(i, i ^ shift) for i in range(size)])  11.5 us
    all_to_all x1, starting transfers between devices, exchange_sum(): return jnp.sum(lax.all_to_all(copies, axes, 0, 0, tiled=True), axis=0)  7.74 us
    ppermute x6, waiting for transfers between devices, exchange_members(): lax.ppermute(blocks[shift], 'mem', [(i, i ^ shift) for i in range(size)])  6.31 us
    ppermute x2, starting transfers between devices, per_device(): below = lax.ppermute(up, 'lat', under)  5.69 us
    all_to_all x1, waiting for transfers between devices, exchange_sum(): return jnp.sum(lax.all_to_all(copies, axes, 0, 0, tiled=True), axis=0)  5.64 us
    ppermute x2, starting transfers between devices, per_device(): above = lax.ppermute(down, 'lat', over)  3.63 us
    ppermute x2, waiting for transfers between devices, per_device(): lax.ppermute(partial, 'mem', [(i, i ^ shift) for i in range(4)])  3.43 us
    pallas_call x1, Pallas kernels, restrict(): call(restrict_kernel, 'restrict', [VMEM, HBM], outs, scratch)(fine, flat)  3.16 us
  transfers between devices with their start and end apart: 15, of which 6 were waited for; matrix products, arithmetic and copies ran while one was open for 0% of the time, Pallas kernels for 10%

profile of v5, /device:TPU:1, one launch (start us, length us, event | category | flops | bytes accessed | tf_op | source)
XLA Modules:
  0.0 65.8 jit_solution(17975496721485021412)
XLA Ops:
  0.6 1.7 %edges.1 = (f32[3,16,96,128]{3,2,1,0:T(8,128)S(1)}, f32[96,128]{1,0:T(8,128)S(1)}, f32[96,128]{1,0:T(8,128)S(1)}) custom-call(f32[16,96,384]{2,1,0:T(8,128)} %bitcast.8), custom_call_target="tpu_custom_call" | custom-call | tf_op jit(solution)/shard_map/edges/pallas_call | solution.py:467
  2.4 2.5 %collective-permute-start = (f32[96,128]{1,0:T(8,128)S(1)}, f32[96,128]{1,0:T(8,128)S(1)}, u32[]{:S(2)}, u32[]{:S(2)}) collective-permute-start(f32[96,128]{1,0:T(8,128)S(1)} %get-tuple-element.37), channel_id=1, source_target_pairs={{0,32},{32,64},{64,96},{96,128},{128,160},{160,192},{192,224},{224... | collective-permute-start | bytes 147464 | tf_op jit(solution)/shard_map/ppermute | solution.py:560
  4.9 4.0 %collective-permute-start.1 = (f32[96,128]{1,0:T(8,128)S(1)}, f32[96,128]{1,0:T(8,128)S(1)}, u32[]{:S(2)}, u32[]{:S(2)}) collective-permute-start(f32[96,128]{1,0:T(8,128)S(1)} %get-tuple-element.38), channel_id=1, source_target_pairs={{32,0},{64,32},{96,64},{128,96},{160,128},{192,160},{224,192},{0,2... | collective-permute-start | bytes 147464 | tf_op jit(solution)/shard_map/ppermute | solution.py:561
  8.9 3.2 %restrict.1 = (f32[10240,128]{1,0:T(8,128)S(1)}, f32[4,128,256]{2,1,0:T(8,128)S(1)}, f32[4,8,256]{2,1,0:T(8,128)S(1)}, f32[80,128]{1,0:T(8,128)S(1)}, f32[80,128...) custom-call(f32[3,16,96,128]{3,2,1,0:T(8,128)S(1)} %get-tuple-element.39.f_ref, f32[10240,128]{1,0:T(8,128)} %bitcast.5), custom_call_target="tpu_custom_call" | custom-call | tf_op jit(solution)/shard_map/restrict/pallas_call | solution.py:481
  12.1 0.5 sides.1
  12.6 1.4 %collective-permute-start.2 = (f32[96,128]{1,0:T(8,128)S(1)}, f32[96,128]{1,0:T(8,128)S(1)}, u32[]{:S(2)}, u32[]{:S(2)}) collective-permute-start(f32[96,128]{1,0:T(8,128)S(1)} %get-tuple-element.45), channel_id=1, source_target_pairs={{0,4},{4,8},{8,12},{12,16},{16,20},{20,24},{24,28},{28,0},{1,5},{5... | collective-permute-start | bytes 147464 | tf_op jit(solution)/shard_map/ppermute | solution.py:565
  14.0 2.3 %collective-permute-start.3 = (f32[96,128]{1,0:T(8,128)S(1)}, f32[96,128]{1,0:T(8,128)S(1)}, u32[]{:S(2)}, u32[]{:S(2)}) collective-permute-start(f32[96,128]{1,0:T(8,128)S(1)} %get-tuple-element.46), channel_id=1, source_target_pairs={{4,0},{8,4},{12,8},{16,12},{20,16},{24,20},{28,24},{0,28},{5,1},{9... | collective-permute-start | bytes 147464 | tf_op jit(solution)/shard_map/ppermute | solution.py:564
  16.3 2.9 %collective-permute-start.4 = (f32[136,128]{1,0:T(8,128)S(1)}, f32[136,128]{1,0:T(8,128)S(1)}, u32[]{:S(2)}, u32[]{:S(2)}) collective-permute-start(f32[136,128]{1,0:T(8,128)S(1)} %get-tuple-element.49), channel_id=1, source_target_pairs={{0,2},{1,3},{2,0},{3,1},{4,6},{5,7},{6,4},{7,5},{8,10},{9,11},{10,... | collective-permute-start | bytes 208904 | tf_op jit(solution)/shard_map/ppermute | solution.py:543
  19.2 1.8 %collective-permute-start.5 = (f32[136,128]{1,0:T(8,128)S(1)}, f32[136,128]{1,0:T(8,128)S(1)}, u32[]{:S(2)}, u32[]{:S(2)}) collective-permute-start(f32[136,128]{1,0:T(8,128)S(1)} %get-tuple-element.50), channel_id=1, source_target_pairs={{0,1},{1,0},{2,3},{3,2},{4,5},{5,4},{6,7},{7,6},{8,9},{9,8},{10,11... | collective-permute-start | bytes 208904 | tf_op jit(solution)/shard_map/ppermute | solution.py:543
  21.0 0.1 collective-permute-done.4.c2_ref
  21.1 1.1 %near.1.near_ref = f32[2,80]{1,0:T(2,128)S(1)} custom-call(f32[10240,128]{1,0:T(8,128)S(1)} %get-tuple-element.47.v_ref, f32[136,128]{1,0:T(8,128)S(1)} %get-tuple-element.48.c0_ref, f32[136,128]{1,0:T(8,128)S(1)} %collective-permute-done.4.c2_ref, f32[96,128]{1,0:T(8,128)S(1)} %collective-permute-done.2.left_ref, f32[96,128]{1,0:T(8,128)S(1)} %collective-permute-done.3.right_ref), custom_call_target="tpu_custom_call" | custom-call | tf_op jit(solution)/shard_map/near/pallas_call | solution.py:495
  22.2 4.1 %collective-permute-done.6.c3_ref = f32[136,128]{1,0:T(8,128)S(1)} collective-permute-done((f32[136,128]{1,0:T(8,128)S(1)}, f32[136,128]{1,0:T(8,128)S(1)}, u32[]{:S(2)}, u32[]{:S(2)}) %collective-permute-start.6) | collective-permute-done | bytes 69664 | tf_op jit(solution)/shard_map/ppermute | solution.py:543
  26.3 0.5 bands.1
  26.8 1.1 %far.1 = f32[4,80]{1,0:T(4,128)S(1)} custom-call(f32[2,80]{1,0:T(2,128)S(1)} %near.1.near_ref, f32[10240,128]{1,0:T(8,128)S(1)} %get-tuple-element.47.v_ref, f32[136,128]{1,0:T(8,128)S(1)} %collective-permute-done.6.c3_ref, f32[136,128]{1,0:T(8,128)S(1)} %collective-permute-done.5.c1_ref, f32[96,128]{1,0:T(8,128)S(1)} %collective-permute-done.2.left_ref, ...), custom_call_target="tpu_custom_call" | custom-call | tf_op jit(solution)/shard_map/far/pallas_call | solution.py:500
  27.9 0.1 collective-permute-start.7
  28.0 1.1 %collective-permute-done.7 = f32[4,80]{1,0:T(4,128)S(1)} collective-permute-done((f32[4,80]{1,0:T(4,128)S(1)}, f32[4,80]{1,0:T(4,128)S(1)}, u32[]{:S(2)}, u32[]{:S(2)}) %collective-permute-start.7) | collective-permute-done | bytes 1312 | tf_op jit(solution)/shard_map/ppermute | solution.py:579
  29.1 1.6 %collective-permute-start.8 = (f32[4,80]{1,0:T(4,128)S(1)}, f32[4,80]{1,0:T(4,128)S(1)}, u32[]{:S(2)}, u32[]{:S(2)}) collective-permute-start(f32[4,80]{1,0:T(4,128)S(1)} %add.7), channel_id=1, source_target_pairs={{0,2},{1,3},{2,0},{3,1},{4,6},{5,7},{6,4},{7,5},{8,10},{9,11},{10,... | collective-permute-start | bytes 3848 | tf_op jit(solution)/shard_map/ppermute | solution.py:579
  30.7 2.3 %collective-permute-done.8 = f32[4,80]{1,0:T(4,128)S(1)} collective-permute-done((f32[4,80]{1,0:T(4,128)S(1)}, f32[4,80]{1,0:T(4,128)S(1)}, u32[]{:S(2)}, u32[]{:S(2)}) %collective-permute-start.8) | collective-permute-done | bytes 1312 | tf_op jit(solution)/shard_map/ppermute | solution.py:579
  33.0 0.7 %broadcast_in_dim.4 = f32[64,4,80]{2,1,0:T(4,128)} broadcast(f32[4,80]{1,0:T(4,128)S(1)} %add.8), dimensions={1,2} | broadcast | bytes 83200 | tf_op jit(solution)/shard_map/broadcast_in_dim | solution.py:549
  33.7 7.7 %all-to-all-start = ((f32[64,4,80]{2,1,0:T(4,128)}), f32[64,4,80]{2,1,0:T(4,128)S(1)}, u32[]{:S(2)}, u32[]{:S(2)}) async-start(f32[64,4,80]{2,1,0:T(4,128)} %broadcast_in_dim.4), calls=%async_computation | async-start | bytes 262144 | tf_op jit(solution)/shard_map/all_to_all | solution.py:550
  41.4 1.1 %collective-permute-start.9 = (f32[328,128]{1,0:T(8,128)S(1)}, f32[328,128]{1,0:T(8,128)S(1)}, u32[]{:S(2)}, u32[]{:S(2)}) collective-permute-start(f32[328,128]{1,0:T(8,128)S(1)} %get-tuple-element.57), channel_id=1, source_target_pairs={{0,32},{32,64},{64,96},{96,128},{128,160},{160,192},{192,224},{224... | collective-permute-start | bytes 503816 | tf_op jit(solution)/shard_map/ppermute | solution.py:570
  42.5 1.7 %collective-permute-start.10 = (f32[328,128]{1,0:T(8,128)S(1)}, f32[328,128]{1,0:T(8,128)S(1)}, u32[]{:S(2)}, u32[]{:S(2)}) collective-permute-start(f32[328,128]{1,0:T(8,128)S(1)} %get-tuple-element.58), channel_id=1, source_target_pairs={{32,0},{64,32},{96,64},{128,96},{160,128},{192,160},{224,192},{0,2... | collective-permute-start | bytes 503816 | tf_op jit(solution)/shard_map/ppermute | solution.py:571
  44.2 1.4 %keep.1.kept_ref = f32[24,2,64,128]{3,2,1,0:T(8,128)S(1)} custom-call(f32[80,2,64,128]{3,2,1,0:T(8,128)} %bitcast.6), custom_call_target="tpu_custom_call" | custom-call | tf_op jit(solution)/shard_map/keep/pallas_call | solution.py:516
  45.6 5.6 %all-to-all-done = f32[64,4,80]{2,1,0:T(4,128)S(1)} async-done(((f32[64,4,80]{2,1,0:T(4,128)}), f32[64,4,80]{2,1,0:T(4,128)S(1)}, u32[]{:S(2)}, u32[]{:S(2)}) %all-to-all-start) | async-done | bytes 81952 | tf_op jit(solution)/shard_map/all_to_all | solution.py:550
  51.3 0.1 reduce_sum.9
  51.4 2.7 %update.1 = (f32[56,2,64,128]{3,2,1,0:T(8,128)S(1)}, f32[320,128]{1,0:T(8,128)S(1)}, f32[16,128]{1,0:T(8,128)S(1)}, f32[144,128]{1,0:T(8,128)S(1)}, f32[144,128]{1,0:T(8,128)S(1)}, /*index=5*/f32[144,128]{1,0:T(8,128)S(1)}) custom-call(f32[8,80]{1,0:T(8,128)S(1)} %pad_maximum_fusion.c_ref, f32[24,2,64,128]{3,2,1,0:T(8,128)S(1)} %keep.1.kept_ref, ...), custom_call_target="tpu_custom_call" | custom-call | tf_op jit(solution)/shard_map/update/pallas_call | solution.py:508
  54.1 1.7 %collective-permute-start.13 = (f32[144,128]{1,0:T(8,128)S(1)}, f32[144,128]{1,0:T(8,128)S(1)}, u32[]{:S(2)}, u32[]{:S(2)}) collective-permute-start(f32[144,128]{1,0:T(8,128)S(1)} %get-tuple-element.71), channel_id=1, source_target_pairs={{0,2},{1,3},{2,0},{3,1},{4,6},{5,7},{6,4},{7,5},{8,10},{9,11},{10,... | collective-permute-start | bytes 221192 | tf_op jit(solution)/shard_map/ppermute | solution.py:543
  55.8 5.1 %collective-permute-start.11 = (f32[144,128]{1,0:T(8,128)S(1)}, f32[144,128]{1,0:T(8,128)S(1)}, u32[]{:S(2)}, u32[]{:S(2)}) collective-permute-start(f32[144,128]{1,0:T(8,128)S(1)} %get-tuple-element.64), channel_id=1, source_target_pairs={{0,3},{1,2},{2,1},{3,0},{4,7},{5,6},{6,5},{7,4},{8,11},{9,10},{10,... | collective-permute-start | bytes 221192 | tf_op jit(solution)/shard_map/ppermute | solution.py:543
  60.9 0.5 own.1.ra_ref
  61.3 0.5 prolong_early.1.refs_0_
  61.9 2.1 %collective-permute-done.11.ra_ref = f32[144,128]{1,0:T(8,128)S(1)} collective-permute-done((f32[144,128]{1,0:T(8,128)S(1)}, f32[144,128]{1,0:T(8,128)S(1)}, u32[]{:S(2)}, u32[]{:S(2)}) %collective-permute-start.11) | collective-permute-done | bytes 73760 | tf_op jit(solution)/shard_map/ppermute | solution.py:543
  64.0 1.8 %prolong_late.1 = f32[16,96,384]{2,1,0:T(8,128)} custom-call(f32[144,128]{1,0:T(8,128)S(1)} %collective-permute-done.11.ra_ref, f32[144,128]{1,0:T(8,128)S(1)} %collective-permute-done.12.rb_ref, f32[4,128,256]{2,1,0:T(8,128)S(1)} %get-tuple-element.66.e2_ref, f32[4,8,256]{2,1,0:T(8,128)S(1)} %get-tuple-element.67.h2_ref, ...), custom_call_target="tpu_custom_call" | custom-call | tf_op jit(solution)/shard_map/prolong_late/pallas_call | solution.py:537
  (20 shorter events, 0.1 us)
Async XLA Ops:
  2.4 9.7 %collective-permute-start = (f32[96,128]{1,0:T(8,128)S(1)}, f32[96,128]{1,0:T(8,128)S(1)}, u32[]{:S(2)}, u32[]{:S(2)}) collective-permute-start(f32[96,128]{1,0:T(8,128)S(1)} %get-tuple-element.37), channel_id=1, source_target_pairs={{0,32},{32,64},{64,96},{96,128},{128,160},{160,192},{192,224},{224... | collective-permute-start | bytes 147464 | tf_op jit(solution)/shard_map/ppermute | solution.py:560
  4.9 7.2 %collective-permute-start.1 = (f32[96,128]{1,0:T(8,128)S(1)}, f32[96,128]{1,0:T(8,128)S(1)}, u32[]{:S(2)}, u32[]{:S(2)}) collective-permute-start(f32[96,128]{1,0:T(8,128)S(1)} %get-tuple-element.38), channel_id=1, source_target_pairs={{32,0},{64,32},{96,64},{128,96},{160,128},{192,160},{224,192},{0,2... | collective-permute-start | bytes 147464 | tf_op jit(solution)/shard_map/ppermute | solution.py:561
  8.9 12.0 %copy-start.1 = (f32[80]{0:T(128)S(1)}, f32[80]{0:T(128)}, u32[]{:S(2)}) copy-start(f32[80]{0:T(128)} %param.5) | copy-start | bytes 964
  12.6 8.4 %collective-permute-start.2 = (f32[96,128]{1,0:T(8,128)S(1)}, f32[96,128]{1,0:T(8,128)S(1)}, u32[]{:S(2)}, u32[]{:S(2)}) collective-permute-start(f32[96,128]{1,0:T(8,128)S(1)} %get-tuple-element.45), channel_id=1, source_target_pairs={{0,4},{4,8},{8,12},{12,16},{16,20},{20,24},{24,28},{28,0},{1,5},{5... | collective-permute-start | bytes 147464 | tf_op jit(solution)/shard_map/ppermute | solution.py:565
  14.0 7.0 %collective-permute-start.3 = (f32[96,128]{1,0:T(8,128)S(1)}, f32[96,128]{1,0:T(8,128)S(1)}, u32[]{:S(2)}, u32[]{:S(2)}) collective-permute-start(f32[96,128]{1,0:T(8,128)S(1)} %get-tuple-element.46), channel_id=1, source_target_pairs={{4,0},{8,4},{12,8},{16,12},{20,16},{24,20},{28,24},{0,28},{5,1},{9... | collective-permute-start | bytes 147464 | tf_op jit(solution)/shard_map/ppermute | solution.py:564
  16.3 4.8 %collective-permute-start.4 = (f32[136,128]{1,0:T(8,128)S(1)}, f32[136,128]{1,0:T(8,128)S(1)}, u32[]{:S(2)}, u32[]{:S(2)}) collective-permute-start(f32[136,128]{1,0:T(8,128)S(1)} %get-tuple-element.49), channel_id=1, source_target_pairs={{0,2},{1,3},{2,0},{3,1},{4,6},{5,7},{6,4},{7,5},{8,10},{9,11},{10,... | collective-permute-start | bytes 208904 | tf_op jit(solution)/shard_map/ppermute | solution.py:543
  19.2 3.0 %collective-permute-start.5 = (f32[136,128]{1,0:T(8,128)S(1)}, f32[136,128]{1,0:T(8,128)S(1)}, u32[]{:S(2)}, u32[]{:S(2)}) collective-permute-start(f32[136,128]{1,0:T(8,128)S(1)} %get-tuple-element.50), channel_id=1, source_target_pairs={{0,1},{1,0},{2,3},{3,2},{4,5},{5,4},{6,7},{7,6},{8,9},{9,8},{10,11... | collective-permute-start | bytes 208904 | tf_op jit(solution)/shard_map/ppermute | solution.py:543
  21.0 5.3 %collective-permute-start.6 = (f32[136,128]{1,0:T(8,128)S(1)}, f32[136,128]{1,0:T(8,128)S(1)}, u32[]{:S(2)}, u32[]{:S(2)}) collective-permute-start(f32[136,128]{1,0:T(8,128)S(1)} %get-tuple-element.51), channel_id=1, source_target_pairs={{0,3},{1,2},{2,1},{3,0},{4,7},{5,6},{6,5},{7,4},{8,11},{9,10},{10,... | collective-permute-start | bytes 208904 | tf_op jit(solution)/shard_map/ppermute | solution.py:543
  27.9 1.2 %collective-permute-start.7 = (f32[4,80]{1,0:T(4,128)S(1)}, f32[4,80]{1,0:T(4,128)S(1)}, u32[]{:S(2)}, u32[]{:S(2)}) collective-permute-start(f32[4,80]{1,0:T(4,128)S(1)} %far.1), channel_id=1, source_target_pairs={{0,1},{1,0},{2,3},{3,2},{4,5},{5,4},{6,7},{7,6},{8,9},{9,8},{10,11... | collective-permute-start | bytes 3848 | tf_op jit(solution)/shard_map/ppermute | solution.py:579
  29.1 3.9 %collective-permute-start.8 = (f32[4,80]{1,0:T(4,128)S(1)}, f32[4,80]{1,0:T(4,128)S(1)}, u32[]{:S(2)}, u32[]{:S(2)}) collective-permute-start(f32[4,80]{1,0:T(4,128)S(1)} %add.7), channel_id=1, source_target_pairs={{0,2},{1,3},{2,0},{3,1},{4,6},{5,7},{6,4},{7,5},{8,10},{9,11},{10,... | collective-permute-start | bytes 3848 | tf_op jit(solution)/shard_map/ppermute | solution.py:579
  33.7 17.6 %all-to-all-start = ((f32[64,4,80]{2,1,0:T(4,128)}), f32[64,4,80]{2,1,0:T(4,128)S(1)}, u32[]{:S(2)}, u32[]{:S(2)}) async-start(f32[64,4,80]{2,1,0:T(4,128)} %broadcast_in_dim.4), calls=%async_computation | async-start | bytes 262144 | tf_op jit(solution)/shard_map/all_to_all | solution.py:550
  41.4 9.9 %collective-permute-start.9 = (f32[328,128]{1,0:T(8,128)S(1)}, f32[328,128]{1,0:T(8,128)S(1)}, u32[]{:S(2)}, u32[]{:S(2)}) collective-permute-start(f32[328,128]{1,0:T(8,128)S(1)} %get-tuple-element.57), channel_id=1, source_target_pairs={{0,32},{32,64},{64,96},{96,128},{128,160},{160,192},{192,224},{224... | collective-permute-start | bytes 503816 | tf_op jit(solution)/shard_map/ppermute | solution.py:570
  42.5 8.8 %collective-permute-start.10 = (f32[328,128]{1,0:T(8,128)S(1)}, f32[328,128]{1,0:T(8,128)S(1)}, u32[]{:S(2)}, u32[]{:S(2)}) collective-permute-start(f32[328,128]{1,0:T(8,128)S(1)} %get-tuple-element.58), channel_id=1, source_target_pairs={{32,0},{64,32},{96,64},{128,96},{160,128},{192,160},{224,192},{0,2... | collective-permute-start | bytes 503816 | tf_op jit(solution)/shard_map/ppermute | solution.py:571
  51.3 2.8 %copy-start = (f32[4,80]{1,0:T(4,128)}, f32[4,80]{1,0:T(4,128)S(1)}, u32[]{:S(2)}) copy-start(f32[4,80]{1,0:T(4,128)S(1)} %broadcast_multiply_fusion) | copy-start | bytes 3844
  54.1 7.2 %collective-permute-start.13 = (f32[144,128]{1,0:T(8,128)S(1)}, f32[144,128]{1,0:T(8,128)S(1)}, u32[]{:S(2)}, u32[]{:S(2)}) collective-permute-start(f32[144,128]{1,0:T(8,128)S(1)} %get-tuple-element.71), channel_id=1, source_target_pairs={{0,2},{1,3},{2,0},{3,1},{4,6},{5,7},{6,4},{7,5},{8,10},{9,11},{10,... | collective-permute-start | bytes 221192 | tf_op jit(solution)/shard_map/ppermute | solution.py:543
  55.8 8.2 %collective-permute-start.11 = (f32[144,128]{1,0:T(8,128)S(1)}, f32[144,128]{1,0:T(8,128)S(1)}, u32[]{:S(2)}, u32[]{:S(2)}) collective-permute-start(f32[144,128]{1,0:T(8,128)S(1)} %get-tuple-element.64), channel_id=1, source_target_pairs={{0,3},{1,2},{2,1},{3,0},{4,7},{5,6},{6,5},{7,4},{8,11},{9,10},{10,... | collective-permute-start | bytes 221192 | tf_op jit(solution)/shard_map/ppermute | solution.py:543
  60.9 3.1 %collective-permute-start.12 = (f32[144,128]{1,0:T(8,128)S(1)}, f32[144,128]{1,0:T(8,128)S(1)}, u32[]{:S(2)}, u32[]{:S(2)}) collective-permute-start(f32[144,128]{1,0:T(8,128)S(1)} %get-tuple-element.65), channel_id=1, source_target_pairs={{0,1},{1,0},{2,3},{3,2},{4,5},{5,4},{6,7},{7,6},{8,9},{9,8},{10,11... | collective-permute-start | bytes 221192 | tf_op jit(solution)/shard_map/ppermute | solution.py:543

commit v6 on v4

--- a/solution.py
+++ b/solution.py
@@ -22,7 +22,7 @@
 EDGE = DEPTH * RITZ
 SIDE = RITZ + 4 * GROUPS
 CHUNK = 8
-PIECE = 16
+PIECE = 8
 EARLY = (0, 2)
 LATE = (3, 1)
 MIB = 1024 * 1024

time: 66.5 us -> 66.8 us (level)
  no operation moved by 1% of the time
where the time goes in v6:
time: 66.8 us; the launch traced here: 66.6 us
  starting transfers between devices  33.9 us (51%)
  waiting for transfers between devices  16.8 us (25%)
  Pallas kernels  14.3 us (21%)
  between operations  0.78 us (1%)
  local copies, waits for them, and re-layouts  0.68 us (1%)
    ppermute x6, starting transfers between devices, exchange_members(): lax.ppermute(blocks[shift], 'mem', [(i, i ^ shift) for i in range(size)])  11.5 us
    all_to_all x1, starting transfers between devices, exchange_sum(): return jnp.sum(lax.all_to_all(copies, axes, 0, 0, tiled=True), axis=0)  7.74 us
    all_to_all x1, waiting for transfers between devices, exchange_sum(): return jnp.sum(lax.all_to_all(copies, axes, 0, 0, tiled=True), axis=0)  7.06 us
    ppermute x6, waiting for transfers between devices, exchange_members(): lax.ppermute(blocks[shift], 'mem', [(i, i ^ shift) for i in range(size)])  6.32 us
    ppermute x2, starting transfers between devices, per_device(): below = lax.ppermute(up, 'lat', under)  5.69 us
    ppermute x2, starting transfers between devices, per_device(): above = lax.ppermute(down, 'lat', over)  3.63 us
    pallas_call x1, Pallas kernels, restrict(): call(restrict_kernel, 'restrict', [VMEM, HBM], outs, scratch)(fine, flat)  3.48 us
    ppermute x2, waiting for transfers between devices, per_device(): lax.ppermute(partial, 'mem', [(i, i ^ shift) for i in range(4)])  3.43 us
  transfers between devices with their start and end apart: 15, of which 6 were waited for; matrix products, arithmetic and copies ran while one was open for 0% of the time, Pallas kernels for 8%

profile of v6, /device:TPU:1, one launch (start us, length us, event | category | flops | bytes accessed | tf_op | source)
XLA Modules:
  0.0 66.6 jit_solution(9693488500777167395)
XLA Ops:
  0.6 1.7 %edges.1 = (f32[3,16,96,128]{3,2,1,0:T(8,128)S(1)}, f32[96,128]{1,0:T(8,128)S(1)}, f32[96,128]{1,0:T(8,128)S(1)}) custom-call(f32[16,96,384]{2,1,0:T(8,128)} %bitcast.6), custom_call_target="tpu_custom_call" | custom-call | tf_op jit(solution)/shard_map/edges/pallas_call | solution.py:456
  2.4 2.5 %collective-permute-start = (f32[96,128]{1,0:T(8,128)S(1)}, f32[96,128]{1,0:T(8,128)S(1)}, u32[]{:S(2)}, u32[]{:S(2)}) collective-permute-start(f32[96,128]{1,0:T(8,128)S(1)} %get-tuple-element.36), channel_id=1, source_target_pairs={{0,32},{32,64},{64,96},{96,128},{128,160},{160,192},{192,224},{224... | collective-permute-start | bytes 147464 | tf_op jit(solution)/shard_map/ppermute | solution.py:543
  4.9 4.0 %collective-permute-start.1 = (f32[96,128]{1,0:T(8,128)S(1)}, f32[96,128]{1,0:T(8,128)S(1)}, u32[]{:S(2)}, u32[]{:S(2)}) collective-permute-start(f32[96,128]{1,0:T(8,128)S(1)} %get-tuple-element.37), channel_id=1, source_target_pairs={{32,0},{64,32},{96,64},{128,96},{160,128},{192,160},{224,192},{0,2... | collective-permute-start | bytes 147464 | tf_op jit(solution)/shard_map/ppermute | solution.py:544
  8.9 3.5 %restrict.1 = (f32[10240,128]{1,0:T(8,128)S(1)}, f32[4,128,256]{2,1,0:T(8,128)S(1)}, f32[4,8,256]{2,1,0:T(8,128)S(1)}, f32[80,128]{1,0:T(8,128)S(1)}, f32[80,128...) custom-call(f32[3,16,96,128]{3,2,1,0:T(8,128)S(1)} %get-tuple-element.38.f_ref, f32[10240,128]{1,0:T(8,128)} %bitcast.4), custom_call_target="tpu_custom_call" | custom-call | tf_op jit(solution)/shard_map/restrict/pallas_call | solution.py:470
  12.4 0.0 collective-permute-done.1.below_ref
  12.5 0.5 sides.1
  12.9 1.4 %collective-permute-start.2 = (f32[96,128]{1,0:T(8,128)S(1)}, f32[96,128]{1,0:T(8,128)S(1)}, u32[]{:S(2)}, u32[]{:S(2)}) collective-permute-start(f32[96,128]{1,0:T(8,128)S(1)} %get-tuple-element.44), channel_id=1, source_target_pairs={{0,4},{4,8},{8,12},{12,16},{16,20},{20,24},{24,28},{28,0},{1,5},{5... | collective-permute-start | bytes 147464 | tf_op jit(solution)/shard_map/ppermute | solution.py:548
  14.3 2.3 %collective-permute-start.3 = (f32[96,128]{1,0:T(8,128)S(1)}, f32[96,128]{1,0:T(8,128)S(1)}, u32[]{:S(2)}, u32[]{:S(2)}) collective-permute-start(f32[96,128]{1,0:T(8,128)S(1)} %get-tuple-element.45), channel_id=1, source_target_pairs={{4,0},{8,4},{12,8},{16,12},{20,16},{24,20},{28,24},{0,28},{5,1},{9... | collective-permute-start | bytes 147464 | tf_op jit(solution)/shard_map/ppermute | solution.py:547
  16.6 2.9 %collective-permute-start.4 = (f32[136,128]{1,0:T(8,128)S(1)}, f32[136,128]{1,0:T(8,128)S(1)}, u32[]{:S(2)}, u32[]{:S(2)}) collective-permute-start(f32[136,128]{1,0:T(8,128)S(1)} %get-tuple-element.48), channel_id=1, source_target_pairs={{0,2},{1,3},{2,0},{3,1},{4,6},{5,7},{6,4},{7,5},{8,10},{9,11},{10,... | collective-permute-start | bytes 208904 | tf_op jit(solution)/shard_map/ppermute | solution.py:526
  19.5 1.8 %collective-permute-start.5 = (f32[136,128]{1,0:T(8,128)S(1)}, f32[136,128]{1,0:T(8,128)S(1)}, u32[]{:S(2)}, u32[]{:S(2)}) collective-permute-start(f32[136,128]{1,0:T(8,128)S(1)} %get-tuple-element.49), channel_id=1, source_target_pairs={{0,1},{1,0},{2,3},{3,2},{4,5},{5,4},{6,7},{7,6},{8,9},{9,8},{10,11... | collective-permute-start | bytes 208904 | tf_op jit(solution)/shard_map/ppermute | solution.py:526
  21.3 0.1 collective-permute-done.4.c2_ref
  21.4 1.1 %near.1.near_ref = f32[2,80]{1,0:T(2,128)S(1)} custom-call(f32[10240,128]{1,0:T(8,128)S(1)} %get-tuple-element.46.v_ref, f32[136,128]{1,0:T(8,128)S(1)} %get-tuple-element.47.c0_ref, f32[136,128]{1,0:T(8,128)S(1)} %collective-permute-done.4.c2_ref, f32[96,128]{1,0:T(8,128)S(1)} %collective-permute-done.2.left_ref, f32[96,128]{1,0:T(8,128)S(1)} %collective-permute-done.3.right_ref), custom_call_target="tpu_custom_call" | custom-call | tf_op jit(solution)/shard_map/near/pallas_call | solution.py:484
  22.5 4.1 %collective-permute-done.6.c3_ref = f32[136,128]{1,0:T(8,128)S(1)} collective-permute-done((f32[136,128]{1,0:T(8,128)S(1)}, f32[136,128]{1,0:T(8,128)S(1)}, u32[]{:S(2)}, u32[]{:S(2)}) %collective-permute-start.6) | collective-permute-done | bytes 69664 | tf_op jit(solution)/shard_map/ppermute | solution.py:526
  26.6 0.5 bands.1
  27.1 1.1 %far.1 = f32[4,80]{1,0:T(4,128)S(1)} custom-call(f32[2,80]{1,0:T(2,128)S(1)} %near.1.near_ref, f32[10240,128]{1,0:T(8,128)S(1)} %get-tuple-element.46.v_ref, f32[136,128]{1,0:T(8,128)S(1)} %collective-permute-done.6.c3_ref, f32[136,128]{1,0:T(8,128)S(1)} %collective-permute-done.5.c1_ref, f32[96,128]{1,0:T(8,128)S(1)} %collective-permute-done.2.left_ref, ...), custom_call_target="tpu_custom_call" | custom-call | tf_op jit(solution)/shard_map/far/pallas_call | solution.py:489
  28.2 0.1 collective-permute-start.7
  28.3 1.1 %collective-permute-done.7 = f32[4,80]{1,0:T(4,128)S(1)} collective-permute-done((f32[4,80]{1,0:T(4,128)S(1)}, f32[4,80]{1,0:T(4,128)S(1)}, u32[]{:S(2)}, u32[]{:S(2)}) %collective-permute-start.7) | collective-permute-done | bytes 1312 | tf_op jit(solution)/shard_map/ppermute | solution.py:561
  29.4 1.6 %collective-permute-start.8 = (f32[4,80]{1,0:T(4,128)S(1)}, f32[4,80]{1,0:T(4,128)S(1)}, u32[]{:S(2)}, u32[]{:S(2)}) collective-permute-start(f32[4,80]{1,0:T(4,128)S(1)} %add.7), channel_id=1, source_target_pairs={{0,2},{1,3},{2,0},{3,1},{4,6},{5,7},{6,4},{7,5},{8,10},{9,11},{10,... | collective-permute-start | bytes 3848 | tf_op jit(solution)/shard_map/ppermute | solution.py:561
  31.0 2.3 %collective-permute-done.8 = f32[4,80]{1,0:T(4,128)S(1)} collective-permute-done((f32[4,80]{1,0:T(4,128)S(1)}, f32[4,80]{1,0:T(4,128)S(1)}, u32[]{:S(2)}, u32[]{:S(2)}) %collective-permute-start.8) | collective-permute-done | bytes 1312 | tf_op jit(solution)/shard_map/ppermute | solution.py:561
  33.3 0.7 %broadcast_in_dim.4 = f32[64,4,80]{2,1,0:T(4,128)} broadcast(f32[4,80]{1,0:T(4,128)S(1)} %add.8), dimensions={1,2} | broadcast | bytes 83200 | tf_op jit(solution)/shard_map/broadcast_in_dim | solution.py:532
  34.0 7.7 %all-to-all-start = ((f32[64,4,80]{2,1,0:T(4,128)}), f32[64,4,80]{2,1,0:T(4,128)S(1)}, u32[]{:S(2)}, u32[]{:S(2)}) async-start(f32[64,4,80]{2,1,0:T(4,128)} %broadcast_in_dim.4), calls=%async_computation | async-start | bytes 262144 | tf_op jit(solution)/shard_map/all_to_all | solution.py:533
  41.8 1.1 %collective-permute-start.9 = (f32[328,128]{1,0:T(8,128)S(1)}, f32[328,128]{1,0:T(8,128)S(1)}, u32[]{:S(2)}, u32[]{:S(2)}) collective-permute-start(f32[328,128]{1,0:T(8,128)S(1)} %get-tuple-element.56), channel_id=1, source_target_pairs={{0,32},{32,64},{64,96},{96,128},{128,160},{160,192},{192,224},{224... | collective-permute-start | bytes 503816 | tf_op jit(solution)/shard_map/ppermute | solution.py:553
  42.9 1.7 %collective-permute-start.10 = (f32[328,128]{1,0:T(8,128)S(1)}, f32[328,128]{1,0:T(8,128)S(1)}, u32[]{:S(2)}, u32[]{:S(2)}) collective-permute-start(f32[328,128]{1,0:T(8,128)S(1)} %get-tuple-element.57), channel_id=1, source_target_pairs={{32,0},{64,32},{96,64},{128,96},{160,128},{192,160},{224,192},{0,2... | collective-permute-start | bytes 503816 | tf_op jit(solution)/shard_map/ppermute | solution.py:554
  44.5 7.1 %all-to-all-done = f32[64,4,80]{2,1,0:T(4,128)S(1)} async-done(((f32[64,4,80]{2,1,0:T(4,128)}), f32[64,4,80]{2,1,0:T(4,128)S(1)}, u32[]{:S(2)}, u32[]{:S(2)}) %all-to-all-start) | async-done | bytes 81952 | tf_op jit(solution)/shard_map/all_to_all | solution.py:533
  51.6 0.1 reduce_sum.9
  51.7 3.2 %update.1 = (f32[80,2,64,128]{3,2,1,0:T(8,128)S(1)}, f32[320,128]{1,0:T(8,128)S(1)}, f32[16,128]{1,0:T(8,128)S(1)}, f32[144,128]{1,0:T(8,128)S(1)}, f32[144,128]{1,0:T(8,128)S(1)}, /*index=5*/f32[144,128]{1,0:T(8,128)S(1)}) custom-call(f32[8,80]{1,0:T(8,128)S(1)} %pad_maximum_fusion.c_ref, f32[80,2,64,128]{3,2,1,0:T(8,128)} %bitcast.5, ...), custom_call_target="tpu_custom_call" | custom-call | tf_op jit(solution)/shard_map/update/pallas_call | solution.py:497
  54.9 1.7 %collective-permute-start.13 = (f32[144,128]{1,0:T(8,128)S(1)}, f32[144,128]{1,0:T(8,128)S(1)}, u32[]{:S(2)}, u32[]{:S(2)}) collective-permute-start(f32[144,128]{1,0:T(8,128)S(1)} %get-tuple-element.69), channel_id=1, source_target_pairs={{0,2},{1,3},{2,0},{3,1},{4,6},{5,7},{6,4},{7,5},{8,10},{9,11},{10,... | collective-permute-start | bytes 221192 | tf_op jit(solution)/shard_map/ppermute | solution.py:526
  56.6 5.1 %collective-permute-start.11 = (f32[144,128]{1,0:T(8,128)S(1)}, f32[144,128]{1,0:T(8,128)S(1)}, u32[]{:S(2)}, u32[]{:S(2)}) collective-permute-start(f32[144,128]{1,0:T(8,128)S(1)} %get-tuple-element.62), channel_id=1, source_target_pairs={{0,3},{1,2},{2,1},{3,0},{4,7},{5,6},{6,5},{7,4},{8,11},{9,10},{10,... | collective-permute-start | bytes 221192 | tf_op jit(solution)/shard_map/ppermute | solution.py:526
  61.7 0.4 own.1.ra_ref
  62.1 0.5 prolong_early.1.refs_0_
  62.7 2.1 %collective-permute-done.11.ra_ref = f32[144,128]{1,0:T(8,128)S(1)} collective-permute-done((f32[144,128]{1,0:T(8,128)S(1)}, f32[144,128]{1,0:T(8,128)S(1)}, u32[]{:S(2)}, u32[]{:S(2)}) %collective-permute-start.11) | collective-permute-done | bytes 73760 | tf_op jit(solution)/shard_map/ppermute | solution.py:526
  64.8 1.8 %prolong_late.1 = f32[16,96,384]{2,1,0:T(8,128)} custom-call(f32[144,128]{1,0:T(8,128)S(1)} %collective-permute-done.11.ra_ref, f32[144,128]{1,0:T(8,128)S(1)} %collective-permute-done.12.rb_ref, f32[4,128,256]{2,1,0:T(8,128)S(1)} %get-tuple-element.64.e2_ref, f32[4,8,256]{2,1,0:T(8,128)S(1)} %get-tuple-element.65.h2_ref, ...), custom_call_target="tpu_custom_call" | custom-call | tf_op jit(solution)/shard_map/prolong_late/pallas_call | solution.py:520
  (19 shorter events, 0.1 us)
Async XLA Ops:
  2.4 10.1 %collective-permute-start = (f32[96,128]{1,0:T(8,128)S(1)}, f32[96,128]{1,0:T(8,128)S(1)}, u32[]{:S(2)}, u32[]{:S(2)}) collective-permute-start(f32[96,128]{1,0:T(8,128)S(1)} %get-tuple-element.36), channel_id=1, source_target_pairs={{0,32},{32,64},{64,96},{96,128},{128,160},{160,192},{192,224},{224... | collective-permute-start | bytes 147464 | tf_op jit(solution)/shard_map/ppermute | solution.py:543
  4.9 7.5 %collective-permute-start.1 = (f32[96,128]{1,0:T(8,128)S(1)}, f32[96,128]{1,0:T(8,128)S(1)}, u32[]{:S(2)}, u32[]{:S(2)}) collective-permute-start(f32[96,128]{1,0:T(8,128)S(1)} %get-tuple-element.37), channel_id=1, source_target_pairs={{32,0},{64,32},{96,64},{128,96},{160,128},{192,160},{224,192},{0,2... | collective-permute-start | bytes 147464 | tf_op jit(solution)/shard_map/ppermute | solution.py:544
  8.9 12.4 %copy-start.1 = (f32[80]{0:T(128)S(1)}, f32[80]{0:T(128)}, u32[]{:S(2)}) copy-start(f32[80]{0:T(128)} %param.5) | copy-start | bytes 964
  12.9 8.4 %collective-permute-start.2 = (f32[96,128]{1,0:T(8,128)S(1)}, f32[96,128]{1,0:T(8,128)S(1)}, u32[]{:S(2)}, u32[]{:S(2)}) collective-permute-start(f32[96,128]{1,0:T(8,128)S(1)} %get-tuple-element.44), channel_id=1, source_target_pairs={{0,4},{4,8},{8,12},{12,16},{16,20},{20,24},{24,28},{28,0},{1,5},{5... | collective-permute-start | bytes 147464 | tf_op jit(solution)/shard_map/ppermute | solution.py:548
  14.3 7.0 %collective-permute-start.3 = (f32[96,128]{1,0:T(8,128)S(1)}, f32[96,128]{1,0:T(8,128)S(1)}, u32[]{:S(2)}, u32[]{:S(2)}) collective-permute-start(f32[96,128]{1,0:T(8,128)S(1)} %get-tuple-element.45), channel_id=1, source_target_pairs={{4,0},{8,4},{12,8},{16,12},{20,16},{24,20},{28,24},{0,28},{5,1},{9... | collective-permute-start | bytes 147464 | tf_op jit(solution)/shard_map/ppermute | solution.py:547
  16.6 4.8 %collective-permute-start.4 = (f32[136,128]{1,0:T(8,128)S(1)}, f32[136,128]{1,0:T(8,128)S(1)}, u32[]{:S(2)}, u32[]{:S(2)}) collective-permute-start(f32[136,128]{1,0:T(8,128)S(1)} %get-tuple-element.48), channel_id=1, source_target_pairs={{0,2},{1,3},{2,0},{3,1},{4,6},{5,7},{6,4},{7,5},{8,10},{9,11},{10,... | collective-permute-start | bytes 208904 | tf_op jit(solution)/shard_map/ppermute | solution.py:526
  19.5 3.0 %collective-permute-start.5 = (f32[136,128]{1,0:T(8,128)S(1)}, f32[136,128]{1,0:T(8,128)S(1)}, u32[]{:S(2)}, u32[]{:S(2)}) collective-permute-start(f32[136,128]{1,0:T(8,128)S(1)} %get-tuple-element.49), channel_id=1, source_target_pairs={{0,1},{1,0},{2,3},{3,2},{4,5},{5,4},{6,7},{7,6},{8,9},{9,8},{10,11... | collective-permute-start | bytes 208904 | tf_op jit(solution)/shard_map/ppermute | solution.py:526
  21.3 5.3 %collective-permute-start.6 = (f32[136,128]{1,0:T(8,128)S(1)}, f32[136,128]{1,0:T(8,128)S(1)}, u32[]{:S(2)}, u32[]{:S(2)}) collective-permute-start(f32[136,128]{1,0:T(8,128)S(1)} %get-tuple-element.50), channel_id=1, source_target_pairs={{0,3},{1,2},{2,1},{3,0},{4,7},{5,6},{6,5},{7,4},{8,11},{9,10},{10,... | collective-permute-start | bytes 208904 | tf_op jit(solution)/shard_map/ppermute | solution.py:526
  28.2 1.2 %collective-permute-start.7 = (f32[4,80]{1,0:T(4,128)S(1)}, f32[4,80]{1,0:T(4,128)S(1)}, u32[]{:S(2)}, u32[]{:S(2)}) collective-permute-start(f32[4,80]{1,0:T(4,128)S(1)} %far.1), channel_id=1, source_target_pairs={{0,1},{1,0},{2,3},{3,2},{4,5},{5,4},{6,7},{7,6},{8,9},{9,8},{10,11... | collective-permute-start | bytes 3848 | tf_op jit(solution)/shard_map/ppermute | solution.py:561
  29.4 3.9 %collective-permute-start.8 = (f32[4,80]{1,0:T(4,128)S(1)}, f32[4,80]{1,0:T(4,128)S(1)}, u32[]{:S(2)}, u32[]{:S(2)}) collective-permute-start(f32[4,80]{1,0:T(4,128)S(1)} %add.7), channel_id=1, source_target_pairs={{0,2},{1,3},{2,0},{3,1},{4,6},{5,7},{6,4},{7,5},{8,10},{9,11},{10,... | collective-permute-start | bytes 3848 | tf_op jit(solution)/shard_map/ppermute | solution.py:561
  34.0 17.6 %all-to-all-start = ((f32[64,4,80]{2,1,0:T(4,128)}), f32[64,4,80]{2,1,0:T(4,128)S(1)}, u32[]{:S(2)}, u32[]{:S(2)}) async-start(f32[64,4,80]{2,1,0:T(4,128)} %broadcast_in_dim.4), calls=%async_computation | async-start | bytes 262144 | tf_op jit(solution)/shard_map/all_to_all | solution.py:533
  41.8 9.9 %collective-permute-start.9 = (f32[328,128]{1,0:T(8,128)S(1)}, f32[328,128]{1,0:T(8,128)S(1)}, u32[]{:S(2)}, u32[]{:S(2)}) collective-permute-start(f32[328,128]{1,0:T(8,128)S(1)} %get-tuple-element.56), channel_id=1, source_target_pairs={{0,32},{32,64},{64,96},{96,128},{128,160},{160,192},{192,224},{224... | collective-permute-start | bytes 503816 | tf_op jit(solution)/shard_map/ppermute | solution.py:553
  42.9 8.8 %collective-permute-start.10 = (f32[328,128]{1,0:T(8,128)S(1)}, f32[328,128]{1,0:T(8,128)S(1)}, u32[]{:S(2)}, u32[]{:S(2)}) collective-permute-start(f32[328,128]{1,0:T(8,128)S(1)} %get-tuple-element.57), channel_id=1, source_target_pairs={{32,0},{64,32},{96,64},{128,96},{160,128},{192,160},{224,192},{0,2... | collective-permute-start | bytes 503816 | tf_op jit(solution)/shard_map/ppermute | solution.py:554
  51.7 3.2 %copy-start = (f32[4,80]{1,0:T(4,128)}, f32[4,80]{1,0:T(4,128)S(1)}, u32[]{:S(2)}) copy-start(f32[4,80]{1,0:T(4,128)S(1)} %broadcast_multiply_fusion) | copy-start | bytes 3844
  54.9 7.2 %collective-permute-start.13 = (f32[144,128]{1,0:T(8,128)S(1)}, f32[144,128]{1,0:T(8,128)S(1)}, u32[]{:S(2)}, u32[]{:S(2)}) collective-permute-start(f32[144,128]{1,0:T(8,128)S(1)} %get-tuple-element.69), channel_id=1, source_target_pairs={{0,2},{1,3},{2,0},{3,1},{4,6},{5,7},{6,4},{7,5},{8,10},{9,11},{10,... | collective-permute-start | bytes 221192 | tf_op jit(solution)/shard_map/ppermute | solution.py:526
  56.6 8.2 %collective-permute-start.11 = (f32[144,128]{1,0:T(8,128)S(1)}, f32[144,128]{1,0:T(8,128)S(1)}, u32[]{:S(2)}, u32[]{:S(2)}) collective-permute-start(f32[144,128]{1,0:T(8,128)S(1)} %get-tuple-element.62), channel_id=1, source_target_pairs={{0,3},{1,2},{2,1},{3,0},{4,7},{5,6},{6,5},{7,4},{8,11},{9,10},{10,... | collective-permute-start | bytes 221192 | tf_op jit(solution)/shard_map/ppermute | solution.py:526
  61.7 3.1 %collective-permute-start.12 = (f32[144,128]{1,0:T(8,128)S(1)}, f32[144,128]{1,0:T(8,128)S(1)}, u32[]{:S(2)}, u32[]{:S(2)}) collective-permute-start(f32[144,128]{1,0:T(8,128)S(1)} %get-tuple-element.63), channel_id=1, source_target_pairs={{0,1},{1,0},{2,3},{3,2},{4,5},{5,4},{6,7},{7,6},{8,9},{9,8},{10,11... | collective-permute-start | bytes 221192 | tf_op jit(solution)/shard_map/ppermute | solution.py:526
